TPU v7x, 32 devices: a whole 2x2x4 slice. The times are simulated.
32 devices in a mesh: page: 8 (over y, x, core), seq: 4 (over z).
Axes of the slice: x: 2, y: 2, z: 4, core: 2. Of those that a mesh axis runs over, the one named last changes fastest.
Arguments:
- tokens: bfloat16 [8, 2048, 1024], P('page', 'seq'), may hold values from -6 to 6
- memory: bfloat16 [8, 640, 1024], P('page', 'seq'), may hold values from -6 to 6
- cotangent: bfloat16 [8, 2048, 1024], P('page', 'seq'), may hold values from -6 to 6
- res_flag: int32 [8], P('page'), may hold values from 0 to 1
- ln_gain: bfloat16 [3, 1024], P(None, ('page', 'seq')), may hold values from 0.5 to 1.5
- ln_bias: bfloat16 [3, 1024], P(None, ('page', 'seq')), may hold values from -1 to 1
- self_in: bfloat16 [3, 1024, 1024], P(None, ('page', 'seq')), may hold values from -0.1875 to 0.1875
- self_out: bfloat16 [1024, 1024], P(('page', 'seq')), may hold values from -1.5 to 1.5
- cross_in: bfloat16 [3, 1024, 1024], P(None, ('page', 'seq')), may hold values from -0.1875 to 0.1875
- cross_out: bfloat16 [1024, 1024], P(('page', 'seq')), may hold values from -1 to 1
- ff_in: bfloat16 [1024, 4096], P(('page', 'seq')), may hold values from -0.1875 to 0.1875
- ff_out: bfloat16 [4096, 1024], P(('page', 'seq')), may hold values from -0.09375 to 0.09375
- proj_bias: bfloat16 [7, 1024], P(None, ('page', 'seq')), may hold values from -0.59765625 to 0.59765625
- ff_bias: bfloat16 [4096], P(('page', 'seq')), may hold values from -0.59765625 to 0.59765625
Outputs:
- layer_out: bfloat16 [8, 2048, 1024], P('page', 'seq')
- grad_tokens: float32 [8, 2048, 1024], P('page', 'seq')
- grad_memory: float32 [8, 640, 1024], P('page', 'seq')
- grad_ln_gain: float32 [3, 1024], P(None, ('page', 'seq'))
- grad_ln_bias: float32 [3, 1024], P(None, ('page', 'seq'))
- grad_self_in: float32 [3, 1024, 1024], P(None, ('page', 'seq'))
- grad_self_out: float32 [1024, 1024], P(('page', 'seq'))
- grad_cross_in: float32 [3, 1024, 1024], P(None, ('page', 'seq'))
- grad_cross_out: float32 [1024, 1024], P(('page', 'seq'))
- grad_ff_in: float32 [1024, 4096], P(('page', 'seq'))
- grad_ff_out: float32 [4096, 1024], P(('page', 'seq'))
- grad_proj_bias: float32 [7, 1024], P(None, ('page', 'seq'))
- grad_ff_bias: float32 [4096], P(('page', 'seq'))
Inputs may be any that keep to these rules, and one draw needn't show every extreme that they name: A page with res_flag 1 has its first 588 memory rows valid, one with 0 its first 140; the other rows are padding.
All inputs are finite; a program needn't handle non-finite values.
Results may differ from a plain program's by a relative error of at most 0.023.
Values may be sent and summed in bfloat16 or wider, within the bound.
No kernel may reach another device: no remote copies, remote signals or barrier semaphores. Data moves between devices by JAX's collectives and lax.ppermute only.
A program may use at most 256 MiB of HBM per device.

v0:
```python
import math

import jax
import jax.numpy as jnp
from jax import lax
from jax.sharding import PartitionSpec as P

HEADS = 16
HEAD_DIM = 64
VALID_HI = 588
VALID_LO = 140


NEGATIVE = -1e30
EPSILON = 1e-05


def for_sending(value):

    def short(part):
        return part.astype(jnp.bfloat16) if part.dtype == jnp.float32 else part

    return jax.tree.map(short, value)


def from_behind(value, axis, by):
    count = lax.axis_size(axis)
    return lax.ppermute(value, axis, [(i, (i + by) % count) for i in range(count)])


def layer_norm(values, ln_scale, ln_shift):
    center_mean = jnp.mean(values, axis=-1, keepdims=True)
    centered = values - center_mean
    variance = jnp.mean(centered * centered, axis=-1, keepdims=True)
    return centered * lax.rsqrt(variance + EPSILON) * ln_scale + ln_shift


def gelu_exact(values):
    return jax.nn.gelu(values, approximate=False)


def forward_dot(left_rows, weight):
    return jnp.dot(left_rows, weight, preferred_element_type=jnp.float32)


def back_dot(grad_rows, weight):
    return jnp.einsum("tb,ab->ta", grad_rows, weight, preferred_element_type=jnp.float32)


def outer_sum(left_rows, right_rows):
    return jnp.einsum("ta,tb->ab", left_rows, right_rows, preferred_element_type=jnp.float32)


def split_heads(values):
    return values.reshape(values.shape[0], HEADS, HEAD_DIM)


def head_scores(queries, key_block):
    return jnp.einsum(
        "qhe,khe->hqk", queries, key_block, preferred_element_type=jnp.float32
    ) * HEAD_DIM ** (-0.5)


def block_loop(step_fn, running, pieces, block_cap):
    piece_rows = pieces[0].shape[0]
    block_rows = math.gcd(piece_rows, block_cap)
    block_count = piece_rows // block_rows
    stacked = tuple((member.reshape(block_count, block_rows, member.shape[1]) for member in pieces))
    firsts = block_rows * jnp.arange(block_count, dtype=jnp.int32)

    def inner_step(carried, packed):
        return (step_fn(carried, packed[0], packed[1]), None)

    result, unused = lax.scan(inner_step, running, (stacked, firsts))
    return result


def on_device(
    tokens,
    memory,
    cotangent,
    res_flag,
    ln_gain,
    ln_bias,
    self_in,
    self_out,
    cross_in,
    cross_out,
    ff_in,
    ff_out,
    proj_bias,
    ff_bias,
):
    gathered = (
        lax.all_gather(ln_gain, ("page", "seq"), axis=1, tiled=True),
        lax.all_gather(ln_bias, ("page", "seq"), axis=1, tiled=True),
        lax.all_gather(self_in, ("page", "seq"), axis=1, tiled=True),
        lax.all_gather(self_out, ("page", "seq"), axis=0, tiled=True),
        lax.all_gather(cross_in, ("page", "seq"), axis=1, tiled=True),
        lax.all_gather(cross_out, ("page", "seq"), axis=0, tiled=True),
        lax.all_gather(ff_in, ("page", "seq"), axis=0, tiled=True),
        lax.all_gather(ff_out, ("page", "seq"), axis=0, tiled=True),
        lax.all_gather(proj_bias, ("page", "seq"), axis=1, tiled=True),
        lax.all_gather(ff_bias, ("page", "seq"), axis=0, tiled=True),
    )
    gain_all = gathered[0].astype(jnp.float32)
    shift_all = gathered[1].astype(jnp.float32)
    w_self = gathered[2]
    w_self_out = gathered[3]
    w_cross = gathered[4]
    w_cross_out = gathered[5]
    w_up = gathered[6]
    w_down = gathered[7]
    bias_all = gathered[8].astype(jnp.float32)
    up_bias = gathered[9].astype(jnp.float32)
    scaling = HEAD_DIM ** (-0.5)
    tok_rows = tokens.shape[1]
    width_all = tokens.shape[2]
    seq_rank = lax.axis_index("seq")
    seq_count = lax.axis_size("seq")
    tok_local = tokens[0]
    cot_local = cotangent[0]
    block_cap = 512
    key_splits = 1

    def visible(update, running):
        return update(running, 0, tok_rows)

    query_places = seq_rank * tok_rows + jnp.arange(tok_rows, dtype=jnp.int32)
    x_in = tok_local.astype(jnp.float32)
    h_one = layer_norm(x_in, gain_all[0], shift_all[0]).astype(jnp.bfloat16)
    q_self = (forward_dot(h_one, w_self[0]) + bias_all[0]).astype(jnp.bfloat16)
    k_self = forward_dot(h_one, w_self[1]).astype(jnp.bfloat16)
    v_self = (forward_dot(h_one, w_self[2]) + bias_all[1]).astype(jnp.bfloat16)
    q_heads = split_heads(q_self)

    def causal_scores(key_heads, key_places, row_start, row_stop):
        allowed = key_places[None, :] <= query_places[row_start:row_stop, None]
        scores = head_scores(q_heads, key_heads)
        return (jnp.where(allowed[None], scores, NEGATIVE), allowed)

    def max_step(running, key_parts, first_row):
        key_heads = split_heads(key_parts[0])
        key_places = first_row + jnp.arange(key_parts[0].shape[0], dtype=jnp.int32)

        def update(stats, row_start, row_stop):
            run_max, run_sum = stats
            scores, allowed = causal_scores(key_heads, key_places, row_start, row_stop)
            new_max = jnp.maximum(run_max, jnp.max(scores, axis=-1))
            exponent = jnp.where(allowed[None], jnp.exp(scores - new_max[:, :, None]), 0.0)
            new_sum = run_sum * jnp.exp(run_max - new_max) + jnp.sum(exponent, axis=-1)
            return (
                run_max.at[:, row_start:row_stop].set(new_max),
                run_sum.at[:, row_start:row_stop].set(new_sum),
            )

        return visible(update, running)

    start_max = jnp.full((HEADS, tok_rows), NEGATIVE, jnp.float32)
    start_sum = jnp.zeros((HEADS, tok_rows), jnp.float32)
    run_max, run_sum = block_loop(
        max_step,
        (start_max, start_sum),
        (lax.all_gather(k_self, "seq", axis=0, tiled=True),),
        block_cap,
    )
    log_total = run_max + jnp.log(run_sum)

    def self_probs(key_heads, key_places, row_start, row_stop):
        scores, allowed = causal_scores(key_heads, key_places, row_start, row_stop)
        return jnp.where(
            allowed[None], jnp.exp(scores - log_total[:, row_start:row_stop, None]), 0.0
        )

    def out_step(running, key_parts, first_row):
        key_heads = split_heads(key_parts[0])
        value_heads = split_heads(key_parts[1])
        key_places = first_row + jnp.arange(key_parts[0].shape[0], dtype=jnp.int32)

        def update(totals, row_start, row_stop):
            attn_probs = self_probs(key_heads, key_places, row_start, row_stop).astype(jnp.bfloat16)
            return totals.at[row_start:row_stop].add(
                jnp.einsum(
                    "hqk,khe->qhe", attn_probs, value_heads, preferred_element_type=jnp.float32
                )
            )

        return visible(update, running)

    self_sum = block_loop(
        out_step,
        jnp.zeros((tok_rows, HEADS, HEAD_DIM), jnp.float32),
        (
            lax.all_gather(k_self, "seq", axis=0, tiled=True),
            lax.all_gather(v_self, "seq", axis=0, tiled=True),
        ),
        block_cap,
    )
    o_self = self_sum.reshape(tok_rows, width_all)
    attended = o_self.astype(jnp.bfloat16)
    x_one = x_in + forward_dot(attended, w_self_out) + bias_all[2]
    h_two = layer_norm(x_one, gain_all[1], shift_all[1]).astype(jnp.bfloat16)
    q_cross = (forward_dot(h_two, w_cross[0]) + bias_all[3]).astype(jnp.bfloat16)
    mem_rows = memory[0]
    all_memory = lax.all_gather(mem_rows, "seq", axis=0, tiled=True)
    k_cross = forward_dot(all_memory, w_cross[1]).astype(jnp.bfloat16)
    v_cross = (forward_dot(all_memory, w_cross[2]) + bias_all[4]).astype(jnp.bfloat16)
    qc_heads = split_heads(q_cross)
    kc_heads = split_heads(k_cross)
    vc_heads = split_heads(v_cross)
    valid_limit = jnp.where(res_flag[0] == 1, VALID_HI, VALID_LO)
    mem_valid = jnp.arange(k_cross.shape[0], dtype=jnp.int32) < valid_limit
    cross_scores = jnp.where(mem_valid[None, None, :], head_scores(qc_heads, kc_heads), NEGATIVE)
    shifted = jnp.exp(cross_scores - jnp.max(cross_scores, axis=-1, keepdims=True))
    p_cross = shifted / jnp.sum(shifted, axis=-1, keepdims=True)
    p_cross_low = p_cross.astype(jnp.bfloat16)
    o_cross = jnp.einsum(
        "hqk,khe->qhe", p_cross_low, vc_heads, preferred_element_type=jnp.float32
    ).reshape(tok_rows, width_all)
    attended_cross = o_cross.astype(jnp.bfloat16)
    x_two = x_one + forward_dot(attended_cross, w_cross_out) + bias_all[5]
    h_three = layer_norm(x_two, gain_all[2], shift_all[2]).astype(jnp.bfloat16)
    pre_act = forward_dot(h_three, w_up) + up_bias
    act_rows = gelu_exact(pre_act).astype(jnp.bfloat16)
    layer_rows = (x_two + forward_dot(act_rows, w_down) + bias_all[6]).astype(jnp.bfloat16)
    grad_out = cot_local.astype(jnp.float32)
    g_mlp = grad_out.astype(jnp.bfloat16)
    grad_down = outer_sum(act_rows, g_mlp)
    unused_act, gelu_pull = jax.vjp(gelu_exact, pre_act)
    g_pre = gelu_pull(back_dot(g_mlp, w_down))[0].astype(jnp.bfloat16)
    grad_up = outer_sum(h_three, g_pre)
    grad_up_bias = jnp.sum(g_pre.astype(jnp.float32), axis=0)
    unused_three, norm_pull_three = jax.vjp(layer_norm, x_two, gain_all[2], shift_all[2])
    back_three = norm_pull_three(back_dot(g_pre, w_up))
    g_two = grad_out + back_three[0]
    g_cross = g_two.astype(jnp.bfloat16)
    grad_cross_out = outer_sum(attended_cross, g_cross)
    d_oc = back_dot(g_cross, w_cross_out).astype(jnp.bfloat16)
    doc_heads = split_heads(d_oc)
    delta_cross = jnp.sum(
        (d_oc.astype(jnp.float32) * o_cross).reshape(tok_rows, HEADS, HEAD_DIM), axis=-1
    ).T
    probs_grad_c = jnp.einsum(
        "qhe,khe->hqk", doc_heads, vc_heads, preferred_element_type=jnp.float32
    )
    scores_grad_c = (p_cross * (probs_grad_c - delta_cross[:, :, None])).astype(jnp.bfloat16)
    dq_cross = (
        (
            jnp.einsum("hqk,khe->qhe", scores_grad_c, kc_heads, preferred_element_type=jnp.float32)
            * scaling
        )
        .reshape(tok_rows, width_all)
        .astype(jnp.bfloat16)
    )
    part_key = (
        jnp.einsum("hqk,qhe->khe", scores_grad_c, qc_heads, preferred_element_type=jnp.float32)
        * scaling
    ).reshape(-1, width_all)
    part_value = jnp.einsum(
        "hqk,qhe->khe", p_cross_low, doc_heads, preferred_element_type=jnp.float32
    ).reshape(-1, width_all)
    key_sum_c, value_sum_c = (
        lax.psum_scatter(
            part_key.astype(jnp.bfloat16), "seq", scatter_dimension=0, tiled=True
        ).astype(jnp.float32),
        lax.psum_scatter(
            part_value.astype(jnp.bfloat16), "seq", scatter_dimension=0, tiled=True
        ).astype(jnp.float32),
    )
    dk_cross = key_sum_c.astype(jnp.bfloat16)
    dv_cross = value_sum_c.astype(jnp.bfloat16)
    grad_memory = back_dot(dk_cross, w_cross[1]) + back_dot(dv_cross, w_cross[2])
    grad_cross_in = jnp.stack(
        [outer_sum(h_two, dq_cross), outer_sum(mem_rows, dk_cross), outer_sum(mem_rows, dv_cross)]
    )
    unused_two, norm_pull_two = jax.vjp(layer_norm, x_one, gain_all[1], shift_all[1])
    back_two = norm_pull_two(back_dot(dq_cross, w_cross[0]))
    g_one = g_two + back_two[0]
    g_self = g_one.astype(jnp.bfloat16)
    grad_self_out = outer_sum(attended, g_self)
    d_os = back_dot(g_self, w_self_out).astype(jnp.bfloat16)
    dos_heads = split_heads(d_os)
    delta_self = jnp.sum(
        (d_os.astype(jnp.float32) * o_self).reshape(tok_rows, HEADS, HEAD_DIM), axis=-1
    ).T
    split_rows = tok_rows // key_splits

    def cycle_step(turn, carried):
        key_part, value_part, key_acc, value_acc, query_acc = carried
        source = (seq_rank - turn) % seq_count
        key_heads = split_heads(key_part)
        value_heads = split_heads(value_part)
        key_places = source * tok_rows + 0 + jnp.arange(split_rows, dtype=jnp.int32)

        def update(grads, row_start, row_stop):
            key_grad, value_grad, query_grad = grads
            attn_probs = self_probs(key_heads, key_places, row_start, row_stop)
            probs_grad = jnp.einsum(
                "qhe,khe->hqk", dos_heads, value_heads, preferred_element_type=jnp.float32
            )
            scores_grad = (
                attn_probs * (probs_grad - delta_self[:, row_start:row_stop, None])
            ).astype(jnp.bfloat16)
            query_grad = query_grad.at[row_start:row_stop].add(
                jnp.einsum(
                    "hqk,khe->qhe", scores_grad, key_heads, preferred_element_type=jnp.float32
                )
            )
            key_grad = key_grad + jnp.einsum(
                "hqk,qhe->khe", scores_grad, q_heads, preferred_element_type=jnp.float32
            ).reshape(-1, width_all)
            value_grad = value_grad + jnp.einsum(
                "hqk,qhe->khe",
                attn_probs.astype(jnp.bfloat16),
                dos_heads,
                preferred_element_type=jnp.float32,
            ).reshape(-1, width_all)
            return (key_grad, value_grad, query_grad)

        part_result = visible(update, (key_acc, value_acc, query_acc))
        key_pieces = [part_result[0]]
        value_pieces = [part_result[1]]
        query_acc = part_result[2]
        key_acc = jnp.concatenate(key_pieces, axis=0)
        value_acc = jnp.concatenate(value_pieces, axis=0)
        key_wide, value_wide, key_acc, value_acc = (
            from_behind(key_part.astype(jnp.float32).astype(jnp.bfloat16), "seq", 1).astype(
                jnp.float32
            ),
            from_behind(value_part.astype(jnp.float32).astype(jnp.bfloat16), "seq", 1).astype(
                jnp.float32
            ),
            from_behind(for_sending(key_acc), "seq", 1).astype(key_acc.dtype),
            from_behind(for_sending(value_acc), "seq", 1).astype(value_acc.dtype),
        )
        return (
            key_wide.astype(jnp.bfloat16),
            value_wide.astype(jnp.bfloat16),
            key_acc,
            value_acc,
            query_acc,
        )

    zero_rows = jnp.zeros((tok_rows, width_all), jnp.float32)
    cycle_start = (
        k_self,
        v_self,
        zero_rows,
        zero_rows,
        jnp.zeros((tok_rows, HEADS, HEAD_DIM), jnp.float32),
    )
    cycle_final = lax.fori_loop(0, seq_count, cycle_step, cycle_start)
    dk_self = (cycle_final[2] * scaling).astype(jnp.bfloat16)
    dv_self = cycle_final[3].astype(jnp.bfloat16)
    dq_self = (cycle_final[4] * scaling).reshape(tok_rows, width_all).astype(jnp.bfloat16)
    grad_self_in = jnp.stack(
        [outer_sum(h_one, dq_self), outer_sum(h_one, dk_self), outer_sum(h_one, dv_self)]
    )
    input_grad_one = (
        back_dot(dq_self, w_self[0]) + back_dot(dk_self, w_self[1]) + back_dot(dv_self, w_self[2])
    )
    unused_one, norm_pull_one = jax.vjp(layer_norm, x_in, gain_all[0], shift_all[0])
    back_one = norm_pull_one(input_grad_one)
    token_grad_rows = g_one + back_one[0]
    grad_gain = jnp.stack([back_one[1], back_two[1], back_three[1]])
    grad_shift = jnp.stack([back_one[2], back_two[2], back_three[2]])
    grad_bias = jnp.stack(
        [
            jnp.sum(dq_self.astype(jnp.float32), axis=0),
            jnp.sum(dv_self.astype(jnp.float32), axis=0),
            jnp.sum(g_one, axis=0),
            jnp.sum(dq_cross.astype(jnp.float32), axis=0),
            jnp.sum(dv_cross.astype(jnp.float32), axis=0),
            jnp.sum(g_two, axis=0),
            jnp.sum(grad_out, axis=0),
        ]
    )
    (
        sum_gain,
        sum_shift,
        sum_self_in,
        sum_self_out,
        sum_cross_in,
        sum_cross_out,
        sum_up,
        sum_down,
        sum_bias,
        sum_up_bias,
    ) = (
        lax.psum_scatter(grad_gain, ("page", "seq"), scatter_dimension=1, tiled=True),
        lax.psum_scatter(grad_shift, ("page", "seq"), scatter_dimension=1, tiled=True),
        lax.psum_scatter(grad_self_in, ("page", "seq"), scatter_dimension=1, tiled=True),
        lax.psum_scatter(grad_self_out, ("page", "seq"), scatter_dimension=0, tiled=True),
        lax.psum_scatter(grad_cross_in, ("page", "seq"), scatter_dimension=1, tiled=True),
        lax.psum_scatter(grad_cross_out, ("page", "seq"), scatter_dimension=0, tiled=True),
        lax.psum_scatter(grad_up, ("page", "seq"), scatter_dimension=0, tiled=True),
        lax.psum_scatter(grad_down, ("page", "seq"), scatter_dimension=0, tiled=True),
        lax.psum_scatter(grad_bias, ("page", "seq"), scatter_dimension=1, tiled=True),
        lax.psum_scatter(grad_up_bias, ("page", "seq"), scatter_dimension=0, tiled=True),
    )
    return (
        layer_rows[None],
        token_grad_rows[None],
        grad_memory[None],
        sum_gain,
        sum_shift,
        sum_self_in,
        sum_self_out,
        sum_cross_in,
        sum_cross_out,
        sum_up,
        sum_down,
        sum_bias,
        sum_up_bias,
    )


def solution(mesh):
    return jax.shard_map(
        on_device,
        mesh=mesh,
        in_specs=(
            P("page", "seq", None),
            P("page", "seq", None),
            P("page", "seq", None),
            P("page"),
            P(None, ("page", "seq")),
            P(None, ("page", "seq")),
            P(None, ("page", "seq"), None),
            P(("page", "seq"), None),
            P(None, ("page", "seq"), None),
            P(("page", "seq"), None),
            P(("page", "seq"), None),
            P(("page", "seq"), None),
            P(None, ("page", "seq")),
            P(("page", "seq")),
        ),
        out_specs=(
            P("page", "seq", None),
            P("page", "seq", None),
            P("page", "seq", None),
            P(None, ("page", "seq")),
            P(None, ("page", "seq")),
            P(None, ("page", "seq"), None),
            P(("page", "seq"), None),
            P(None, ("page", "seq"), None),
            P(("page", "seq"), None),
            P(("page", "seq"), None),
            P(("page", "seq"), None),
            P(None, ("page", "seq")),
            P(("page", "seq")),
        ),
        check_vma=False,
    )
```

profile of v0, /device:TPU:0, one launch (start us, length us, event | category | flops | bytes accessed | tf_op | source)
XLA Modules:
  0.0 3190.2 jit_solution(12310249652979881234)
XLA Ops:
  9.5 70.2 %all-gather.1 = bf16[32,32,3]{1,2,0:T(4,128)(2,1)S(1)} all-gather(bf16[1,32,3]{1,2,0:T(4,128)(2,1)} %bitcast.463), channel_id=1, replica_groups=mesh['page'=8,'seq'=4] {'page','seq'}, dimensions={0}, use_global_device_ids=true | all-gather | bytes 6336 | tf_op jit(solution)/shard_map/all_gather | solution.py:95
  79.8 64.1 %all-gather.2 = bf16[32,32,3]{1,2,0:T(4,128)(2,1)S(1)} all-gather(bf16[1,32,3]{1,2,0:T(4,128)(2,1)} %bitcast.464), channel_id=1, replica_groups=mesh['page'=8,'seq'=4] {'page','seq'}, dimensions={0}, use_global_device_ids=true | all-gather | bytes 6336 | tf_op jit(solution)/shard_map/all_gather | solution.py:96
  151.1 67.3 %all-gather.3 = bf16[32,32,7]{1,2,0:T(8,128)(2,1)S(1)} all-gather(bf16[1,32,7]{1,2,0:T(8,128)(2,1)S(1)} %bitcast.462), channel_id=1, replica_groups=mesh['page'=8,'seq'=4] {'page','seq'}, dimensions={0}, use_global_device_ids=true | all-gather | bytes 14784 | tf_op jit(solution)/shard_map/all_gather | solution.py:103
  226.6 64.3 %all-gather.4 = bf16[32,1,128]{2,1,0:T(2,128)(2,1)S(1)} all-gather(bf16[1,1,128]{2,1,0:T(2,128)(2,1)S(1)} %bitcast.465), channel_id=1, replica_groups=mesh['page'=8,'seq'=4] {'page','seq'}, dimensions={0}, use_global_device_ids=true | all-gather | bytes 8448 | tf_op jit(solution)/shard_map/all_gather | solution.py:104
  314.0 72.2 %while.69 = (s32[]{:T(128)}, f32[16,512]{1,0:T(8,128)S(1)}, f32[16,512]{1,0:T(8,128)S(1)}, s32[4]{0:T(128)S(1)}, bf16[4,512,1024]{1,2,0:T(8,128)(2,1)}, /*index=...) while((s32[]{:T(128)}, f32[16,512]{1,0:T(8,128)S(1)}, ...), condition=%wide.region_5.6_spmd.clone, body=%wide.region_2.5_spmd.clone.sunk | while | flops 570729472 | bytes 38969468 | solution.py:74
  386.3 49.3 %while.70 = (s32[]{:T(128)}, f32[512,16,64]{0,2,1:T(8,128)}, bf16[4,512,1024]{2,1,0:T(8,128)(2,1)}, s32[4]{0:T(128)S(1)}, bf16[4,512,1024]{1,2,0:T(8,128)(2,1)},...) while((s32[]{:T(128)}, f32[512,16,64]{0,2,1:T(8,128)}, ...), condition=%wide.region_7.8_spmd.clone, body=%wide.region_6.7_spmd.clone.sunk | while | flops 1096025088 | bytes 14196875 | solution.py:74
  475.9 70.4 %all-gather.27.cloned.1.call-done = bf16[1024,4096]{1,0:T(8,128)(2,1)} async-done(((bf16[32,4096]{1,0:T(8,128)(2,1)}), bf16[1024,4096]{1,0:T(8,128)(2,1)}) %all-gather.27.cloned.1.call-update) | async-done | bytes 8388624 | tf_op jit(solution)/shard_map/all_gather | solution.py:101
  546.3 28.2 multiply_convert_fusion.2
  574.6 50.7 %all-gather.29.cloned.1.call-done = bf16[4096,1024]{1,0:T(8,128)(2,1)} async-done(((bf16[128,1024]{1,0:T(8,128)(2,1)}), bf16[4096,1024]{1,0:T(8,128)(2,1)}) %all-gather.29.cloned.1.call-update) | async-done | bytes 8388624 | tf_op jit(solution)/shard_map/all_gather | solution.py:102
  625.3 15.4 convert_reduce_fusion
  722.9 477.0 %while.71 = (s32[]{:T(128)}, bf16[512,1024]{0,1:T(8,128)(2,1)}, bf16[512,1024]{0,1:T(8,128)(2,1)S(1)}, f32[512,1024]{0,1:T(8,128)}, f32[512,1024]{0,1:T(8,128)},...) while((s32[]{:T(128)}, bf16[512,1024]{0,1:T(8,128)(2,1)}, ...), condition=%wide.region_21.22_spmd.clone, body=%wide.region_20.21_spmd.clone.sunk | while | flops 2740192256 | bytes 184394288 | solution.py:352
  779.7 19.6 collective-permute-done.3
  802.2 19.6 collective-permute-done
  821.8 21.8 collective-permute-done.1
  900.2 19.6 collective-permute-done.3
  922.7 19.6 collective-permute-done
  942.3 20.9 collective-permute-done.1
  1019.9 19.6 collective-permute-done.3
  1042.3 19.6 collective-permute-done
  1062.0 20.0 collective-permute-done.1
  1138.6 19.6 collective-permute-done.3
  1161.1 19.6 collective-permute-done
  1180.7 19.0 collective-permute-done.1
  1285.9 37.1 %all-reduce = f32[4096]{0:T(1024)S(1)} all-reduce(f32[4096]{0:T(1024)S(1)} %copy-done.69), channel_id=14, replica_groups=mesh['page'=8,'seq'=4] {'page','seq'}, use_global_device_ids=true, to_apply=%region_49.50.clone | all-reduce | flops 4096 | bytes 32768
  1345.2 132.1 %reduce-scatter.38.cloned.1.call-done = f32[32,3]{1,0:T(8,128)} async-done(((f32[1024,3]{1,0:T(8,128)}), f32[32,3]{1,0:T(8,128)}) %reduce-scatter.38.cloned.1.call-update) | async-done | bytes 400
  1484.4 125.4 %reduce-scatter.42.cloned.1.call-done = f32[32,7]{1,0:T(8,128)} async-done(((f32[1024,7]{1,0:T(8,128)}), f32[32,7]{1,0:T(8,128)}) %reduce-scatter.42.cloned.1.call-update) | async-done | bytes 912
  1611.2 145.2 %reduce-scatter.28.cloned.1.call-done = f32[32,1024]{1,0:T(8,128)} async-done(((f32[1024,1024]{1,0:T(8,128)}), f32[32,1024]{1,0:T(8,128)}) %reduce-scatter.28.cloned.1.call-update) | async-done | bytes 131088 | tf_op jit(solution)/shard_map/reduce_scatter | solution.py:395
  1756.4 149.4 %reduce-scatter.24.cloned.1.call-done = f32[32,1024]{1,0:T(8,128)} async-done(((f32[1024,1024]{1,0:T(8,128)}), f32[32,1024]{1,0:T(8,128)}) %reduce-scatter.24.cloned.1.call-update) | async-done | bytes 131088 | tf_op jit(solution)/shard_map/reduce_scatter | solution.py:393
  1905.8 274.6 %reduce-scatter.22.cloned.1.call-done = f32[3,32,1024]{2,1,0:T(8,128)} async-done(((f32[3,1024,1024]{2,1,0:T(8,128)}), f32[3,32,1024]{2,1,0:T(8,128)}) %reduce-scatter.22.cloned.1.call-update) | async-done | bytes 393232 | tf_op jit(solution)/shard_map/reduce_scatter | solution.py:392
  2180.4 273.0 %reduce-scatter.26.cloned.1.call-done = f32[3,32,1024]{2,1,0:T(8,128)} async-done(((f32[3,1024,1024]{2,1,0:T(8,128)}), f32[3,32,1024]{2,1,0:T(8,128)}) %reduce-scatter.26.cloned.1.call-update) | async-done | bytes 393232 | tf_op jit(solution)/shard_map/reduce_scatter | solution.py:394
  2453.4 364.7 %reduce-scatter.30.cloned.1.call-done = f32[32,4096]{1,0:T(8,128)} async-done(((f32[1024,4096]{1,0:T(8,128)}), f32[32,4096]{1,0:T(8,128)}) %reduce-scatter.30.cloned.1.call-update) | async-done | bytes 524304 | tf_op jit(solution)/shard_map/reduce_scatter | solution.py:396
  2818.1 365.0 %reduce-scatter.32.cloned.1.call-done = f32[128,1024]{1,0:T(8,128)} async-done(((f32[4096,1024]{1,0:T(8,128)}), f32[128,1024]{1,0:T(8,128)}) %reduce-scatter.32.cloned.1.call-update) | async-done | bytes 524304 | tf_op jit(solution)/shard_map/reduce_scatter | solution.py:397
  (516 shorter events, 636.9 us)
Async XLA Ops:
  7.2 139.9 %all-gather.15.cloned.1.call-start = ((), (), s32[]{:S(2)}) async-start(), calls=%async_computation.11 | async-start | bytes 6488064 | tf_op jit(solution)/shard_map/all_gather | solution.py:97
  7.9 289.8 %all-gather.31.cloned.1.call-start = ((), (), s32[]{:S(2)}) async-start(), calls=%async_computation.25 | async-start | bytes 1638400 | tf_op jit(solution)/shard_map/all_gather | solution.py:205
  8.7 289.1 %all-gather.23.cloned.1.call-start = ((), (), s32[]{:S(2)}) async-start(), calls=%async_computation.15 | async-start | bytes 6488064 | tf_op jit(solution)/shard_map/all_gather | solution.py:99
  9.4 298.4 %all-gather.19.cloned.1.call-start = ((), (), s32[]{:S(2)}) async-start(), calls=%async_computation.13 | async-start | bytes 5242880 | tf_op jit(solution)/shard_map/all_gather | solution.py:194
  151.0 235.3 %all-gather.17.cloned.1.call-start = ((), (), s32[]{:S(2)}) async-start(), calls=%async_computation.12 | async-start | bytes 5242880 | tf_op jit(solution)/shard_map/all_gather | solution.py:195
  223.0 212.6 %all-gather.21.cloned.1.call-start = ((), (), s32[]{:S(2)}) async-start(), calls=%async_computation.14 | async-start | bytes 2162688 | tf_op jit(solution)/shard_map/all_gather | solution.py:98
  223.6 247.0 %all-gather.25.cloned.1.call-start = ((), (), s32[]{:S(2)}) async-start(), calls=%async_computation.16 | async-start | bytes 2162688 | tf_op jit(solution)/shard_map/all_gather | solution.py:100
  224.4 321.9 %all-gather.27.cloned.1.call-start = ((), (), s32[]{:S(2)}) async-start(), calls=%async_computation.17 | async-start | bytes 8650752 | tf_op jit(solution)/shard_map/all_gather | solution.py:101
  225.1 400.2 %all-gather.29.cloned.1.call-start = ((), (), s32[]{:S(2)}) async-start(), calls=%async_computation.18 | async-start | bytes 8650752 | tf_op jit(solution)/shard_map/all_gather | solution.py:102
  225.8 990.4 %reduce-scatter.36.cloned.1.call-start = ((), (), s32[]{:S(2)}) async-start(), calls=%async_computation.27 | async-start | bytes 1638400
  668.6 584.0 %reduce-scatter.34.cloned.1.call-start = ((), (), s32[]{:S(2)}) async-start(), calls=%async_computation.26 | async-start | bytes 1638400
  722.8 621.0 %reduce-scatter.40.cloned.1.call-start = ((), (), s32[]{:S(2)}) async-start(), calls=%async_computation.29 | async-start | bytes 540672
  760.5 38.8 %collective-permute-start.3 = (bf16[512,1024]{0,1:T(8,128)(2,1)}, bf16[512,1024]{0,1:T(8,128)(2,1)}, u32[]{:S(2)}, u32[]{:S(2)}) collective-permute-start(bf16[512,1024]{0,1:T(8,128)(2,1)} %fusion.219), channel_id=1, source_target_pairs={{0,1},{1,2},{2,3},{3,0},{4,5},{5,6},{6,7},{7,4},{8,9},{9,10},{10,1... | collective-permute-start | bytes 3145736 | tf_op jit(solution)/shard_map/while/body/eval_jaxpr/ppermute | solution.py:28
  761.5 60.3 %collective-permute-start = (bf16[512,1024]{0,1:T(8,128)(2,1)S(1)}, bf16[512,1024]{0,1:T(8,128)(2,1)}, u32[]{:S(2)}, u32[]{:S(2)}) collective-permute-start(bf16[512,1024]{0,1:T(8,128)(2,1)S(1)} %copy.150), channel_id=1, source_target_pairs={{0,1},{1,2},{2,3},{3,0},{4,5},{5,6},{6,7},{7,4},{8,9},{9,10},{10,1... | collective-permute-start | bytes 3145736 | tf_op jit(solution)/shard_map/while/body/eval_jaxpr/ppermute | solution.py:28
  762.2 81.3 %collective-permute-start.1 = (bf16[512,1024]{0,1:T(8,128)(2,1)}, bf16[512,1024]{0,1:T(8,128)(2,1)S(1)}, u32[]{:S(2)}, u32[]{:S(2)}) collective-permute-start(bf16[512,1024]{0,1:T(8,128)(2,1)} %copy.151), channel_id=1, source_target_pairs={{0,1},{1,2},{2,3},{3,0},{4,5},{5,6},{6,7},{7,4},{8,9},{9,10},{10,1... | collective-permute-start | bytes 3145736 | tf_op jit(solution)/shard_map/while/body/eval_jaxpr/ppermute | solution.py:28
  879.4 40.4 %collective-permute-start.3 = (bf16[512,1024]{0,1:T(8,128)(2,1)}, bf16[512,1024]{0,1:T(8,128)(2,1)}, u32[]{:S(2)}, u32[]{:S(2)}) collective-permute-start(bf16[512,1024]{0,1:T(8,128)(2,1)} %fusion.219), channel_id=1, source_target_pairs={{0,1},{1,2},{2,3},{3,0},{4,5},{5,6},{6,7},{7,4},{8,9},{9,10},{10,1... | collective-permute-start | bytes 3145736 | tf_op jit(solution)/shard_map/while/body/eval_jaxpr/ppermute | solution.py:28
  879.9 62.4 %collective-permute-start = (bf16[512,1024]{0,1:T(8,128)(2,1)S(1)}, bf16[512,1024]{0,1:T(8,128)(2,1)}, u32[]{:S(2)}, u32[]{:S(2)}) collective-permute-start(bf16[512,1024]{0,1:T(8,128)(2,1)S(1)} %copy.150), channel_id=1, source_target_pairs={{0,1},{1,2},{2,3},{3,0},{4,5},{5,6},{6,7},{7,4},{8,9},{9,10},{10,1... | collective-permute-start | bytes 3145736 | tf_op jit(solution)/shard_map/while/body/eval_jaxpr/ppermute | solution.py:28
  880.8 82.5 %collective-permute-start.1 = (bf16[512,1024]{0,1:T(8,128)(2,1)}, bf16[512,1024]{0,1:T(8,128)(2,1)S(1)}, u32[]{:S(2)}, u32[]{:S(2)}) collective-permute-start(bf16[512,1024]{0,1:T(8,128)(2,1)} %copy.151), channel_id=1, source_target_pairs={{0,1},{1,2},{2,3},{3,0},{4,5},{5,6},{6,7},{7,4},{8,9},{9,10},{10,1... | collective-permute-start | bytes 3145736 | tf_op jit(solution)/shard_map/while/body/eval_jaxpr/ppermute | solution.py:28
  999.1 40.4 %collective-permute-start.3 = (bf16[512,1024]{0,1:T(8,128)(2,1)}, bf16[512,1024]{0,1:T(8,128)(2,1)}, u32[]{:S(2)}, u32[]{:S(2)}) collective-permute-start(bf16[512,1024]{0,1:T(8,128)(2,1)} %fusion.219), channel_id=1, source_target_pairs={{0,1},{1,2},{2,3},{3,0},{4,5},{5,6},{6,7},{7,4},{8,9},{9,10},{10,1... | collective-permute-start | bytes 3145736 | tf_op jit(solution)/shard_map/while/body/eval_jaxpr/ppermute | solution.py:28
  999.1 62.9 %collective-permute-start = (bf16[512,1024]{0,1:T(8,128)(2,1)S(1)}, bf16[512,1024]{0,1:T(8,128)(2,1)}, u32[]{:S(2)}, u32[]{:S(2)}) collective-permute-start(bf16[512,1024]{0,1:T(8,128)(2,1)S(1)} %copy.150), channel_id=1, source_target_pairs={{0,1},{1,2},{2,3},{3,0},{4,5},{5,6},{6,7},{7,4},{8,9},{9,10},{10,1... | collective-permute-start | bytes 3145736 | tf_op jit(solution)/shard_map/while/body/eval_jaxpr/ppermute | solution.py:28
  999.7 82.2 %collective-permute-start.1 = (bf16[512,1024]{0,1:T(8,128)(2,1)}, bf16[512,1024]{0,1:T(8,128)(2,1)S(1)}, u32[]{:S(2)}, u32[]{:S(2)}) collective-permute-start(bf16[512,1024]{0,1:T(8,128)(2,1)} %copy.151), channel_id=1, source_target_pairs={{0,1},{1,2},{2,3},{3,0},{4,5},{5,6},{6,7},{7,4},{8,9},{9,10},{10,1... | collective-permute-start | bytes 3145736 | tf_op jit(solution)/shard_map/while/body/eval_jaxpr/ppermute | solution.py:28
  1117.8 40.4 %collective-permute-start.3 = (bf16[512,1024]{0,1:T(8,128)(2,1)}, bf16[512,1024]{0,1:T(8,128)(2,1)}, u32[]{:S(2)}, u32[]{:S(2)}) collective-permute-start(bf16[512,1024]{0,1:T(8,128)(2,1)} %fusion.219), channel_id=1, source_target_pairs={{0,1},{1,2},{2,3},{3,0},{4,5},{5,6},{6,7},{7,4},{8,9},{9,10},{10,1... | collective-permute-start | bytes 3145736 | tf_op jit(solution)/shard_map/while/body/eval_jaxpr/ppermute | solution.py:28
  1117.8 62.9 %collective-permute-start = (bf16[512,1024]{0,1:T(8,128)(2,1)S(1)}, bf16[512,1024]{0,1:T(8,128)(2,1)}, u32[]{:S(2)}, u32[]{:S(2)}) collective-permute-start(bf16[512,1024]{0,1:T(8,128)(2,1)S(1)} %copy.150), channel_id=1, source_target_pairs={{0,1},{1,2},{2,3},{3,0},{4,5},{5,6},{6,7},{7,4},{8,9},{9,10},{10,1... | collective-permute-start | bytes 3145736 | tf_op jit(solution)/shard_map/while/body/eval_jaxpr/ppermute | solution.py:28
  1118.4 81.3 %collective-permute-start.1 = (bf16[512,1024]{0,1:T(8,128)(2,1)}, bf16[512,1024]{0,1:T(8,128)(2,1)S(1)}, u32[]{:S(2)}, u32[]{:S(2)}) collective-permute-start(bf16[512,1024]{0,1:T(8,128)(2,1)} %copy.151), channel_id=1, source_target_pairs={{0,1},{1,2},{2,3},{3,0},{4,5},{5,6},{6,7},{7,4},{8,9},{9,10},{10,1... | collective-permute-start | bytes 3145736 | tf_op jit(solution)/shard_map/while/body/eval_jaxpr/ppermute | solution.py:28
  1212.2 265.1 %reduce-scatter.38.cloned.1.call-start = ((), (), s32[]{:S(2)}) async-start(), calls=%async_computation.28 | async-start | bytes 540672
  1216.2 393.7 %reduce-scatter.42.cloned.1.call-start = ((), (), s32[]{:S(2)}) async-start(), calls=%async_computation.30 | async-start | bytes 540672
  1220.6 535.8 %reduce-scatter.28.cloned.1.call-start = ((), (), s32[]{:S(2)}) async-start(), calls=%async_computation.22 | async-start | bytes 4325376 | tf_op jit(solution)/shard_map/reduce_scatter | solution.py:395
  1226.5 679.3 %reduce-scatter.24.cloned.1.call-start = ((), (), s32[]{:S(2)}) async-start(), calls=%async_computation.20 | async-start | bytes 4325376 | tf_op jit(solution)/shard_map/reduce_scatter | solution.py:393
  1232.1 948.3 %reduce-scatter.22.cloned.1.call-start = ((), (), s32[]{:S(2)}) async-start(), calls=%async_computation.19 | async-start | bytes 12976128 | tf_op jit(solution)/shard_map/reduce_scatter | solution.py:392
  1243.5 1209.9 %reduce-scatter.26.cloned.1.call-start = ((), (), s32[]{:S(2)}) async-start(), calls=%async_computation.21 | async-start | bytes 12976128 | tf_op jit(solution)/shard_map/reduce_scatter | solution.py:394
  1261.5 1556.7 %reduce-scatter.30.cloned.1.call-start = ((), (), s32[]{:S(2)}) async-start(), calls=%async_computation.23 | async-start | bytes 17301504 | tf_op jit(solution)/shard_map/reduce_scatter | solution.py:396
  1273.6 1909.5 %reduce-scatter.32.cloned.1.call-start = ((), (), s32[]{:S(2)}) async-start(), calls=%async_computation.24 | async-start | bytes 17301504 | tf_op jit(solution)/shard_map/reduce_scatter | solution.py:397
  (112 other events, 3020.6 us)
Sparse Core Ops, SparseCore 0:
  11.0 71.9 all-gather.14
  84.6 31.9 all-gather.30
  119.6 68.7 all-gather.22
  189.9 79.5 all-gather.18
  271.4 79.4 all-gather.16
  353.7 54.9 all-gather.20
  411.6 55.4 all-gather.24
  470.0 76.2 all-gather.26
  549.2 75.9 all-gather.28
  668.7 29.8 reduce-scatter.35
  722.9 30.0 reduce-scatter.33
  1212.4 131.3 reduce-scatter.39
  1346.7 130.5 reduce-scatter.37
  1479.4 130.3 reduce-scatter.41
  1612.6 143.7 reduce-scatter.27
  1759.2 146.5 reduce-scatter.23
  1908.6 271.6 reduce-scatter.21
  2183.2 270.1 reduce-scatter.25
  2456.4 361.7 reduce-scatter.29
  2821.0 362.1 reduce-scatter.31
where the time goes:
time: 3200 us; the launch traced here: 3190 us
  waiting for transfers between devices  2220 us (69%)
  matrix products  414 us (13%)
  blocking collectives  303 us (9%)
  other arithmetic  116 us (4%)
  local copies, waits for them, and re-layouts  96.1 us (3%)
    reduce_scatter x1, waiting for transfers between devices, on_device(): lax.psum_scatter(grad_down, ('page', 'seq'), scatter_dimension=0, tiled=T...  365 us
    reduce_scatter x1, waiting for transfers between devices, on_device(): lax.psum_scatter(grad_up, ('page', 'seq'), scatter_dimension=0, tiled=True)  365 us
    reduce_scatter x1, waiting for transfers between devices, on_device(): lax.psum_scatter(grad_self_in, ('page', 'seq'), scatter_dimension=1, tile...  275 us
    reduce_scatter x1, waiting for transfers between devices, on_device(): lax.psum_scatter(grad_cross_in, ('page', 'seq'), scatter_dimension=1, til...  273 us
    unnamed x25, waiting for transfers between devices  270 us
    ppermute x16, waiting for transfers between devices, from_behind(): lax.ppermute(value, axis, [(i, (i + by) % count) for i in range(count)])  260 us
    reduce_scatter x1, waiting for transfers between devices, on_device(): lax.psum_scatter(grad_self_out, ('page', 'seq'), scatter_dimension=0, til...  149 us
    reduce_scatter x1, waiting for transfers between devices, on_device(): lax.psum_scatter(grad_cross_out, ('page', 'seq'), scatter_dimension=0, ti...  145 us
  transfers between devices with their start and end apart: 36, of which 27 were waited for; matrix products, arithmetic and copies ran while one was open for 18% of the time, Pallas kernels for 0%

commit v1 on v0

v1 whole, which is shorter than its diff:
```python
import functools

import jax
import jax.numpy as jnp
from jax import lax
from jax.experimental import pallas as pl
from jax.experimental.pallas import tpu as pltpu
from jax.sharding import PartitionSpec as P

HEADS = 16
HEAD_DIM = 64
VALID_HI = 588
VALID_LO = 140

NEGATIVE = -1e30
EPSILON = 1e-05
LOG2E = 1.4426950408889634
SCALING = HEAD_DIM ** (-0.5)
AXES = ("page", "seq")
F32 = jnp.float32
BF16 = jnp.bfloat16
NT = (((1,), (1,)), ((), ()))
NN = (((1,), (0,)), ((), ()))
TN = (((0,), (0,)), ((), ()))


def dot(a, b, dims=NN):
    return lax.dot_general(a, b, dims, preferred_element_type=F32)


def self_fwd_kernel(q_ref, kv_ref, o_ref, lse_ref, *, rows, width):
    i = pl.program_id(1)
    heads = width // HEAD_DIM
    queries = [q_ref[0, :, h * HEAD_DIM : (h + 1) * HEAD_DIM] for h in range(heads)]
    ones = jnp.ones((16, rows), BF16)

    def step(j, carry, diagonal):
        at = pl.ds(pl.multiple_of(j * rows, rows), rows)
        keys_all = kv_ref[0, at, width : 2 * width]
        values_t = kv_ref[0, at, 2 * width : 3 * width].T
        out = []
        for h in range(heads):
            run_max, acc = carry[h]
            lanes = slice(h * HEAD_DIM, (h + 1) * HEAD_DIM)
            scores = dot(keys_all[:, lanes], queries[h], NT) * (SCALING * LOG2E)
            if diagonal:
                place_k = lax.broadcasted_iota(jnp.int32, (rows, rows), 0)
                place_q = lax.broadcasted_iota(jnp.int32, (rows, rows), 1)
                scores = jnp.where(place_k <= place_q, scores, NEGATIVE)
            new_max = jnp.maximum(run_max, jnp.max(scores, axis=0, keepdims=True))
            probs = jnp.exp2(scores - new_max).astype(BF16)
            wide = jnp.concatenate([values_t[lanes], ones], axis=0)
            out.append((new_max, acc * jnp.exp2(run_max - new_max) + dot(wide, probs)))
        return tuple(out)

    start = tuple(
        (jnp.full((1, rows), NEGATIVE, F32), jnp.zeros((HEAD_DIM + 16, rows), F32))
        for _ in range(heads)
    )
    carry = lax.fori_loop(0, i, lambda j, c: step(j, c, False), start)
    carry = step(i, carry, True)
    outs = []
    for h in range(heads):
        run_max, acc = carry[h]
        total = acc[HEAD_DIM : HEAD_DIM + 1]
        outs.append(acc[:HEAD_DIM] / total)
        lse_ref[0, h] = run_max + jnp.log2(total)
    o_ref[0] = jnp.concatenate(outs, axis=0).T.astype(BF16)


def self_fwd(qkv, rows):
    pages, length, three = qkv.shape
    width = three // 3
    heads = width // HEAD_DIM
    blocks = length // rows
    cost = pages * heads * length * length * HEAD_DIM * 2
    return pl.pallas_call(
        functools.partial(self_fwd_kernel, rows=rows, width=width),
        grid=(pages, blocks),
        in_specs=[
            pl.BlockSpec((1, rows, three), lambda p, i: (p, i, 0)),
            pl.BlockSpec((1, length, three), lambda p, i: (p, 0, 0)),
        ],
        out_specs=[
            pl.BlockSpec((1, rows, width), lambda p, i: (p, i, 0)),
            pl.BlockSpec((1, heads, 1, rows), lambda p, i: (p, 0, 0, i)),
        ],
        out_shape=[
            jax.ShapeDtypeStruct((pages, length, width), BF16),
            jax.ShapeDtypeStruct((pages, heads, 1, length), F32),
        ],
        compiler_params=pltpu.CompilerParams(vmem_limit_bytes=48 * 1024 * 1024),
        cost_estimate=pl.CostEstimate(
            flops=2 * cost, bytes_accessed=8 * qkv.size, transcendentals=cost // 256
        ),
    )(qkv, qkv)


def self_bwd_kernel(q_ref, kv_ref, do_ref, o_ref, lse_ref, out_ref, dk_acc, dv_acc, *, rows, width):
    i = pl.program_id(1)
    heads = width // HEAD_DIM

    @pl.when(i == 0)
    def _():
        dk_acc[...] = jnp.zeros_like(dk_acc)
        dv_acc[...] = jnp.zeros_like(dv_acc)

    q_all = q_ref[0, :, :width]
    do_all = do_ref[0]
    prod = (do_all.astype(F32) * o_ref[0].astype(F32)).T
    per_head = [slice(h * HEAD_DIM, (h + 1) * HEAD_DIM) for h in range(heads)]
    deltas = [jnp.sum(prod[s], axis=0, keepdims=True) for s in per_head]

    def step(j, carry, diagonal):
        at = pl.ds(pl.multiple_of(j * rows, rows), rows)
        k_all = kv_ref[0, at, width : 2 * width]
        v_all = kv_ref[0, at, 2 * width : 3 * width]
        k_t = k_all.T
        new, dks, dvs = [], [], []
        for h in range(heads):
            s = per_head[h]
            scores = dot(k_all[:, s], q_all[:, s], NT) * (SCALING * LOG2E)
            probs = jnp.exp2(scores - lse_ref[0, h])
            if diagonal:
                place_k = lax.broadcasted_iota(jnp.int32, (rows, rows), 0)
                place_q = lax.broadcasted_iota(jnp.int32, (rows, rows), 1)
                probs = jnp.where(place_k <= place_q, probs, 0.0)
            d_probs = dot(v_all[:, s], do_all[:, s], NT)
            d_scores = (probs * (d_probs - deltas[h])).astype(BF16)
            dvs.append(dot(probs.astype(BF16), do_all[:, s]))
            dks.append(dot(d_scores, q_all[:, s]))
            new.append(carry[h] + dot(k_t[s], d_scores))
        dk_acc[at, :] += jnp.concatenate(dks, axis=1)
        dv_acc[at, :] += jnp.concatenate(dvs, axis=1)
        return tuple(new)

    start = tuple(jnp.zeros((HEAD_DIM, rows), F32) for _ in range(heads))
    carry = lax.fori_loop(0, i, lambda j, c: step(j, c, False), start)
    carry = step(i, carry, True)
    dq = (jnp.concatenate(carry, axis=0) * SCALING).T.astype(BF16)
    out_ref[0, pl.ds(pl.multiple_of(i * rows, rows), rows), :width] = dq

    @pl.when(i == pl.num_programs(1) - 1)
    def _():
        out_ref[0, :, width : 2 * width] = (dk_acc[...] * SCALING).astype(BF16)
        out_ref[0, :, 2 * width :] = dv_acc[...].astype(BF16)


def self_bwd(qkv, d_out, out, lse, rows):
    pages, length, three = qkv.shape
    width = three // 3
    heads = width // HEAD_DIM
    cost = pages * heads * length * length * HEAD_DIM * 5
    return pl.pallas_call(
        functools.partial(self_bwd_kernel, rows=rows, width=width),
        grid=(pages, length // rows),
        in_specs=[
            pl.BlockSpec((1, rows, three), lambda p, i: (p, i, 0)),
            pl.BlockSpec((1, length, three), lambda p, i: (p, 0, 0)),
            pl.BlockSpec((1, rows, width), lambda p, i: (p, i, 0)),
            pl.BlockSpec((1, rows, width), lambda p, i: (p, i, 0)),
            pl.BlockSpec((1, heads, 1, rows), lambda p, i: (p, 0, 0, i)),
        ],
        out_specs=pl.BlockSpec((1, length, three), lambda p, i: (p, 0, 0)),
        out_shape=jax.ShapeDtypeStruct((pages, length, three), BF16),
        scratch_shapes=[pltpu.VMEM((length, width), F32), pltpu.VMEM((length, width), F32)],
        compiler_params=pltpu.CompilerParams(vmem_limit_bytes=48 * 1024 * 1024),
        cost_estimate=pl.CostEstimate(
            flops=2 * cost, bytes_accessed=12 * qkv.size, transcendentals=cost // 640
        ),
    )(qkv, qkv, d_out, out, lse)


def cross_fwd_kernel(limit_ref, q_ref, k_ref, v_ref, o_ref, lse_ref):
    limit = limit_ref[0]
    rows, mem = q_ref.shape[0], k_ref.shape[0]
    valid = lax.broadcasted_iota(jnp.int32, (mem, rows), 0) < limit
    values_t = v_ref[...].T
    ones = jnp.ones((16, mem), BF16)
    outs = []
    for h in range(2):
        s = slice(h * HEAD_DIM, (h + 1) * HEAD_DIM)
        scores = dot(k_ref[:, s], q_ref[:, s], NT) * (SCALING * LOG2E)
        scores = jnp.where(valid, scores, NEGATIVE)
        top = jnp.max(scores, axis=0, keepdims=True)
        probs = jnp.exp2(scores - top).astype(BF16)
        acc = dot(jnp.concatenate([values_t[s], ones], axis=0), probs)
        total = acc[HEAD_DIM : HEAD_DIM + 1]
        outs.append(acc[:HEAD_DIM] / total)
        lse_ref[0, h : h + 1] = top + jnp.log2(total)
    o_ref[...] = jnp.concatenate(outs, axis=0).T.astype(BF16)


def cross_fwd(limit, q, kv):
    rows, width = q.shape
    mem = kv.shape[0]
    pairs = width // (2 * HEAD_DIM)
    wide = 2 * HEAD_DIM
    cost = width * rows * mem * 2
    return pl.pallas_call(
        cross_fwd_kernel,
        grid_spec=pltpu.PrefetchScalarGridSpec(
            num_scalar_prefetch=1,
            grid=(pairs,),
            in_specs=[
                pl.BlockSpec((rows, wide), lambda p, n: (0, p)),
                pl.BlockSpec((mem, wide), lambda p, n: (0, p)),
                pl.BlockSpec((mem, wide), lambda p, n: (0, p + pairs)),
            ],
            out_specs=[
                pl.BlockSpec((rows, wide), lambda p, n: (0, p)),
                pl.BlockSpec((1, 2, rows), lambda p, n: (p, 0, 0)),
            ],
        ),
        out_shape=[
            jax.ShapeDtypeStruct((rows, width), BF16),
            jax.ShapeDtypeStruct((pairs, 2, rows), F32),
        ],
        compiler_params=pltpu.CompilerParams(vmem_limit_bytes=48 * 1024 * 1024),
        cost_estimate=pl.CostEstimate(
            flops=2 * cost, bytes_accessed=4 * (q.size + kv.size), transcendentals=cost // 128
        ),
    )(limit, q, kv, kv)


def cross_bwd_kernel(limit_ref, q_ref, k_ref, v_ref, do_ref, o_ref, lse_ref, dq_ref, dk_ref, dv_ref):
    limit = limit_ref[0]
    rows, mem = q_ref.shape[0], k_ref.shape[0]
    valid = lax.broadcasted_iota(jnp.int32, (mem, rows), 0) < limit
    k_t = k_ref[...].T
    prod = (do_ref[...].astype(F32) * o_ref[...].astype(F32)).T
    dqs, dks, dvs = [], [], []
    for h in range(2):
        s = slice(h * HEAD_DIM, (h + 1) * HEAD_DIM)
        delta = jnp.sum(prod[s], axis=0, keepdims=True)
        scores = dot(k_ref[:, s], q_ref[:, s], NT) * (SCALING * LOG2E)
        scores = jnp.where(valid, scores, NEGATIVE)
        probs = jnp.exp2(scores - lse_ref[0, h : h + 1])
        d_probs = dot(v_ref[:, s], do_ref[:, s], NT)
        d_scores = (probs * (d_probs - delta)).astype(BF16)
        dvs.append(dot(probs.astype(BF16), do_ref[:, s]))
        dks.append(dot(d_scores, q_ref[:, s]))
        dqs.append(dot(k_t[s], d_scores))
    dq_ref[...] = (jnp.concatenate(dqs, axis=0) * SCALING).T.astype(BF16)
    dk_ref[...] = (jnp.concatenate(dks, axis=1) * SCALING).astype(BF16)
    dv_ref[...] = jnp.concatenate(dvs, axis=1).astype(BF16)


def cross_bwd(limit, q, kv, d_out, out, lse):
    rows, width = q.shape
    mem = kv.shape[0]
    pairs = width // (2 * HEAD_DIM)
    wide = 2 * HEAD_DIM
    cost = width * rows * mem * 5
    token_block = pl.BlockSpec((rows, wide), lambda p, n: (0, p))
    memory_block = pl.BlockSpec((mem, wide), lambda p, n: (0, p))
    return pl.pallas_call(
        cross_bwd_kernel,
        grid_spec=pltpu.PrefetchScalarGridSpec(
            num_scalar_prefetch=1,
            grid=(pairs,),
            in_specs=[
                token_block,
                memory_block,
                pl.BlockSpec((mem, wide), lambda p, n: (0, p + pairs)),
                token_block,
                token_block,
                pl.BlockSpec((1, 2, rows), lambda p, n: (p, 0, 0)),
            ],
            out_specs=[token_block, memory_block, memory_block],
        ),
        out_shape=[
            jax.ShapeDtypeStruct((rows, width), BF16),
            jax.ShapeDtypeStruct((mem, width), BF16),
            jax.ShapeDtypeStruct((mem, width), BF16),
        ],
        compiler_params=pltpu.CompilerParams(vmem_limit_bytes=48 * 1024 * 1024),
        cost_estimate=pl.CostEstimate(
            flops=2 * cost, bytes_accessed=6 * (q.size + kv.size), transcendentals=cost // 320
        ),
    )(limit, q, kv, kv, d_out, out, lse)


def gray(n):
    return n ^ (n >> 1)


class Net:
    def __init__(self, mesh):
        self.pages, self.seq = mesh.shape["page"], mesh.shape["seq"]
        self.chips = self.pages // 2
        page = lax.axis_index("page")
        self.core = lax.rem(page, 2)
        self.chip = lax.div(page, 2)
        self.z = lax.axis_index("seq")
        place = self.chip
        shift = 1
        while (self.chips - 1) >> shift:
            place = place ^ (self.chip >> shift)
            shift += 1
        self.place = place
        where = {gray(j): j for j in range(self.chips)}

        def index(chip, core, z):
            return (chip * 2 + core) * self.seq + z

        everyone = [
            (chip, core, z)
            for chip in range(self.chips)
            for core in range(2)
            for z in range(self.seq)
        ]
        self.pair_map = [(index(h, c, z), index(h, 1 - c, z)) for h, c, z in everyone]
        self.line_map = [
            [(index(h, c, z), index(h, c, (z + s) % self.seq)) for h, c, z in everyone]
            for s in range(self.seq)
        ]
        self.ring_map = {
            way: [
                (index(h, c, z), index(gray((where[h] + way) % self.chips), c, z))
                for h, c, z in everyone
            ]
            for way in (1, -1)
        }

    def sibling(self, value):
        return lax.ppermute(value, AXES, self.pair_map)

    def along(self, value, by):
        return lax.ppermute(value, AXES, self.line_map[by % self.seq])

    def around(self, value, way):
        return lax.ppermute(value, AXES, self.ring_map[way])

    def chip_at(self, by):
        j = lax.rem(self.place + by + self.chips, self.chips)
        return j ^ (j >> 1)

    def z_at(self, by):
        return lax.rem(self.z + by + self.seq, self.seq)


def put(buffer, piece, index, axis):
    return lax.dynamic_update_slice_in_dim(buffer, jnp.expand_dims(piece, axis), index, axis)


def pick(buffer, index, axis=0):
    return lax.dynamic_index_in_dim(buffer, index, axis, keepdims=False)


def line_gather(net, piece, axis):
    shape = piece.shape[:axis] + (net.seq,) + piece.shape[axis:]
    out = put(jnp.zeros(shape, piece.dtype), piece, net.z, axis)
    for s in range(1, net.seq):
        out = put(out, net.along(piece, s), net.z_at(-s), axis)
    return out


def ring_gather(net, piece):
    half = piece.shape[0] // 2
    out = put(jnp.zeros((net.chips,) + piece.shape, piece.dtype), piece, net.chip, 0)
    right, left = piece, piece
    for t in range(1, net.chips // 2):
        right, left = net.around(right, 1), net.around(left, -1)
        out = put(out, right, net.chip_at(-t), 0)
        out = put(out, left, net.chip_at(t), 0)
    far = net.chip_at(net.chips // 2)
    right, left = net.around(right[:half], 1), net.around(left[half:], -1)
    return put(out, jnp.concatenate([right, left], axis=0), far, 0)


def ring_scatter(net, parts):
    half = parts.shape[1] // 2
    steps = net.chips // 2
    far = pick(parts, net.chip_at(steps))
    right, left = net.around(far[:half], 1), net.around(far[half:], -1)
    for t in range(1, steps):
        k = steps - t
        mine = pick(parts, net.chip_at(k))
        if t == 1:
            first = mine[:half].astype(F32) + right.astype(F32)
            sent = jnp.concatenate([first.astype(BF16), mine[half:]], axis=0)
        else:
            sent = (mine.astype(F32) + right.astype(F32)).astype(BF16)
        mine = pick(parts, net.chip_at(-k))
        if t == 1:
            first = mine[half:].astype(F32) + left.astype(F32)
            back = jnp.concatenate([mine[:half], first.astype(BF16)], axis=0)
        else:
            back = (mine.astype(F32) + left.astype(F32)).astype(BF16)
        right, left = net.around(sent, 1), net.around(back, -1)
    return pick(parts, net.chip).astype(F32) + right.astype(F32) + left.astype(F32)


def line_scatter(net, parts, axis):
    low = parts.astype(BF16)
    total = pick(parts, net.z, axis).astype(F32)
    for s in range(1, net.seq):
        total += net.along(pick(low, net.z_at(s), axis), s).astype(F32)
    return total


def own_first(net, value):
    return pick(value, net.core), pick(value, 1 - net.core)


def by_core(net, own, other):
    return jnp.where(net.core == 0, jnp.stack([own, other]), jnp.stack([other, own]))


def gather_columns(net, shard):
    own, other = own_first(net, jnp.moveaxis(shard, 1, 0))
    piece = by_core(net, own, net.sibling(other))
    full = ring_gather(net, line_gather(net, piece, 1))
    return full.reshape(-1, full.shape[-1])


def gather_rows(net, shard):
    full = ring_gather(net, line_gather(net, shard, 0))
    return full.reshape(-1, full.shape[-1])


def scatter_columns(net, grad, rows):
    parts = grad.reshape(net.chips, 2, net.seq, rows, grad.shape[-1])
    mine = line_scatter(net, ring_scatter(net, parts), 1)
    own, other = own_first(net, mine)
    return jnp.moveaxis(by_core(net, own, net.sibling(other)), 0, 1)


def scatter_rows(net, grad, rows):
    parts = grad.reshape(net.chips, net.seq, rows, grad.shape[-1])
    return line_scatter(net, ring_scatter(net, parts), 0)


def norm_parts(values):
    centered = values - jnp.mean(values, axis=-1, keepdims=True)
    scale = lax.rsqrt(jnp.mean(centered * centered, axis=-1, keepdims=True) + EPSILON)
    return centered * scale, scale


def layer_norm(values, gain, shift):
    return (norm_parts(values)[0] * gain + shift).astype(BF16)


def norm_back(values, gain, upstream):
    normed, scale = norm_parts(values)
    scaled = upstream * gain
    mean_g = jnp.mean(scaled, axis=-1, keepdims=True)
    mean_gn = jnp.mean(scaled * normed, axis=-1, keepdims=True)
    grad = (scaled - mean_g - normed * mean_gn) * scale
    return grad, jnp.sum(upstream * normed, axis=0), jnp.sum(upstream, axis=0)


def column_sum(values):
    return jnp.sum(values.astype(F32), axis=0)


def on_device(
    tokens,
    memory,
    cotangent,
    res_flag,
    ln_gain,
    ln_bias,
    self_in,
    self_out,
    cross_in,
    cross_out,
    ff_in,
    ff_out,
    proj_bias,
    ff_bias,
    *,
    mesh,
):
    net = Net(mesh)
    core, z = net.core, net.z
    rows, width = tokens.shape[1], tokens.shape[2]
    seq, chips, pages = net.seq, net.chips, net.pages
    shard = self_in.shape[1]
    hidden = ff_in.shape[1]
    ff_shard = ff_out.shape[0]
    lanes = width // (2 * seq)
    half = width // 2
    tok, mem, cot = tokens[0], memory[0], cotangent[0]

    flag = jnp.broadcast_to(res_flag.astype(BF16)[:, None], (1, shard))
    small = jnp.concatenate(
        [ln_gain, ln_bias, proj_bias, flag, ff_bias.reshape(ff_shard // shard, shard)], axis=0
    )
    small = lax.all_gather(small, AXES, axis=0)
    vectors = jnp.moveaxis(small[:, :13], 0, 1).reshape(13, width).astype(F32)
    gain, shift, bias = vectors[0:3], vectors[3:6], vectors[6:13]
    flags = small[:, 13, 0].reshape(pages, seq)[:, 0].astype(F32)
    up_bias = small[:, 14:].reshape(chips, 2, seq * ff_shard)
    up_bias = pick(up_bias, core, 1).reshape(hidden // 2).astype(F32)
    page = lax.axis_index("page")

    def limit_of(which):
        return jnp.where(pick(flags, which) > 0.5, VALID_HI, VALID_LO).astype(jnp.int32).reshape(1)

    limit_own, limit_other = limit_of(page), limit_of(page ^ 1)

    def halves(vector):
        return pick(vector.reshape(pages // 2, 2, width // pages), core, 1).reshape(half)

    def column_halves(weight):
        lead, columns = weight.shape[:-1], weight.shape[-1]
        split = weight.reshape(lead + (pages // 2, 2, columns // pages))
        return jnp.moveaxis(split, -2, -3).reshape(lead + (2, columns // 2))

    def join_halves(weight):
        lead, columns = weight.shape[:-2], weight.shape[-1] * 2
        split = weight.reshape(lead + (2, pages // 2, columns // pages))
        return jnp.moveaxis(split, -3, -2).reshape(lead + (columns,))

    blocks = self_in.reshape(3, shard, seq, 2, lanes).transpose(3, 2, 1, 0, 4)
    blocks = blocks.reshape(2, seq, shard, 3 * lanes)
    own, other = own_first(net, blocks)
    blocks = by_core(net, own, net.sibling(other))
    piece = jnp.zeros_like(blocks)
    piece = put(piece, pick(blocks, z, 1), z, 1)
    for s in range(1, seq):
        piece = put(piece, net.along(pick(blocks, net.z_at(s), 1), s), net.z_at(-s), 1)
    w_qkv = ring_gather(net, piece).reshape(width, 3 * lanes)
    first = (2 * z + core) * lanes
    b_qkv = jnp.concatenate(
        [
            lax.dynamic_slice_in_dim(bias[0], first, lanes),
            jnp.zeros((lanes,), F32),
            lax.dynamic_slice_in_dim(bias[1], first, lanes),
        ]
    )

    h_all = jnp.zeros((2, seq, rows, width), BF16)
    qkv = jnp.zeros((2, seq, rows, 3 * lanes), BF16)
    passing = tok
    h_one = None
    for t in range(seq):
        if t:
            passing = net.along(passing, 1)
        both = jnp.stack([passing, net.sibling(passing)])
        h = layer_norm(both.astype(F32), gain[0], shift[0])
        h_all = put(h_all, h, net.z_at(-t), 1)
        part = dot(h.reshape(2 * rows, width), w_qkv) + b_qkv
        qkv = put(qkv, part.astype(BF16).reshape(2, rows, 3 * lanes), net.z_at(-t), 1)
    h_all = h_all.reshape(2 * seq * rows, width)
    qkv = qkv.reshape(2, seq * rows, 3 * lanes)

    w_outs = gather_rows(net, jnp.concatenate([self_out, cross_out], axis=1))
    w_self_out, w_cross_out = w_outs[:, :width], w_outs[:, width:]
    cross_halves = column_halves(cross_in)
    cross_halves = cross_halves.transpose(1, 2, 0, 3).reshape(shard, 2, 3 * half)
    w_cross = gather_columns(net, cross_halves)
    w_cross_q, w_cross_kv = w_cross[:, :half], w_cross[:, half:]
    w_up = gather_columns(net, column_halves(ff_in))
    w_down = gather_rows(net, ff_out)
    cot_two = jnp.concatenate([cot, net.sibling(cot)], axis=0)

    mem_page = line_gather(net, mem, 0).reshape(-1, width)
    mem_all = jnp.concatenate([mem_page, net.sibling(mem_page)], axis=0)
    mem_rows = mem_page.shape[0]
    b_kv = jnp.concatenate([jnp.zeros((half,), F32), halves(bias[4])])
    kv_cross = (dot(mem_all, w_cross_kv) + b_kv).astype(BF16)
    kv_own, kv_other = kv_cross[:mem_rows], kv_cross[mem_rows:]

    att_rows = min(512, rows)
    o_self, lse_self = self_fwd(qkv, att_rows)

    def to_tokens(value):
        blocks = value.reshape(2, seq, rows, lanes)
        out = jnp.zeros((2, rows, seq, lanes), BF16)
        out = put(out, pick(blocks, z, 1), z, 2)
        for s in range(1, seq):
            out = put(out, net.along(pick(blocks, net.z_at(s), 1), s), net.z_at(-s), 2)
        return out.reshape(2 * rows, half)

    def to_heads(value):
        blocks = value.reshape(2, rows, seq, lanes)
        out = jnp.zeros((2, seq, rows, lanes), BF16)
        out = put(out, pick(blocks, z, 2), z, 1)
        for s in range(1, seq):
            out = put(out, net.along(pick(blocks, net.z_at(s), 2), s), net.z_at(-s), 1)
        return out.reshape(2, seq * rows, lanes)

    def summed(rows_two, weight, dims=NN):
        sent = dot(rows_two[rows:], weight, dims).astype(BF16)
        back = net.sibling(sent)
        return dot(rows_two[:rows], weight, dims) + back.astype(F32)

    def both_pages(value):
        return jnp.concatenate([value, net.sibling(value)], axis=0)

    attended = to_tokens(o_self)
    x_in = tok.astype(F32)
    x_one = x_in + summed(attended, w_self_out) + bias[2]

    h_two = both_pages(layer_norm(x_one, gain[1], shift[1]))
    q_cross = (dot(h_two, w_cross_q) + halves(bias[3])).astype(BF16)
    oc_own, lse_own = cross_fwd(limit_own, q_cross[:rows], kv_own)
    oc_other, lse_other = cross_fwd(limit_other, q_cross[rows:], kv_other)
    o_cross = jnp.concatenate([oc_own, oc_other], axis=0)
    x_two = x_one + summed(o_cross, w_cross_out) + bias[5]

    h_three = both_pages(layer_norm(x_two, gain[2], shift[2]))
    pre_act = dot(h_three, w_up) + up_bias
    cdf = 0.5 + 0.5 * lax.erf(pre_act * (0.5**0.5))
    act = (pre_act * cdf).astype(BF16)
    layer_rows = (x_two + summed(act, w_down) + bias[6]).astype(BF16)

    slope = cdf + pre_act * (jnp.exp(-0.5 * pre_act * pre_act) * 0.3989422804014327)
    g_pre = (dot(cot_two, w_down, NT) * slope).astype(BF16)
    grad_down = dot(act, cot_two, TN).astype(BF16)
    grad_up = dot(h_three, g_pre, TN).astype(BF16)
    sum_down = scatter_rows(net, grad_down, ff_shard)
    sum_up = join_halves(scatter_columns(net, grad_up, shard))
    cot_wide = cot.astype(F32)
    back, d_gain2, d_shift2 = norm_back(x_two, gain[2], summed(g_pre, w_up, NT))
    g_two = cot_wide + back

    g_cross = both_pages(g_two.astype(BF16))
    grad_cross_out = dot(o_cross, g_cross, TN).astype(BF16)
    d_oc = dot(g_cross, w_cross_out, NT).astype(BF16)
    dq_own, dk_own, dv_own = cross_bwd(
        limit_own, q_cross[:rows], kv_own, d_oc[:rows], oc_own, lse_own
    )
    dq_other, dk_other, dv_other = cross_bwd(
        limit_other, q_cross[rows:], kv_other, d_oc[rows:], oc_other, lse_other
    )
    dq_cross = jnp.concatenate([dq_own, dq_other], axis=0)
    dkv_own = jnp.concatenate([dk_own, dv_own], axis=1)
    dkv_other = jnp.concatenate([dk_other, dv_other], axis=1)
    dkv_cross = jnp.concatenate([dkv_own, dkv_other], axis=0)
    grad_cross = jnp.concatenate(
        [dot(h_two, dq_cross, TN).astype(BF16), dot(mem_all, dkv_cross, TN).astype(BF16)], axis=1
    )
    sum_cross = scatter_columns(net, grad_cross, shard)
    sum_cross = sum_cross.reshape(shard, 2, 3, half).transpose(2, 0, 1, 3)
    sum_cross = join_halves(sum_cross)
    mem_sent = dot(dkv_other, w_cross_kv, NT).astype(BF16)
    mem_grad = dot(dkv_own, w_cross_kv, NT) + net.sibling(mem_sent).astype(F32)
    grad_memory = line_scatter(net, mem_grad.reshape(seq, -1, width), 0)
    back, d_gain1, d_shift1 = norm_back(x_one, gain[1], summed(dq_cross, w_cross_q, NT))
    g_one = g_two + back

    g_self = both_pages(g_one.astype(BF16))
    grad_self_out = dot(attended, g_self, TN).astype(BF16)
    sum_outs = scatter_rows(net, jnp.concatenate([grad_self_out, grad_cross_out], axis=1), shard)
    d_os = to_heads(dot(g_self, w_self_out, NT).astype(BF16))
    d_qkv = self_bwd(qkv, d_os, o_self, lse_self, att_rows)
    other_h = dot(d_qkv[1], w_qkv, NT).astype(BF16)
    d_h = dot(d_qkv[0], w_qkv, NT) + net.sibling(other_h).astype(F32)
    d_h = line_scatter(net, d_h.reshape(seq, rows, width), 0)
    flat = d_qkv.reshape(2 * seq * rows, 3 * lanes)
    grad_qkv = dot(h_all, flat, TN).astype(BF16)
    parts = ring_scatter(net, grad_qkv.reshape(chips, 2, seq * shard, 3 * lanes))
    parts = parts.astype(BF16).reshape(2, seq, shard, 3 * lanes)
    piece = jnp.zeros_like(parts)
    piece = put(piece, pick(parts, z, 1), z, 1)
    for s in range(1, seq):
        piece = put(piece, net.along(pick(parts, net.z_at(s), 1), s), net.z_at(-s), 1)
    own, other = own_first(net, piece)
    piece = by_core(net, own, net.sibling(other))
    sum_self = piece.reshape(2, seq, shard, 3, lanes).transpose(3, 2, 1, 0, 4)
    sum_self = sum_self.reshape(3, shard, width).astype(F32)
    back, d_gain0, d_shift0 = norm_back(x_in, gain[0], d_h)
    token_grad = g_one + back

    def spread(vector):
        split = vector.reshape(pages // 2, 1, width // pages)
        here = jnp.arange(2)[None, :, None] == core
        return jnp.where(here, split, 0.0).reshape(width)

    def spread_heads(vector):
        return lax.dynamic_update_slice_in_dim(jnp.zeros((width,), F32), vector, first, 0)

    sums_qkv = column_sum(flat)
    up_sum = column_sum(g_pre).reshape(chips, 1, seq * ff_shard)
    up_sum = jnp.where(jnp.arange(2)[None, :, None] == core, up_sum, 0.0)
    vectors = jnp.stack(
        [
            d_gain0,
            d_gain1,
            d_gain2,
            d_shift0,
            d_shift1,
            d_shift2,
            spread_heads(sums_qkv[:lanes]),
            spread_heads(sums_qkv[2 * lanes :]),
            column_sum(g_one),
            spread(column_sum(dq_cross)),
            spread(column_sum(dkv_cross[:, half:])),
            column_sum(g_two),
            column_sum(cot_wide),
        ]
    )
    vectors = jnp.moveaxis(vectors.reshape(13, pages * seq, shard), 0, 1)
    packed = jnp.concatenate(
        [vectors.reshape(pages * seq, 13 * shard), up_sum.reshape(pages * seq, ff_shard)], axis=1
    )
    packed = lax.psum_scatter(packed, AXES, scatter_dimension=0, tiled=True)[0]
    vectors = packed[: 13 * shard].reshape(13, shard)
    return (
        layer_rows[None],
        token_grad[None],
        grad_memory[None],
        vectors[0:3],
        vectors[3:6],
        sum_self,
        sum_outs[:, :width],
        sum_cross,
        sum_outs[:, width:],
        sum_up,
        sum_down,
        vectors[6:13],
        packed[13 * shard :],
    )


def solution(mesh):
    weight = P(AXES, None)
    return jax.shard_map(
        functools.partial(on_device, mesh=mesh),
        mesh=mesh,
        in_specs=(
            P("page", "seq", None),
            P("page", "seq", None),
            P("page", "seq", None),
            P("page"),
            P(None, AXES),
            P(None, AXES),
            P(None, AXES, None),
            weight,
            P(None, AXES, None),
            weight,
            weight,
            weight,
            P(None, AXES),
            P(AXES),
        ),
        out_specs=(
            P("page", "seq", None),
            P("page", "seq", None),
            P("page", "seq", None),
            P(None, AXES),
            P(None, AXES),
            P(None, AXES, None),
            weight,
            P(None, AXES, None),
            weight,
            weight,
            weight,
            P(None, AXES),
            P(AXES),
        ),
        check_vma=False,
    )
```

time: 3200 us -> 1100 us (0.34)
  waiting for transfers between devices: 2220 us -> 468 us
  matrix products: 414 us -> 111 us
  blocking collectives: 303 us -> 66.9 us
  starting transfers between devices: 20.7 us -> 143 us
  Pallas kernels: 0 us -> 85.4 us
  other arithmetic: 116 us -> 69.4 us
    reduce_scatter x6 -> x0, waiting for transfers between devices: 1570 us -> none  [the longest x1 365 us: on_device(): lax.psum_scatter(grad_down, ('page', 'seq'), scatter_dimension=0, tiled=T...]
    dot_general x63 -> x31, matrix products: 403 us -> 111 us  [dot(): return lax.dot_general(a, b, dims, preferred_element_type=F32)]
    all_gather x4 -> x1, blocking collectives: 266 us -> 66.9 us  [on_device(): small = lax.all_gather(small, AXES, axis=0)]
    unnamed x25 -> x2, waiting for transfers between devices: 270 us -> 114 us
    ppermute x16 -> x111, starting transfers between devices: 19.3 us -> 143 us  [the longest x48 96.9 us: along(): return lax.ppermute(value, AXES, self.line_map[by % self.seq])]
    all_gather x9 -> x0, waiting for transfers between devices: 121 us -> none  [the longest x1 70.4 us: on_device(): lax.all_gather(ff_in, ('page', 'seq'), axis=0, tiled=True)]
    ppermute x16 -> x111, waiting for transfers between devices: 260 us -> 354 us  [the longest x48 260 us: along(): return lax.ppermute(value, AXES, self.line_map[by % self.seq])]
    pallas_call x0 -> x6, Pallas kernels: none -> 85.4 us  [the longest x1 33.2 us: self_bwd(): pl.pallas_call(functools.partial(self_bwd_kernel, rows=rows, width=width)...]
  transfers between devices with their start and end apart: 36 -> 112, of which waited for: 27 -> 48; matrix products, arithmetic and copies ran while one was open for 18% -> 24% of each run, Pallas kernels for 0% -> 8%
where the time goes in v1:
time: 1100 us; the launch traced here: 1090 us
  waiting for transfers between devices  468 us (43%)
  starting transfers between devices  143 us (13%)
  local copies, waits for them, and re-layouts  127 us (12%)
  matrix products  111 us (10%)
  Pallas kernels  85.4 us (8%)
  other arithmetic  69.4 us (6%)
  blocking collectives  66.9 us (6%)
  between operations  18.9 us (2%)
    ppermute x48, waiting for transfers between devices, along(): return lax.ppermute(value, AXES, self.line_map[by % self.seq])  260 us
    unnamed x2, waiting for transfers between devices  114 us
    dot_general x31, matrix products, dot(): return lax.dot_general(a, b, dims, preferred_element_type=F32)  111 us
    ppermute x48, starting transfers between devices, along(): return lax.ppermute(value, AXES, self.line_map[by % self.seq])  96.9 us
    ppermute x40, waiting for transfers between devices, around(): return lax.ppermute(value, AXES, self.ring_map[way])  91.9 us
    all_gather x1, blocking collectives, on_device(): small = lax.all_gather(small, AXES, axis=0)  66.9 us
    ppermute x40, starting transfers between devices, around(): return lax.ppermute(value, AXES, self.ring_map[way])  43.7 us
    pallas_call x1, Pallas kernels, self_bwd(): pl.pallas_call(functools.partial(self_bwd_kernel, rows=rows, width=width)...  33.2 us
  transfers between devices with their start and end apart: 112, of which 48 were waited for; matrix products, arithmetic and copies ran while one was open for 24% of the time, Pallas kernels for 8%

profile of v1, /device:TPU:0, one launch (start us, length us, event | category | flops | bytes accessed | tf_op | source)
XLA Modules:
  0.0 1089.3 jit_solution(14809019965645088515)
XLA Ops:
  21.8 66.9 %all-gather.1 = bf16[32,18,32]{2,1,0:T(8,128)(2,1)S(1)} all-gather(bf16[1,18,32]{2,1,0:T(8,128)(2,1)S(1)} %bitcast.644), channel_id=2, replica_groups=mesh['page'=8,'seq'=4] {'page','seq'}, dimensions={0}, use_global_device_ids=true | all-gather | bytes 38016 | tf_op jit(solution)/shard_map/all_gather | solution.py:491
  121.8 11.5 %collective-permute-done.2 = bf16[2,32,384]{2,1,0:T(8,128)(2,1)S(1)} collective-permute-done((bf16[2,32,384]{2,1,0:T(8,128)(2,1)S(1)}, bf16[2,32,384]{2,1,0:T(8,128)(2,1)S(1)}, u32[]{:S(2)}, u32[]{:S(2)}) %collective-permute-start.2) | collective-permute-done | bytes 49184 | tf_op jit(solution)/shard_map/ppermute | solution.py:330
  133.3 7.3 collective-permute-start.3
  154.3 6.3 collective-permute-done.50
  165.9 27.0 %collective-permute-done.28 = bf16[2,32,1536]{2,1,0:T(8,128)(2,1)S(1)} collective-permute-done((bf16[2,32,1536]{2,1,0:T(8,128)(2,1)S(1)}, bf16[2,32,1536]{2,1,0:T(8,128)(2,1)S(1)}, u32[]{:S(2)}, u32[]{:S(2)}) %collective-permute-start.28) | collective-permute-done | bytes 196640 | tf_op jit(solution)/shard_map/ppermute | solution.py:330
  193.6 8.4 collective-permute-done.29
  215.9 10.1 collective-permute-done.5
  237.2 8.8 collective-permute-done.43
  264.2 20.9 %collective-permute-done.11 = bf16[512,1024]{1,0:T(8,128)(2,1)S(1)} collective-permute-done((bf16[512,1024]{1,0:T(8,128)(2,1)S(1)}, bf16[512,1024]{1,0:T(8,128)(2,1)S(1)}, u32[]{:S(2)}, u32[]{:S(2)}) %collective-permute-start.11) | collective-permute-done | bytes 1048608 | tf_op jit(solution)/shard_map/ppermute | solution.py:330
  290.0 21.6 %collective-permute-done.13 = bf16[512,1024]{1,0:T(8,128)(2,1)S(1)} collective-permute-done((bf16[512,1024]{1,0:T(8,128)(2,1)S(1)}, bf16[512,1024]{1,0:T(8,128)(2,1)S(1)}, u32[]{:S(2)}, u32[]{:S(2)}) %collective-permute-start.13) | collective-permute-done | bytes 1048608 | tf_op jit(solution)/shard_map/ppermute | solution.py:330
  326.6 22.4 %shard_map.237 = (bf16[2,2048,128]{2,1,0:T(8,128)(2,1)S(1)}, f32[2,2,1,2048]{3,2,1,0:T(1,128)S(1)}) custom-call(bf16[2,2048,384]{2,1,0:T(8,128)(2,1)S(1)} %bitcast.533, bf16[2,2048,384]{2,1,0:T(8,128)(2,1)S(1)} %bitcast.534), custom_call_target="tpu_custom_call" | custom-call | flops 4294967296 | bytes 12582912 | tf_op jit(solution)/shard_map/pallas_call | solution.py:77
  365.0 9.2 collective-permute-done.16
  388.7 8.9 collective-permute-done.46
  408.0 9.6 collective-permute-done.33
  463.9 10.1 multiply_convert_fusion
  477.3 10.4 convert_reduce_fusion
  491.6 6.4 convolution_convert_fusion.2
  502.7 7.7 convolution_convert_fusion.1
  561.0 11.9 %collective-permute-done.107 = bf16[4,128,1024]{2,1,0:T(8,128)(2,1)} collective-permute-done((bf16[4,128,1024]{2,1,0:T(8,128)(2,1)}, bf16[4,128,1024]{2,1,0:T(8,128)(2,1)}, u32[]{:S(2)}, u32[]{:S(2)}) %collective-permute-start.107) | collective-permute-done | bytes 1048608 | tf_op jit(solution)/shard_map/ppermute | solution.py:333
  588.9 16.9 %collective-permute-done.109 = bf16[128,1024]{1,0:T(8,128)(2,1)S(1)} collective-permute-done((bf16[128,1024]{1,0:T(8,128)(2,1)S(1)}, bf16[128,1024]{1,0:T(8,128)(2,1)S(1)}, u32[]{:S(2)}, u32[]{:S(2)}) %collective-permute-start.109) | collective-permute-done | bytes 262176 | tf_op jit(solution)/shard_map/ppermute | solution.py:330
  611.1 8.9 shard_map.241
  625.1 8.7 shard_map.240
  669.7 11.7 %collective-permute-done.91 = bf16[2,4,32,1536]{3,2,1,0:T(8,128)(2,1)S(1)} collective-permute-done((bf16[2,4,32,1536]{3,2,1,0:T(8,128)(2,1)S(1)}, bf16[2,4,32,1536]{3,2,1,0:T(8,128)(2,1)S(1)}, u32[]{:S(2)}, u32[]{:S(2)}) %collective-permute-start.91) | collective-permute-done | bytes 786464 | tf_op jit(solution)/shard_map/ppermute | solution.py:333
  694.8 12.1 %collective-permute-done.93 = bf16[2,32,1536]{2,1,0:T(8,128)(2,1)S(1)} collective-permute-done((bf16[2,32,1536]{2,1,0:T(8,128)(2,1)S(1)}, bf16[2,32,1536]{2,1,0:T(8,128)(2,1)S(1)}, u32[]{:S(2)}, u32[]{:S(2)}) %collective-permute-start.93) | collective-permute-done | bytes 196640 | tf_op jit(solution)/shard_map/ppermute | solution.py:330
  706.9 8.2 collective-permute-start.70
  754.6 8.4 collective-permute-done.63
  763.2 33.2 %shard_map.242 = bf16[2,2048,384]{2,1,0:T(8,128)(2,1)S(1)} custom-call(bf16[2,2048,384]{2,1,0:T(8,128)(2,1)} %bitcast.535, bf16[2,2048,384]{2,1,0:T(8,128)(2,1)} %bitcast.536, bf16[2,2048,128]{2,1,0:T(8,128)(2,1)S(1)} %bitcast.538, bf16[2,2048,128]{2,1,0:T(8,128)(2,1)S(1)} %copy-done.2, f32[2,2,1,2048]{3,2,1,0:T(1,128)S(1)} %get-tuple-element.32.lse_ref), custom_call_target="tpu_custom_call" | custom-call | flops 10737418240 | bytes 18874368 | tf_op jit(solution)/shard_map/pallas_call | solution.py:154
  798.9 7.0 convolution_convert_fusion.11
  815.2 11.9 %collective-permute-done.76 = bf16[2,128,384]{2,1,0:T(8,128)(2,1)S(1)} collective-permute-done((bf16[2,128,384]{2,1,0:T(8,128)(2,1)S(1)}, bf16[2,128,384]{2,1,0:T(8,128)(2,1)S(1)}, u32[]{:S(2)}, u32[]{:S(2)}) %collective-permute-start.76) | collective-permute-done | bytes 196640 | tf_op jit(solution)/shard_map/ppermute | solution.py:333
  866.3 15.9 %collective-permute-done.68 = bf16[512,1024]{1,0:T(8,128)(2,1)} collective-permute-done((bf16[512,1024]{1,0:T(8,128)(2,1)}, bf16[512,1024]{1,0:T(8,128)(2,1)}, u32[]{:S(2)}, u32[]{:S(2)}) %collective-permute-start.68) | collective-permute-done | bytes 1048608 | tf_op jit(solution)/shard_map/ppermute | solution.py:330
  882.2 67.6 %collective-permute-done.67 = bf16[512,1024]{1,0:T(8,128)(2,1)} collective-permute-done((bf16[512,1024]{1,0:T(8,128)(2,1)}, bf16[512,1024]{1,0:T(8,128)(2,1)}, u32[]{:S(2)}, u32[]{:S(2)}) %collective-permute-start.67) | collective-permute-done | bytes 1048608 | tf_op jit(solution)/shard_map/ppermute | solution.py:330
  963.2 114.2 %all-reduce.4.cloned.1.call-done = f32[32,544]{1,0:T(8,128)} async-done(((f32[32,544]{1,0:T(8,128)}), f32[32,544]{1,0:T(8,128)}) %all-reduce.4.cloned.1.call-update) | async-done | bytes 69648
  (758 shorter events, 460.3 us)
Async XLA Ops:
  7.2 1070.1 %all-reduce.4.cloned.1.call-start = ((), (), s32[]{:S(2)}) async-start(), calls=%async_computation | async-start | bytes 163840
  10.3 97.5 %collective-permute-start.18 = (bf16[32,2048]{1,0:T(8,128)(2,1)}, bf16[32,2048]{1,0:T(8,128)(2,1)}, u32[]{:S(2)}, u32[]{:S(2)}) collective-permute-start(bf16[32,2048]{1,0:T(8,128)(2,1)} %constant_dynamic-update-slice_fusion.7), channel_id=1, source_target_pairs={{0,1},{1,2},{2,3},{3,0},{4,5},{5,6},{6,7},{7,4},{8,9},{9,10},{10,1... | collective-permute-start | bytes 393224 | tf_op jit(solution)/shard_map/ppermute | solution.py:330
  13.3 99.0 %collective-permute-start.19 = (bf16[32,2048]{1,0:T(8,128)(2,1)}, bf16[32,2048]{1,0:T(8,128)(2,1)}, u32[]{:S(2)}, u32[]{:S(2)}) collective-permute-start(bf16[32,2048]{1,0:T(8,128)(2,1)} %constant_dynamic-update-slice_fusion.7), channel_id=1, source_target_pairs={{0,2},{1,3},{2,0},{3,1},{4,6},{5,7},{6,4},{7,5},{8,10},{9,11},{10,... | collective-permute-start | bytes 393224 | tf_op jit(solution)/shard_map/ppermute | solution.py:330
  15.9 98.6 %collective-permute-start.20 = (bf16[32,2048]{1,0:T(8,128)(2,1)}, bf16[32,2048]{1,0:T(8,128)(2,1)}, u32[]{:S(2)}, u32[]{:S(2)}) collective-permute-start(bf16[32,2048]{1,0:T(8,128)(2,1)} %constant_dynamic-update-slice_fusion.7), channel_id=1, source_target_pairs={{0,3},{1,0},{2,1},{3,2},{4,7},{5,4},{6,5},{7,6},{8,11},{9,8},{10,9... | collective-permute-start | bytes 393224 | tf_op jit(solution)/shard_map/ppermute | solution.py:330
  19.3 88.3 %collective-permute-start.1 = (bf16[4,32,384]{2,1,0:T(8,128)(2,1)}, bf16[4,32,384]{2,1,0:T(8,128)(2,1)S(1)}, u32[]{:S(2)}, u32[]{:S(2)}) collective-permute-start(bf16[4,32,384]{2,1,0:T(8,128)(2,1)} %get-tuple-element.165), channel_id=1, source_target_pairs={{0,4},{1,5},{2,6},{3,7},{4,0},{5,1},{6,2},{7,3},{8,12},{9,13},{10,... | collective-permute-start | bytes 294920 | tf_op jit(solution)/shard_map/ppermute | solution.py:327
  20.3 85.4 %collective-permute-start.27 = (bf16[32,1536]{1,0:T(8,128)(2,1)}, bf16[32,1536]{1,0:T(8,128)(2,1)S(1)}, u32[]{:S(2)}, u32[]{:S(2)}) collective-permute-start(bf16[32,1536]{1,0:T(8,128)(2,1)} %get-tuple-element.158), channel_id=1, source_target_pairs={{0,4},{1,5},{2,6},{3,7},{4,0},{5,1},{6,2},{7,3},{8,12},{9,13},{10,... | collective-permute-start | bytes 294920 | tf_op jit(solution)/shard_map/ppermute | solution.py:327
  105.7 107.9 %collective-permute-start.35 = (bf16[160,1024]{1,0:T(8,128)(2,1)}, bf16[160,1024]{1,0:T(8,128)(2,1)S(1)}, u32[]{:S(2)}, u32[]{:S(2)}) collective-permute-start(bf16[160,1024]{1,0:T(8,128)(2,1)} %bitcast.635), channel_id=1, source_target_pairs={{0,1},{1,2},{2,3},{3,0},{4,5},{5,6},{6,7},{7,4},{8,9},{9,10},{10,1... | collective-permute-start | bytes 983048 | tf_op jit(solution)/shard_map/ppermute | solution.py:330
  107.6 106.0 %collective-permute-start.36 = (bf16[160,1024]{1,0:T(8,128)(2,1)}, bf16[160,1024]{1,0:T(8,128)(2,1)S(1)}, u32[]{:S(2)}, u32[]{:S(2)}) collective-permute-start(bf16[160,1024]{1,0:T(8,128)(2,1)} %bitcast.636), channel_id=1, source_target_pairs={{0,2},{1,3},{2,0},{3,1},{4,6},{5,7},{6,4},{7,5},{8,10},{9,11},{10,... | collective-permute-start | bytes 983048 | tf_op jit(solution)/shard_map/ppermute | solution.py:330
  107.8 106.0 %collective-permute-start.37 = (bf16[160,1024]{1,0:T(8,128)(2,1)S(1)}, bf16[160,1024]{1,0:T(8,128)(2,1)S(1)}, u32[]{:S(2)}, u32[]{:S(2)}) collective-permute-start(bf16[160,1024]{1,0:T(8,128)(2,1)S(1)} %bitcast.637), channel_id=1, source_target_pairs={{0,3},{1,0},{2,1},{3,2},{4,7},{5,4},{6,5},{7,6},{8,11},{9,8},{10,9... | collective-permute-start | bytes 983048 | tf_op jit(solution)/shard_map/ppermute | solution.py:330
  160.6 94.5 %collective-permute-start.9 = (bf16[512,1024]{1,0:T(8,128)(2,1)S(1)}, bf16[512,1024]{1,0:T(8,128)(2,1)S(1)}, u32[]{:S(2)}, u32[]{:S(2)}) collective-permute-start(bf16[512,1024]{1,0:T(8,128)(2,1)S(1)} %bitcast.540), channel_id=1, source_target_pairs={{0,1},{1,2},{2,3},{3,0},{4,5},{5,6},{6,7},{7,4},{8,9},{9,10},{10,1... | collective-permute-start | bytes 3145736 | tf_op jit(solution)/shard_map/ppermute | solution.py:330
  208.6 45.9 %collective-permute-start.21 = (bf16[4,32,2048]{2,1,0:T(8,128)(2,1)S(1)}, bf16[4,32,2048]{2,1,0:T(8,128)(2,1)S(1)}, u32[]{:S(2)}, u32[]{:S(2)}) collective-permute-start(bf16[4,32,2048]{2,1,0:T(8,128)(2,1)S(1)} %copy-done.59), channel_id=1, source_target_pairs={{0,8},{1,9},{2,10},{3,11},{4,12},{5,13},{6,14},{7,15},{8,24},{9,25... | collective-permute-start | bytes 1572872 | tf_op jit(solution)/shard_map/ppermute | solution.py:333
  213.6 39.4 %collective-permute-start.22 = (bf16[4,32,2048]{2,1,0:T(8,128)(2,1)S(1)}, bf16[4,32,2048]{2,1,0:T(8,128)(2,1)S(1)}, u32[]{:S(2)}, u32[]{:S(2)}) collective-permute-start(bf16[4,32,2048]{2,1,0:T(8,128)(2,1)S(1)} %copy-done.59), channel_id=1, source_target_pairs={{0,16},{1,17},{2,18},{3,19},{4,20},{5,21},{6,22},{7,23},{8,0},{9,1... | collective-permute-start | bytes 1572872 | tf_op jit(solution)/shard_map/ppermute | solution.py:333
  252.9 224.4 %collective-permute-start.57 = (bf16[512,1024]{1,0:T(8,128)(2,1)}, bf16[512,1024]{1,0:T(8,128)(2,1)}, u32[]{:S(2)}, u32[]{:S(2)}) collective-permute-start(bf16[512,1024]{1,0:T(8,128)(2,1)} %bitcast.112), channel_id=1, source_target_pairs={{0,4},{1,5},{2,6},{3,7},{4,0},{5,1},{6,2},{7,3},{8,12},{9,13},{10,... | collective-permute-start | bytes 3145736 | tf_op jit(solution)/shard_map/ppermute | solution.py:327
  261.8 121.2 %collective-permute-start.52 = (bf16[4,128,1024]{2,1,0:T(8,128)(2,1)S(1)}, bf16[4,128,1024]{2,1,0:T(8,128)(2,1)}, u32[]{:S(2)}, u32[]{:S(2)}) collective-permute-start(bf16[4,128,1024]{2,1,0:T(8,128)(2,1)S(1)} %bitcast_dynamic-update-slice_fusion.20), channel_id=1, source_target_pairs={{0,8},{1,9},{2,10},{3,11},{4,12},{5,13},{6,14},{7,15},{8,24},{9,25... | collective-permute-start | bytes 3145736 | tf_op jit(solution)/shard_map/ppermute | solution.py:333
  288.2 92.9 %collective-permute-start.53 = (bf16[4,128,1024]{2,1,0:T(8,128)(2,1)S(1)}, bf16[4,128,1024]{2,1,0:T(8,128)(2,1)}, u32[]{:S(2)}, u32[]{:S(2)}) collective-permute-start(bf16[4,128,1024]{2,1,0:T(8,128)(2,1)S(1)} %bitcast_dynamic-update-slice_fusion.20), channel_id=1, source_target_pairs={{0,16},{1,17},{2,18},{3,19},{4,20},{5,21},{6,22},{7,23},{8,0},{9,1... | collective-permute-start | bytes 3145736 | tf_op jit(solution)/shard_map/ppermute | solution.py:333
  312.3 38.6 %collective-permute-start.31 = (bf16[2,4,32,1536]{3,2,1,0:T(8,128)(2,1)}, bf16[2,4,32,1536]{3,2,1,0:T(8,128)(2,1)}, u32[]{:S(2)}, u32[]{:S(2)}) collective-permute-start(bf16[2,4,32,1536]{3,2,1,0:T(8,128)(2,1)} %bitcast_dynamic-update-slice_fusion.31), channel_id=1, source_target_pairs={{0,8},{1,9},{2,10},{3,11},{4,12},{5,13},{6,14},{7,15},{8,24},{9,25... | collective-permute-start | bytes 2359304 | tf_op jit(solution)/shard_map/ppermute | solution.py:333
  314.3 40.5 %collective-permute-start.32 = (bf16[2,4,32,1536]{3,2,1,0:T(8,128)(2,1)}, bf16[2,4,32,1536]{3,2,1,0:T(8,128)(2,1)}, u32[]{:S(2)}, u32[]{:S(2)}) collective-permute-start(bf16[2,4,32,1536]{3,2,1,0:T(8,128)(2,1)} %bitcast_dynamic-update-slice_fusion.31), channel_id=1, source_target_pairs={{0,16},{1,17},{2,18},{3,19},{4,20},{5,21},{6,22},{7,23},{8,0},{9,1... | collective-permute-start | bytes 2359304 | tf_op jit(solution)/shard_map/ppermute | solution.py:333
  383.0 51.8 %collective-permute-start.45 = (bf16[2,4,32,2048]{3,2,1,0:T(8,128)(2,1)}, bf16[2,4,32,2048]{3,2,1,0:T(8,128)(2,1)}, u32[]{:S(2)}, u32[]{:S(2)}) collective-permute-start(bf16[2,4,32,2048]{3,2,1,0:T(8,128)(2,1)} %bitcast_dynamic-update-slice_fusion.24), channel_id=1, source_target_pairs={{0,8},{1,9},{2,10},{3,11},{4,12},{5,13},{6,14},{7,15},{8,24},{9,25... | collective-permute-start | bytes 3145736 | tf_op jit(solution)/shard_map/ppermute | solution.py:333
  477.3 66.7 %collective-permute-start.56 = (bf16[512,1024]{1,0:T(8,128)(2,1)}, bf16[512,1024]{1,0:T(8,128)(2,1)}, u32[]{:S(2)}, u32[]{:S(2)}) collective-permute-start(bf16[512,1024]{1,0:T(8,128)(2,1)} %fusion.81), channel_id=1, source_target_pairs={{0,4},{1,5},{2,6},{3,7},{4,0},{5,1},{6,2},{7,3},{8,12},{9,13},{10,... | collective-permute-start | bytes 3145736 | tf_op jit(solution)/shard_map/ppermute | solution.py:327
  491.1 43.2 %collective-permute-start.58 = (bf16[512,1024]{1,0:T(8,128)(2,1)}, bf16[512,1024]{1,0:T(8,128)(2,1)}, u32[]{:S(2)}, u32[]{:S(2)}) collective-permute-start(bf16[512,1024]{1,0:T(8,128)(2,1)} %fusion.84), channel_id=1, source_target_pairs={{0,4},{1,5},{2,6},{3,7},{4,0},{5,1},{6,2},{7,3},{8,12},{9,13},{10,... | collective-permute-start | bytes 3145736 | tf_op jit(solution)/shard_map/ppermute | solution.py:327
  532.6 40.4 %collective-permute-start.107 = (bf16[4,128,1024]{2,1,0:T(8,128)(2,1)}, bf16[4,128,1024]{2,1,0:T(8,128)(2,1)}, u32[]{:S(2)}, u32[]{:S(2)}) collective-permute-start(bf16[4,128,1024]{2,1,0:T(8,128)(2,1)} %pad_maximum_fusion.27), channel_id=1, source_target_pairs={{0,16},{1,17},{2,18},{3,19},{4,20},{5,21},{6,22},{7,23},{8,0},{9,1... | collective-permute-start | bytes 3145736 | tf_op jit(solution)/shard_map/ppermute | solution.py:333
  534.3 41.6 %collective-permute-start.105 = (bf16[4,128,1024]{2,1,0:T(8,128)(2,1)}, bf16[4,128,1024]{2,1,0:T(8,128)(2,1)}, u32[]{:S(2)}, u32[]{:S(2)}) collective-permute-start(bf16[4,128,1024]{2,1,0:T(8,128)(2,1)} %pad_maximum_fusion.26), channel_id=1, source_target_pairs={{0,8},{1,9},{2,10},{3,11},{4,12},{5,13},{6,14},{7,15},{8,24},{9,25... | collective-permute-start | bytes 3145736 | tf_op jit(solution)/shard_map/ppermute | solution.py:333
  544.0 62.7 %collective-permute-start.59 = (bf16[512,1024]{1,0:T(8,128)(2,1)}, bf16[512,1024]{1,0:T(8,128)(2,1)}, u32[]{:S(2)}, u32[]{:S(2)}) collective-permute-start(bf16[512,1024]{1,0:T(8,128)(2,1)} %convert_element_type.670), channel_id=1, source_target_pairs={{0,4},{1,5},{2,6},{3,7},{4,0},{5,1},{6,2},{7,3},{8,12},{9,13},{10,... | collective-permute-start | bytes 3145736 | tf_op jit(solution)/shard_map/ppermute | solution.py:327
  585.7 129.6 %collective-permute-start.103 = (f32[32,2048]{1,0:T(8,128)}, f32[32,2048]{1,0:T(8,128)}, u32[]{:S(2)}, u32[]{:S(2)}) collective-permute-start(f32[32,2048]{1,0:T(8,128)} %get-tuple-element.140), channel_id=1, source_target_pairs={{0,4},{1,5},{2,6},{3,7},{4,0},{5,1},{6,2},{7,3},{8,12},{9,13},{10,... | collective-permute-start | bytes 786440 | tf_op jit(solution)/shard_map/ppermute | solution.py:327
  621.7 43.5 %collective-permute-start.60 = (bf16[512,1024]{1,0:T(8,128)(2,1)}, bf16[512,1024]{1,0:T(8,128)(2,1)}, u32[]{:S(2)}, u32[]{:S(2)}) collective-permute-start(bf16[512,1024]{1,0:T(8,128)(2,1)} %convolution_convert_fusion.8), channel_id=1, source_target_pairs={{0,4},{1,5},{2,6},{3,7},{4,0},{5,1},{6,2},{7,3},{8,12},{9,13},{10,... | collective-permute-start | bytes 3145736 | tf_op jit(solution)/shard_map/ppermute | solution.py:327
  624.6 61.7 %collective-permute-start.69 = (bf16[640,1024]{1,0:T(8,128)(2,1)}, bf16[640,1024]{1,0:T(8,128)(2,1)}, u32[]{:S(2)}, u32[]{:S(2)}) collective-permute-start(bf16[640,1024]{1,0:T(8,128)(2,1)} %fusion.73), channel_id=1, source_target_pairs={{0,4},{1,5},{2,6},{3,7},{4,0},{5,1},{6,2},{7,3},{8,12},{9,13},{10,... | collective-permute-start | bytes 3932168 | tf_op jit(solution)/shard_map/ppermute | solution.py:327
  669.7 62.5 %collective-permute-start.61 = (bf16[512,1024]{1,0:T(8,128)(2,1)}, bf16[512,1024]{1,0:T(8,128)(2,1)}, u32[]{:S(2)}, u32[]{:S(2)}) collective-permute-start(bf16[512,1024]{1,0:T(8,128)(2,1)} %convert_element_type.674), channel_id=1, source_target_pairs={{0,4},{1,5},{2,6},{3,7},{4,0},{5,1},{6,2},{7,3},{8,12},{9,13},{10,... | collective-permute-start | bytes 3145736 | tf_op jit(solution)/shard_map/ppermute | solution.py:327
  750.8 57.3 %collective-permute-start.81 = (bf16[2,32,2048]{2,1,0:T(8,128)(2,1)S(1)}, bf16[2,32,2048]{2,1,0:T(8,128)(2,1)S(1)}, u32[]{:S(2)}, u32[]{:S(2)}) collective-permute-start(bf16[2,32,2048]{2,1,0:T(8,128)(2,1)S(1)} %get-tuple-element.102), channel_id=1, source_target_pairs={{0,8},{1,9},{2,10},{3,11},{4,12},{5,13},{6,14},{7,15},{8,24},{9,25... | collective-permute-start | bytes 786440 | tf_op jit(solution)/shard_map/ppermute | solution.py:333
  751.5 56.6 %collective-permute-start.83 = (bf16[2,32,2048]{2,1,0:T(8,128)(2,1)S(1)}, bf16[2,32,2048]{2,1,0:T(8,128)(2,1)S(1)}, u32[]{:S(2)}, u32[]{:S(2)}) collective-permute-start(bf16[2,32,2048]{2,1,0:T(8,128)(2,1)S(1)} %get-tuple-element.104), channel_id=1, source_target_pairs={{0,16},{1,17},{2,18},{3,19},{4,20},{5,21},{6,22},{7,23},{8,0},{9,1... | collective-permute-start | bytes 786440 | tf_op jit(solution)/shard_map/ppermute | solution.py:333
  798.8 48.8 %collective-permute-start.65 = (bf16[2048,1024]{1,0:T(8,128)(2,1)S(1)}, bf16[2048,1024]{1,0:T(8,128)(2,1)S(1)}, u32[]{:S(2)}, u32[]{:S(2)}) collective-permute-start(bf16[2048,1024]{1,0:T(8,128)(2,1)S(1)} %convolution_convert_fusion), channel_id=1, source_target_pairs={{0,4},{1,5},{2,6},{3,7},{4,0},{5,1},{6,2},{7,3},{8,12},{9,13},{10,... | collective-permute-start | bytes 12582920 | tf_op jit(solution)/shard_map/ppermute | solution.py:327
  858.3 91.5 %collective-permute-start.67 = (bf16[512,1024]{1,0:T(8,128)(2,1)}, bf16[512,1024]{1,0:T(8,128)(2,1)}, u32[]{:S(2)}, u32[]{:S(2)}) collective-permute-start(bf16[512,1024]{1,0:T(8,128)(2,1)} %get-tuple-element.91), channel_id=1, source_target_pairs={{0,2},{1,3},{2,0},{3,1},{4,6},{5,7},{6,4},{7,5},{8,10},{9,11},{10,... | collective-permute-start | bytes 3145736 | tf_op jit(solution)/shard_map/ppermute | solution.py:330
  859.5 90.4 %collective-permute-start.66 = (bf16[512,1024]{1,0:T(8,128)(2,1)}, bf16[512,1024]{1,0:T(8,128)(2,1)}, u32[]{:S(2)}, u32[]{:S(2)}) collective-permute-start(bf16[512,1024]{1,0:T(8,128)(2,1)} %get-tuple-element.89), channel_id=1, source_target_pairs={{0,1},{1,2},{2,3},{3,0},{4,5},{5,6},{6,7},{7,4},{8,9},{9,10},{10,1... | collective-permute-start | bytes 3145736 | tf_op jit(solution)/shard_map/ppermute | solution.py:330
  (195 other events, 3330.7 us)
Sparse Core Ops, SparseCore 0:
  959.7 117.6 all-reduce.3

commit v2 on v1

--- a/solution.py
+++ b/solution.py
@@ -28,7 +28,54 @@
     return lax.dot_general(a, b, dims, preferred_element_type=F32)
 
 
-def self_fwd_kernel(q_ref, kv_ref, o_ref, lse_ref, *, rows, width):
+def project_kernel(spot_ref, x_ref, gain_ref, shift_ref, w_ref, b_ref, h_in, qkv_in, h_ref, qkv_ref):
+    del spot_ref, h_in, qkv_in
+    x = x_ref[...].astype(F32)
+    centered = x - jnp.mean(x, axis=-1, keepdims=True)
+    scale = lax.rsqrt(jnp.mean(centered * centered, axis=-1, keepdims=True) + EPSILON)
+    h = (centered * scale * gain_ref[...] + shift_ref[...]).astype(BF16)
+    h_ref[0, 0] = h
+    qkv_ref[0, 0] = (dot(h, w_ref[...]) + b_ref[...]).astype(BF16)
+
+
+def project(spot, x, gain, shift, w_qkv, b_qkv, h_all, qkv):
+    rows, width = x.shape
+    wide = w_qkv.shape[1]
+    block = min(256, rows)
+    whole = lambda shape: pl.BlockSpec(shape, lambda i, n: (0, 0))
+    return pl.pallas_call(
+        project_kernel,
+        grid_spec=pltpu.PrefetchScalarGridSpec(
+            num_scalar_prefetch=1,
+            grid=(rows // block,),
+            in_specs=[
+                pl.BlockSpec((block, width), lambda i, n: (i, 0)),
+                whole((1, width)),
+                whole((1, width)),
+                whole((width, wide)),
+                whole((1, wide)),
+                pl.BlockSpec(memory_space=pl.ANY),
+                pl.BlockSpec(memory_space=pl.ANY),
+            ],
+            out_specs=[
+                pl.BlockSpec((1, 1, block, width), lambda i, n: (n[0], n[1], i, 0)),
+                pl.BlockSpec((1, 1, block, wide), lambda i, n: (n[0], n[1], i, 0)),
+            ],
+        ),
+        out_shape=[
+            jax.ShapeDtypeStruct(h_all.shape, BF16),
+            jax.ShapeDtypeStruct(qkv.shape, BF16),
+        ],
+        input_output_aliases={6: 0, 7: 1},
+        compiler_params=pltpu.CompilerParams(vmem_limit_bytes=32 * 1024 * 1024),
+        cost_estimate=pl.CostEstimate(
+            flops=2 * rows * width * wide, bytes_accessed=4 * rows * width, transcendentals=0
+        ),
+    )(spot, x, gain[None], shift[None], w_qkv, b_qkv[None], h_all, qkv)
+
+
+def self_fwd_kernel(order_ref, q_ref, kv_ref, o_ref, lse_ref, *, rows, width):
+    del order_ref
     i = pl.program_id(1)
     heads = width // HEAD_DIM
     queries = [q_ref[0, :, h * HEAD_DIM : (h + 1) * HEAD_DIM] for h in range(heads)]
@@ -68,32 +115,32 @@
     o_ref[0] = jnp.concatenate(outs, axis=0).T.astype(BF16)
 
 
-def self_fwd(qkv, rows):
-    pages, length, three = qkv.shape
+def self_fwd(order, qkv, rows, page):
+    length, three = qkv.shape[1:]
     width = three // 3
     heads = width // HEAD_DIM
-    blocks = length // rows
-    cost = pages * heads * length * length * HEAD_DIM * 2
+    cost = heads * length * length * HEAD_DIM * 2
     return pl.pallas_call(
         functools.partial(self_fwd_kernel, rows=rows, width=width),
-        grid=(pages, blocks),
+        grid=(1, length // rows),
         in_specs=[
-            pl.BlockSpec((1, rows, three), lambda p, i: (p, i, 0)),
-            pl.BlockSpec((1, length, three), lambda p, i: (p, 0, 0)),
+            pl.BlockSpec(memory_space=pltpu.SMEM),
+            pl.BlockSpec((1, rows, three), lambda p, i: (page, i, 0)),
+            pl.BlockSpec((1, length, three), lambda p, i: (page, 0, 0)),
         ],
         out_specs=[
-            pl.BlockSpec((1, rows, width), lambda p, i: (p, i, 0)),
-            pl.BlockSpec((1, heads, 1, rows), lambda p, i: (p, 0, 0, i)),
+            pl.BlockSpec((1, rows, width), lambda p, i: (0, i, 0)),
+            pl.BlockSpec((1, heads, 1, rows), lambda p, i: (0, 0, 0, i)),
         ],
         out_shape=[
-            jax.ShapeDtypeStruct((pages, length, width), BF16),
-            jax.ShapeDtypeStruct((pages, heads, 1, length), F32),
+            jax.ShapeDtypeStruct((1, length, width), BF16),
+            jax.ShapeDtypeStruct((1, heads, 1, length), F32),
         ],
         compiler_params=pltpu.CompilerParams(vmem_limit_bytes=48 * 1024 * 1024),
         cost_estimate=pl.CostEstimate(
-            flops=2 * cost, bytes_accessed=8 * qkv.size, transcendentals=cost // 256
+            flops=2 * cost, bytes_accessed=4 * qkv.size, transcendentals=cost // 256
         ),
-    )(qkv, qkv)
+    )(order, qkv, qkv)
 
 
 def self_bwd_kernel(q_ref, kv_ref, do_ref, o_ref, lse_ref, out_ref, dk_acc, dv_acc, *, rows, width):
@@ -146,27 +193,27 @@
         out_ref[0, :, 2 * width :] = dv_acc[...].astype(BF16)
 
 
-def self_bwd(qkv, d_out, out, lse, rows):
-    pages, length, three = qkv.shape
+def self_bwd(qkv, d_out, out, lse, rows, page):
+    length, three = qkv.shape[1:]
     width = three // 3
     heads = width // HEAD_DIM
-    cost = pages * heads * length * length * HEAD_DIM * 5
+    cost = heads * length * length * HEAD_DIM * 5
     return pl.pallas_call(
         functools.partial(self_bwd_kernel, rows=rows, width=width),
-        grid=(pages, length // rows),
+        grid=(1, length // rows),
         in_specs=[
-            pl.BlockSpec((1, rows, three), lambda p, i: (p, i, 0)),
-            pl.BlockSpec((1, length, three), lambda p, i: (p, 0, 0)),
-            pl.BlockSpec((1, rows, width), lambda p, i: (p, i, 0)),
-            pl.BlockSpec((1, rows, width), lambda p, i: (p, i, 0)),
-            pl.BlockSpec((1, heads, 1, rows), lambda p, i: (p, 0, 0, i)),
+            pl.BlockSpec((1, rows, three), lambda p, i: (page, i, 0)),
+            pl.BlockSpec((1, length, three), lambda p, i: (page, 0, 0)),
+            pl.BlockSpec((1, rows, width), lambda p, i: (page, i, 0)),
+            pl.BlockSpec((1, rows, width), lambda p, i: (0, i, 0)),
+            pl.BlockSpec((1, heads, 1, rows), lambda p, i: (0, 0, 0, i)),
         ],
-        out_specs=pl.BlockSpec((1, length, three), lambda p, i: (p, 0, 0)),
-        out_shape=jax.ShapeDtypeStruct((pages, length, three), BF16),
+        out_specs=pl.BlockSpec((1, length, three), lambda p, i: (0, 0, 0)),
+        out_shape=jax.ShapeDtypeStruct((1, length, three), BF16),
         scratch_shapes=[pltpu.VMEM((length, width), F32), pltpu.VMEM((length, width), F32)],
         compiler_params=pltpu.CompilerParams(vmem_limit_bytes=48 * 1024 * 1024),
         cost_estimate=pl.CostEstimate(
-            flops=2 * cost, bytes_accessed=12 * qkv.size, transcendentals=cost // 640
+            flops=2 * cost, bytes_accessed=6 * qkv.size, transcendentals=cost // 640
         ),
     )(qkv, qkv, d_out, out, lse)
 
@@ -310,6 +357,11 @@
             for core in range(2)
             for z in range(self.seq)
         ]
+        self.planes = [
+            [index(chip, core, z) for chip in range(self.chips)]
+            for core in range(2)
+            for z in range(self.seq)
+        ]
         self.pair_map = [(index(h, c, z), index(h, 1 - c, z)) for h, c, z in everyone]
         self.line_map = [
             [(index(h, c, z), index(h, c, (z + s) % self.seq)) for h, c, z in everyone]
@@ -348,11 +400,28 @@
     return lax.dynamic_index_in_dim(buffer, index, axis, keepdims=False)
 
 
+def line_pieces(net, piece):
+    yield 0, piece
+    right, left = piece, piece
+    for t in range(1, net.seq // 2 + 1):
+        right = net.along(right, 1)
+        yield -t, right
+        if t <= (net.seq - 1) // 2:
+            left = net.along(left, -1)
+            yield t, left
+
+
 def line_gather(net, piece, axis):
-    shape = piece.shape[:axis] + (net.seq,) + piece.shape[axis:]
-    out = put(jnp.zeros(shape, piece.dtype), piece, net.z, axis)
+    out = jnp.zeros(piece.shape[:axis] + (net.seq,) + piece.shape[axis:], piece.dtype)
+    for by, got in line_pieces(net, piece):
+        out = put(out, got, net.z_at(by), axis)
+    return out
+
+
+def line_gather_held(net, piece, axis, *others):
+    out = put(jnp.zeros(piece.shape[:axis] + (net.seq,) + piece.shape[axis:], piece.dtype), piece, net.z, axis)
     for s in range(1, net.seq):
-        out = put(out, net.along(piece, s), net.z_at(-s), axis)
+        out = put(out, after(net.along(piece, s), *others), net.z_at(-s), axis)
     return out
 
 
@@ -394,10 +463,9 @@
 
 def line_scatter(net, parts, axis):
     low = parts.astype(BF16)
-    total = pick(parts, net.z, axis).astype(F32)
-    for s in range(1, net.seq):
-        total += net.along(pick(low, net.z_at(s), axis), s).astype(F32)
-    return total
+    sent = [pick(low, net.z_at(s), axis) for s in range(1, net.seq)]
+    got = [net.along(value, s + 1) for s, value in enumerate(sent)]
+    return pick(parts, net.z, axis).astype(F32) + sum(value.astype(F32) for value in got)
 
 
 def own_first(net, value):
@@ -408,28 +476,54 @@
     return jnp.where(net.core == 0, jnp.stack([own, other]), jnp.stack([other, own]))
 
 
-def gather_columns(net, shard):
-    own, other = own_first(net, jnp.moveaxis(shard, 1, 0))
-    piece = by_core(net, own, net.sibling(other))
-    full = ring_gather(net, line_gather(net, piece, 1))
-    return full.reshape(-1, full.shape[-1])
-
-
-def gather_rows(net, shard):
-    full = ring_gather(net, line_gather(net, shard, 0))
-    return full.reshape(-1, full.shape[-1])
+def plane_gather(net, piece):
+    return lax.all_gather(piece, AXES, axis=0, axis_index_groups=net.planes)
+
+
+def plane_scatter(net, parts):
+    flat = parts.reshape(-1, parts.shape[-1])
+    mine = lax.psum_scatter(
+        flat, AXES, scatter_dimension=0, axis_index_groups=net.planes, tiled=True
+    )
+    return mine.reshape(parts.shape[1:])
+
+
+def seq_scatter(parts):
+    flat = parts.reshape(-1, parts.shape[-1])
+    mine = lax.psum_scatter(flat, "seq", scatter_dimension=0, tiled=True)
+    return mine.reshape(parts.shape[1:]).astype(F32)
+
+
+def after(value, *others):
+    for other in others:
+        element = lax.optimization_barrier(other)[(0,) * other.ndim].astype(F32)
+        value = value + jnp.minimum(jnp.abs(element), 0.0).astype(value.dtype)
+    return value
 
 
 def scatter_columns(net, grad, rows):
     parts = grad.reshape(net.chips, 2, net.seq, rows, grad.shape[-1])
-    mine = line_scatter(net, ring_scatter(net, parts), 1)
+    mine = line_scatter(net, plane_scatter(net, parts), 1)
     own, other = own_first(net, mine)
     return jnp.moveaxis(by_core(net, own, net.sibling(other)), 0, 1)
 
 
 def scatter_rows(net, grad, rows):
     parts = grad.reshape(net.chips, net.seq, rows, grad.shape[-1])
-    return line_scatter(net, ring_scatter(net, parts), 0)
+    return line_scatter(net, plane_scatter(net, parts), 0)
+
+
+def line_two_way_scatter(net, parts):
+    total = pick(parts, net.z)
+    for way, far in ((1, net.seq // 2), (-1, (net.seq - 1) // 2)):
+        got = None
+        for by in range(far, 0, -1):
+            mine = pick(parts, net.z_at(way * by))
+            sent = (mine if got is None else mine + got).astype(BF16)
+            got = net.along(sent, way).astype(F32)
+        if got is not None:
+            total += got
+    return total
 
 
 def norm_parts(values):
@@ -484,23 +578,6 @@
     half = width // 2
     tok, mem, cot = tokens[0], memory[0], cotangent[0]
 
-    flag = jnp.broadcast_to(res_flag.astype(BF16)[:, None], (1, shard))
-    small = jnp.concatenate(
-        [ln_gain, ln_bias, proj_bias, flag, ff_bias.reshape(ff_shard // shard, shard)], axis=0
-    )
-    small = lax.all_gather(small, AXES, axis=0)
-    vectors = jnp.moveaxis(small[:, :13], 0, 1).reshape(13, width).astype(F32)
-    gain, shift, bias = vectors[0:3], vectors[3:6], vectors[6:13]
-    flags = small[:, 13, 0].reshape(pages, seq)[:, 0].astype(F32)
-    up_bias = small[:, 14:].reshape(chips, 2, seq * ff_shard)
-    up_bias = pick(up_bias, core, 1).reshape(hidden // 2).astype(F32)
-    page = lax.axis_index("page")
-
-    def limit_of(which):
-        return jnp.where(pick(flags, which) > 0.5, VALID_HI, VALID_LO).astype(jnp.int32).reshape(1)
-
-    limit_own, limit_other = limit_of(page), limit_of(page ^ 1)
-
     def halves(vector):
         return pick(vector.reshape(pages // 2, 2, width // pages), core, 1).reshape(half)
 
@@ -514,15 +591,45 @@
         split = weight.reshape(lead + (2, pages // 2, columns // pages))
         return jnp.moveaxis(split, -3, -2).reshape(lead + (columns,))
 
+    side = 128
+    small = jnp.concatenate(
+        [
+            ln_gain.T,
+            ln_bias.T,
+            proj_bias.T,
+            jnp.broadcast_to(res_flag.astype(BF16)[:, None], (shard, 1)),
+            ff_bias.reshape(shard, ff_shard // shard),
+        ],
+        axis=1,
+    )
+    small = jnp.pad(small, ((0, 0), (0, side - small.shape[1])))
     blocks = self_in.reshape(3, shard, seq, 2, lanes).transpose(3, 2, 1, 0, 4)
     blocks = blocks.reshape(2, seq, shard, 3 * lanes)
+    small = jnp.broadcast_to(small, (2, seq, shard, side))
+    blocks = jnp.concatenate([blocks, small], axis=3)
     own, other = own_first(net, blocks)
     blocks = by_core(net, own, net.sibling(other))
     piece = jnp.zeros_like(blocks)
     piece = put(piece, pick(blocks, z, 1), z, 1)
     for s in range(1, seq):
         piece = put(piece, net.along(pick(blocks, net.z_at(s), 1), s), net.z_at(-s), 1)
-    w_qkv = ring_gather(net, piece).reshape(width, 3 * lanes)
+    qkv_line = piece
+    w_wide = ring_gather(net, piece).reshape(width, 3 * lanes + side)
+    w_qkv = w_wide[:, : 3 * lanes]
+    small = w_wide[:, 3 * lanes :].astype(F32)
+    vectors = small[:, :13].T
+    gain, shift, bias = vectors[0:3], vectors[3:6], vectors[6:13]
+    flags = small[:, 13].reshape(pages, seq * shard)[:, 0]
+    up_bias = small[:, 14 : 14 + ff_shard // shard].reshape(chips, 2, seq * ff_shard)
+    up_bias = pick(up_bias, core, 1).reshape(hidden // 2)
+    page = lax.axis_index("page")
+
+    def limit_of(which):
+        return jnp.where(pick(flags, which) > 0.5, VALID_HI, VALID_LO).astype(jnp.int32).reshape(1)
+
+    limit_own, limit_other = limit_of(page), limit_of(page ^ 1)
+
+    limit_own, limit_other = limit_of(page), limit_of(page ^ 1)
     first = (2 * z + core) * lanes
     b_qkv = jnp.concatenate(
         [
@@ -532,56 +639,85 @@
         ]
     )
 
+    cross_halves = column_halves(cross_in).transpose(2, 1, 0, 3).reshape(2, shard, 3 * half)
+    column_parts = jnp.concatenate([cross_halves, column_halves(ff_in).transpose(1, 0, 2)], axis=2)
+    own, other = own_first(net, column_parts)
+    column_parts = by_core(net, own, net.sibling(other))
+    cross_parts, up_parts = column_parts[:, :, : 3 * half], column_parts[:, :, 3 * half :]
+    bundle = jnp.concatenate([cross_parts[0], cross_parts[1], self_out, cross_out], axis=1)
+    bundle_line = line_gather(net, after(bundle, qkv_line), 0)
+    bundle = plane_gather(net, bundle_line)
+
+    def rows_of(at, columns):
+        two = [bundle[..., c * 3 * half + at : c * 3 * half + at + columns] for c in range(2)]
+        return jnp.stack(two, axis=1).reshape(width, columns)
+
+    w_cross_q, w_cross_kv = rows_of(0, half), rows_of(half, width)
+    w_self_out = bundle[..., 6 * half : 6 * half + width].reshape(half, width)
+    w_cross_out = bundle[..., 6 * half + width :].reshape(half, width)
     h_all = jnp.zeros((2, seq, rows, width), BF16)
     qkv = jnp.zeros((2, seq, rows, 3 * lanes), BF16)
-    passing = tok
-    h_one = None
-    for t in range(seq):
+    right = left = passing = after(tok, qkv_line)
+    for t in range(seq // 2 + 1):
+        if t == 1:
+            own_qkv = qkv
+        if t == 2:
+            right = after(right, own_qkv)
+        ways = [(0, passing)]
         if t:
-            passing = net.along(passing, 1)
-        both = jnp.stack([passing, net.sibling(passing)])
-        h = layer_norm(both.astype(F32), gain[0], shift[0])
-        h_all = put(h_all, h, net.z_at(-t), 1)
-        part = dot(h.reshape(2 * rows, width), w_qkv) + b_qkv
-        qkv = put(qkv, part.astype(BF16).reshape(2, rows, 3 * lanes), net.z_at(-t), 1)
+            right = passing = net.along(right, 1)
+            ways = [(-t, right)]
+            if t <= (seq - 1) // 2:
+                left = net.along(left, -1)
+                ways.append((t, left))
+        for by, value in ways:
+            for page_at, x in ((core, value), (1 - core, net.sibling(value))):
+                spot = jnp.stack([page_at, net.z_at(by)]).astype(jnp.int32)
+                h_all, qkv = project(spot, x, gain[0], shift[0], w_qkv, b_qkv, h_all, qkv)
     h_all = h_all.reshape(2 * seq * rows, width)
     qkv = qkv.reshape(2, seq * rows, 3 * lanes)
 
-    w_outs = gather_rows(net, jnp.concatenate([self_out, cross_out], axis=1))
-    w_self_out, w_cross_out = w_outs[:, :width], w_outs[:, width:]
-    cross_halves = column_halves(cross_in)
-    cross_halves = cross_halves.transpose(1, 2, 0, 3).reshape(shard, 2, 3 * half)
-    w_cross = gather_columns(net, cross_halves)
-    w_cross_q, w_cross_kv = w_cross[:, :half], w_cross[:, half:]
-    w_up = gather_columns(net, column_halves(ff_in))
-    w_down = gather_rows(net, ff_out)
     cot_two = jnp.concatenate([cot, net.sibling(cot)], axis=0)
 
+    att_rows = min(512, rows)
+    def to_tokens(value):
+        blocks = value.reshape(seq, rows, lanes)
+        sent = [pick(blocks, net.z_at(-s)) for s in range(1, seq)]
+        got = [net.along(value, -s - 1) for s, value in enumerate(sent)]
+        return jnp.concatenate([pick(blocks, z)] + got, axis=1)
+
+    def to_heads(value):
+        blocks = by_core(net, value[:rows], value[rows:])
+        out = put(jnp.zeros((2, seq, rows, lanes), BF16), blocks[..., :lanes], z, 1)
+        for s in range(1, seq):
+            got = net.along(blocks[..., s * lanes : (s + 1) * lanes], s)
+            out = put(out, got, net.z_at(-s), 1)
+        return out.reshape(2, seq * rows, lanes)
+
+    def turned(weight, by):
+        twice = jnp.concatenate([weight, weight], axis=0)
+        return lax.dynamic_slice_in_dim(twice, by * lanes, half, axis=0)
+
+    o_self, lse_self, attended = [], [], []
+    order = jnp.zeros((1,), jnp.int32)
+    for k in range(2):
+        order = after(order, o_self[0]) if k else order
+        out, lse = self_fwd(order, qkv, att_rows, k)
+        o_self.append(out)
+        lse_self.append(lse)
+        attended.append(to_tokens(out[0]))
+    attended = jnp.concatenate(own_first(net, jnp.stack(attended)), axis=0)
+    up_line = line_gather_held(net, after(up_parts, passing), 1, o_self[1])
+    w_up = plane_gather(net, up_line).reshape(width, hidden // 2)
     mem_page = line_gather(net, mem, 0).reshape(-1, width)
+    down_line = line_gather_held(net, after(ff_out, o_self[1]), 0, attended)
+    w_down = plane_gather(net, down_line).reshape(hidden // 2, width)
     mem_all = jnp.concatenate([mem_page, net.sibling(mem_page)], axis=0)
     mem_rows = mem_page.shape[0]
     b_kv = jnp.concatenate([jnp.zeros((half,), F32), halves(bias[4])])
     kv_cross = (dot(mem_all, w_cross_kv) + b_kv).astype(BF16)
     kv_own, kv_other = kv_cross[:mem_rows], kv_cross[mem_rows:]
 
-    att_rows = min(512, rows)
-    o_self, lse_self = self_fwd(qkv, att_rows)
-
-    def to_tokens(value):
-        blocks = value.reshape(2, seq, rows, lanes)
-        out = jnp.zeros((2, rows, seq, lanes), BF16)
-        out = put(out, pick(blocks, z, 1), z, 2)
-        for s in range(1, seq):
-            out = put(out, net.along(pick(blocks, net.z_at(s), 1), s), net.z_at(-s), 2)
-        return out.reshape(2 * rows, half)
-
-    def to_heads(value):
-        blocks = value.reshape(2, rows, seq, lanes)
-        out = jnp.zeros((2, seq, rows, lanes), BF16)
-        out = put(out, pick(blocks, z, 2), z, 1)
-        for s in range(1, seq):
-            out = put(out, net.along(pick(blocks, net.z_at(s), 2), s), net.z_at(-s), 1)
-        return out.reshape(2, seq * rows, lanes)
 
     def summed(rows_two, weight, dims=NN):
         sent = dot(rows_two[rows:], weight, dims).astype(BF16)
@@ -591,7 +727,7 @@
     def both_pages(value):
         return jnp.concatenate([value, net.sibling(value)], axis=0)
 
-    attended = to_tokens(o_self)
+    w_self_out = turned(w_self_out, z)
     x_in = tok.astype(F32)
     x_one = x_in + summed(attended, w_self_out) + bias[2]
 
@@ -612,15 +748,16 @@
     g_pre = (dot(cot_two, w_down, NT) * slope).astype(BF16)
     grad_down = dot(act, cot_two, TN).astype(BF16)
     grad_up = dot(h_three, g_pre, TN).astype(BF16)
-    sum_down = scatter_rows(net, grad_down, ff_shard)
-    sum_up = join_halves(scatter_columns(net, grad_up, shard))
+    part_down = plane_scatter(net, grad_down.reshape(chips, seq, ff_shard, width))
+    part_up = plane_scatter(net, grad_up.reshape(chips, 2, seq, shard, hidden // 2))
     cot_wide = cot.astype(F32)
     back, d_gain2, d_shift2 = norm_back(x_two, gain[2], summed(g_pre, w_up, NT))
     g_two = cot_wide + back
 
-    g_cross = both_pages(g_two.astype(BF16))
+    g_cross = both_pages(after(g_two.astype(BF16), grad_down, grad_up))
     grad_cross_out = dot(o_cross, g_cross, TN).astype(BF16)
     d_oc = dot(g_cross, w_cross_out, NT).astype(BF16)
+    sum_down = line_scatter(net, after(part_down, g_cross), 0)
     dq_own, dk_own, dv_own = cross_bwd(
         limit_own, q_cross[:rows], kv_own, d_oc[:rows], oc_own, lse_own
     )
@@ -628,42 +765,58 @@
         limit_other, q_cross[rows:], kv_other, d_oc[rows:], oc_other, lse_other
     )
     dq_cross = jnp.concatenate([dq_own, dq_other], axis=0)
+    dq_cross = after(dq_cross, sum_down)
     dkv_own = jnp.concatenate([dk_own, dv_own], axis=1)
     dkv_other = jnp.concatenate([dk_other, dv_other], axis=1)
     dkv_cross = jnp.concatenate([dkv_own, dkv_other], axis=0)
     grad_cross = jnp.concatenate(
         [dot(h_two, dq_cross, TN).astype(BF16), dot(mem_all, dkv_cross, TN).astype(BF16)], axis=1
     )
-    sum_cross = scatter_columns(net, grad_cross, shard)
-    sum_cross = sum_cross.reshape(shard, 2, 3, half).transpose(2, 0, 1, 3)
-    sum_cross = join_halves(sum_cross)
+    part_cross = plane_scatter(net, grad_cross.reshape(chips, 2, seq, shard, 3 * half))
     mem_sent = dot(dkv_other, w_cross_kv, NT).astype(BF16)
     mem_grad = dot(dkv_own, w_cross_kv, NT) + net.sibling(mem_sent).astype(F32)
-    grad_memory = line_scatter(net, mem_grad.reshape(seq, -1, width), 0)
     back, d_gain1, d_shift1 = norm_back(x_one, gain[1], summed(dq_cross, w_cross_q, NT))
     g_one = g_two + back
 
-    g_self = both_pages(g_one.astype(BF16))
-    grad_self_out = dot(attended, g_self, TN).astype(BF16)
-    sum_outs = scatter_rows(net, jnp.concatenate([grad_self_out, grad_cross_out], axis=1), shard)
+    g_self = both_pages(after(g_one.astype(BF16), grad_cross))
+    grad_self_out = turned(dot(attended, g_self, TN).astype(BF16), lax.rem(seq - z, seq))
+    grad_outs = jnp.concatenate([grad_self_out, grad_cross_out], axis=1)
+    part_outs = plane_scatter(net, grad_outs.reshape(chips, seq, shard, 2 * width))
     d_os = to_heads(dot(g_self, w_self_out, NT).astype(BF16))
-    d_qkv = self_bwd(qkv, d_os, o_self, lse_self, att_rows)
-    other_h = dot(d_qkv[1], w_qkv, NT).astype(BF16)
-    d_h = dot(d_qkv[0], w_qkv, NT) + net.sibling(other_h).astype(F32)
-    d_h = line_scatter(net, d_h.reshape(seq, rows, width), 0)
-    flat = d_qkv.reshape(2 * seq * rows, 3 * lanes)
-    grad_qkv = dot(h_all, flat, TN).astype(BF16)
-    parts = ring_scatter(net, grad_qkv.reshape(chips, 2, seq * shard, 3 * lanes))
-    parts = parts.astype(BF16).reshape(2, seq, shard, 3 * lanes)
-    piece = jnp.zeros_like(parts)
-    piece = put(piece, pick(parts, z, 1), z, 1)
-    for s in range(1, seq):
-        piece = put(piece, net.along(pick(parts, net.z_at(s), 1), s), net.z_at(-s), 1)
-    own, other = own_first(net, piece)
-    piece = by_core(net, own, net.sibling(other))
-    sum_self = piece.reshape(2, seq, shard, 3, lanes).transpose(3, 2, 1, 0, 4)
-    sum_self = sum_self.reshape(3, shard, width).astype(F32)
-    back, d_gain0, d_shift0 = norm_back(x_in, gain[0], d_h)
+    sum_up = jnp.concatenate([part_up[0], part_up[1]], axis=1)
+    sum_up = seq_scatter(sum_up).reshape(2, shard, hidden // 2)
+    d_os = after(d_os, grad_outs, sum_up)
+    grad_memory = seq_scatter(after(mem_grad, part_outs).reshape(seq, -1, width).astype(BF16))
+    page_grads, d_hs = [], []
+    for k in range(2):
+        lse = after(lse_self[k], here, part_cross) if k else lse_self[k]
+        page_grad = self_bwd(qkv, d_os, o_self[k], lse, att_rows, k)[0]
+        page_grads.append(page_grad)
+        sides = w_qkv.reshape(2, half, 3 * lanes)
+        there = dot(page_grad, pick(sides, 1 - core), NT).astype(BF16)
+        here = dot(page_grad, pick(sides, core), NT) + net.sibling(there).astype(F32)
+        d_hs.append(line_two_way_scatter(net, here.reshape(seq, rows, half)))
+    own, other = own_first(net, jnp.stack(d_hs))
+    other = net.sibling(other)
+    d_h = jnp.concatenate(
+        [jnp.where(core == 0, own, other), jnp.where(core == 0, other, own)], axis=1
+    )
+    last = seq_scatter(jnp.concatenate([part_cross[0], part_cross[1], part_outs], axis=2))
+    sum_outs = last[:, 6 * half :]
+    sum_cross = jnp.stack([last[:, : 3 * half], last[:, 3 * half : 6 * half]])
+    columns = jnp.concatenate([sum_up, sum_cross], axis=2)
+    own, other = own_first(net, columns)
+    other = net.sibling(other)
+    sides = [jnp.where(core == k, own, other) for k in range(2)]
+
+    def joined(at, count):
+        two = jnp.stack([side[:, at : at + count] for side in sides], axis=1)
+        return join_halves(two)
+
+    sum_up = joined(0, hidden // 2)
+    sum_cross = jnp.stack([joined(hidden // 2 + k * half, half) for k in range(3)])
+    flat = after(jnp.concatenate(page_grads, axis=0), here, part_outs)
+    back, _, _ = norm_back(x_in, gain[0], d_h)
     token_grad = g_one + back
 
     def spread(vector):
@@ -675,6 +828,11 @@
         return lax.dynamic_update_slice_in_dim(jnp.zeros((width,), F32), vector, first, 0)
 
     sums_qkv = column_sum(flat)
+    grad_qkv = dot(h_all, flat, TN)
+    w_wide = w_qkv.astype(F32)
+    by_row = (grad_qkv - shift[0][:, None] * sums_qkv) / gain[0][:, None]
+    d_gain0 = jnp.sum(w_wide * by_row, axis=1)
+    d_shift0 = jnp.sum(w_wide * sums_qkv, axis=1)
     up_sum = column_sum(g_pre).reshape(chips, 1, seq * ff_shard)
     up_sum = jnp.where(jnp.arange(2)[None, :, None] == core, up_sum, 0.0)
     vectors = jnp.stack(
@@ -694,12 +852,26 @@
             column_sum(cot_wide),
         ]
     )
-    vectors = jnp.moveaxis(vectors.reshape(13, pages * seq, shard), 0, 1)
-    packed = jnp.concatenate(
-        [vectors.reshape(pages * seq, 13 * shard), up_sum.reshape(pages * seq, ff_shard)], axis=1
-    )
-    packed = lax.psum_scatter(packed, AXES, scatter_dimension=0, tiled=True)[0]
-    vectors = packed[: 13 * shard].reshape(13, shard)
+    small = jnp.concatenate([vectors.T, up_sum.reshape(width, ff_shard // shard)], axis=1)
+    small = jnp.pad(small, ((0, 0), (0, side - small.shape[1])))
+    parts = jnp.concatenate([grad_qkv.astype(BF16), small.astype(BF16)], axis=1)
+    parts = ring_scatter(net, parts.reshape(chips, 2, seq * shard, 3 * lanes + side))
+    parts = parts.reshape(2, seq, shard, 3 * lanes + side)
+    low = parts.astype(BF16)
+    piece = jnp.zeros((2, seq, shard, 3 * lanes), BF16)
+    piece = put(piece, pick(low, z, 1)[..., : 3 * lanes], z, 1)
+    small = pick(parts, z, 1)[..., 3 * lanes :]
+    for s in range(1, seq):
+        got = net.along(pick(low, net.z_at(s), 1), s)
+        piece = put(piece, got[..., : 3 * lanes], net.z_at(-s), 1)
+        small += got[..., 3 * lanes :].astype(F32)
+    own, other = own_first(net, piece)
+    piece = by_core(net, own, net.sibling(other))
+    sum_self = piece.reshape(2, seq, shard, 3, lanes).transpose(3, 2, 1, 0, 4)
+    sum_self = sum_self.reshape(3, shard, width).astype(F32)
+    own, other = own_first(net, small)
+    small = own + net.sibling(other)
+    vectors = small[:, :13].T
     return (
         layer_rows[None],
         token_grad[None],
@@ -713,7 +885,7 @@
         sum_up,
         sum_down,
         vectors[6:13],
-        packed[13 * shard :],
+        small[:, 13 : 13 + ff_shard // shard].reshape(ff_shard),
     )
 
 

time: 1100 us -> 703 us (0.64)
  waiting for transfers between devices: 468 us -> 216 us
  blocking collectives: 66.9 us -> 0 us
  starting transfers between devices: 143 us -> 76.3 us
  local copies, waits for them, and re-layouts: 127 us -> 101 us
  Pallas kernels: 85.4 us -> 104 us
  other arithmetic: 69.4 us -> 54 us
  between operations: 18.9 us -> 30.6 us
    unnamed x2 -> x10, waiting for transfers between devices: 114 us -> 0.16 us
    ppermute x48 -> x39, waiting for transfers between devices: 260 us -> 171 us  [along(): return lax.ppermute(value, AXES, self.line_map[by % self.seq])]
    ppermute x40 -> x8, waiting for transfers between devices: 91.9 us -> 11 us  [around(): return lax.ppermute(value, AXES, self.ring_map[way])]
    all_gather x1 -> x0, blocking collectives: 66.9 us -> none  [on_device(): small = lax.all_gather(small, AXES, axis=0)]
    ppermute x40 -> x8, starting transfers between devices: 43.7 us -> 8.31 us  [around(): return lax.ppermute(value, AXES, self.ring_map[way])]
    ppermute x48 -> x39, starting transfers between devices: 96.9 us -> 62.8 us  [along(): return lax.ppermute(value, AXES, self.line_map[by % self.seq])]
    reduce_scatter x0 -> x7, waiting for transfers between devices: none -> 30 us  [the longest x4 30 us: plane_scatter(): lax.psum_scatter(flat, AXES, scatter_dimension=0, axis_index_groups=net.p...]
    slice x9 -> x33, local copies, waits for them, and re-layouts: 4.41 us -> 29.4 us  [the longest x17 12.3 us: after(): element = lax.optimization_barrier(other)[(0,) * other.ndim].astype(F32)]
  transfers between devices with their start and end apart: 112 -> 81, of which waited for: 48 -> 30; matrix products, arithmetic and copies ran while one was open for 24% -> 33% of each run, Pallas kernels for 8% -> 15%
where the time goes in v2:
time: 703 us; the launch traced here: 693 us
  waiting for transfers between devices  216 us (31%)
  matrix products  111 us (16%)
  Pallas kernels  104 us (15%)
  local copies, waits for them, and re-layouts  101 us (14%)
  starting transfers between devices  76.3 us (11%)
  other arithmetic  54 us (8%)
  between operations  30.6 us (4%)
    ppermute x39, waiting for transfers between devices, along(): return lax.ppermute(value, AXES, self.line_map[by % self.seq])  171 us
    dot_general x29, matrix products, dot(): return lax.dot_general(a, b, dims, preferred_element_type=F32)  111 us
    ppermute x39, starting transfers between devices, along(): return lax.ppermute(value, AXES, self.line_map[by % self.seq])  62.8 us
    pallas_call x2, Pallas kernels, self_bwd(): pl.pallas_call(functools.partial(self_bwd_kernel, rows=rows, width=width)...  34.7 us
    unnamed x224, local copies, waits for them, and re-layouts  31.8 us
    reduce_scatter x4, waiting for transfers between devices, plane_scatter(): lax.psum_scatter(flat, AXES, scatter_dimension=0, axis_index_groups=net.p...  30 us
    pallas_call x2, Pallas kernels, self_fwd(): pl.pallas_call(functools.partial(self_fwd_kernel, rows=rows, width=width)...  22.4 us
    pallas_call x8, Pallas kernels, project(): pl.pallas_call(project_kernel, grid_spec=pltpu.PrefetchScalarGridSpec(num...  17.4 us
  transfers between devices with their start and end apart: 81, of which 30 were waited for; matrix products, arithmetic and copies ran while one was open for 33% of the time, Pallas kernels for 15%

profile of v2, /device:TPU:0, one launch (start us, length us, event | category | flops | bytes accessed | tf_op | source)
XLA Modules:
  0.0 692.8 jit_solution(11327661163006601954)
XLA Ops:
  29.7 8.4 %collective-permute-done.22 = bf16[32,5120]{1,0:T(8,128)(2,1)S(1)} collective-permute-done((bf16[32,5120]{1,0:T(8,128)(2,1)S(1)}, bf16[32,5120]{1,0:T(8,128)(2,1)S(1)}, u32[]{:S(2)}, u32[]{:S(2)}) %collective-permute-start.22) | collective-permute-done | bytes 327712 | tf_op jit(solution)/shard_map/ppermute | solution.py:382
  38.2 6.7 collective-permute-done.23
  44.9 5.8 collective-permute-done.24
  61.2 5.6 collective-permute-done.8
  71.3 4.5 slice_reduce_fusion.10
  87.4 14.9 %collective-permute-done.12.x_ref = bf16[512,1024]{1,0:T(8,128)(2,1)S(1)} collective-permute-done((bf16[512,1024]{1,0:T(8,128)(2,1)S(1)}, bf16[512,1024]{1,0:T(8,128)(2,1)S(1)}, u32[]{:S(2)}, u32[]{:S(2)}) %collective-permute-start.12) | collective-permute-done | bytes 1048608 | tf_op jit(solution)/shard_map/ppermute | solution.py:382
  102.4 24.2 %collective-permute-done.10.x_ref = bf16[512,1024]{1,0:T(8,128)(2,1)S(1)} collective-permute-done((bf16[512,1024]{1,0:T(8,128)(2,1)S(1)}, bf16[512,1024]{1,0:T(8,128)(2,1)S(1)}, u32[]{:S(2)}, u32[]{:S(2)}) %collective-permute-start.10) | collective-permute-done | bytes 1048608 | tf_op jit(solution)/shard_map/ppermute | solution.py:382
  148.1 11.2 %shard_map.245 = (bf16[1,2048,128]{2,1,0:T(8,128)(2,1)S(1)}, f32[1,2,1,2048]{3,2,1,0:T(1,128)S(1)}) custom-call(s32[1]{0:T(128)} %constant.278.clone.1.order_ref, bf16[2,2048,384]{2,1,0:T(8,128)(2,1)S(1)} %bitcast.446, bf16[2,2048,384]{2,1,0:T(8,128)(2,1)S(1)} %bitcast.447), custom_call_target="tpu_custom_call" | custom-call | flops 2147483648 | bytes 6291456 | tf_op jit(solution)/shard_map/pallas_call | solution.py:123
  160.5 11.2 %shard_map.246 = (bf16[1,2048,128]{2,1,0:T(8,128)(2,1)S(1)}, f32[1,2,1,2048]{3,2,1,0:T(1,128)S(1)}) custom-call(s32[1]{0:T(128)} %bitcast.36.order_ref, bf16[2,2048,384]{2,1,0:T(8,128)(2,1)S(1)} %bitcast.448, bf16[2,2048,384]{2,1,0:T(8,128)(2,1)S(1)} %bitcast.449), custom_call_target="tpu_custom_call" | custom-call | flops 2147483648 | bytes 6291456 | tf_op jit(solution)/shard_map/pallas_call | solution.py:123
  182.3 6.4 collective-permute-done.27
  209.8 9.1 %collective-permute-done.19 = bf16[512,128]{1,0:T(8,128)(2,1)S(1)} collective-permute-done((bf16[512,128]{1,0:T(8,128)(2,1)S(1)}, bf16[512,128]{1,0:T(8,128)(2,1)S(1)}, u32[]{:S(2)}, u32[]{:S(2)}) %collective-permute-start.19) | collective-permute-done | bytes 131104 | tf_op jit(solution)/shard_map/ppermute | solution.py:382
  221.2 14.5 %collective-permute-done.16 = bf16[512,128]{1,0:T(8,128)(2,1)S(1)} collective-permute-done((bf16[512,128]{1,0:T(8,128)(2,1)S(1)}, bf16[512,128]{1,0:T(8,128)(2,1)S(1)}, u32[]{:S(2)}, u32[]{:S(2)}) %collective-permute-start.16) | collective-permute-done | bytes 131104 | tf_op jit(solution)/shard_map/ppermute | solution.py:382
  258.0 5.4 add_convert_fusion
  265.1 6.1 shard_map.248
  272.9 6.1 shard_map.247
  284.7 10.0 %multiply_convert_fusion = (bf16[1024,2048]{1,0:T(8,128)(2,1)S(1)}, f32[1024,2048]{1,0:T(8,128)}) fusion(f32[2048]{0:T(1024)S(1)} %bitcast.513, bf16[1024,2048]{1,0:T(8,128)(2,1)} %bitcast.523, bf16[512,1024]{1,0:T(8,128)(2,1)} %collective-permute-done.32, bf16[512,1024]{1,0:T(8,128)(2,1)} %add_convert_fusion.3), kind=kOutput, calls=%fused_computation.8 | convolution fusion | flops 4311744512 | bytes 18882560 | tf_op jit(solution)/shard_map/dot_general | solution.py:28
  296.6 8.0 %convolution_convert_fusion.1 = bf16[2048,1024]{1,0:T(8,128)(2,1)} fusion(bf16[1024,2048]{1,0:T(8,128)(2,1)S(1)} %get-tuple-element.225, bf16[512,1024]{1,0:T(8,128)(2,1)} %collective-permute-done.40, bf16[512,1024]{1,0:T(8,128)(2,1)} %bitcast.96), kind=kOutput, calls=%fused_computation.15 | convolution fusion | flops 4301258752 | bytes 10485760 | tf_op jit(solution)/shard_map/dot_general | solution.py:28
  304.7 11.1 %convert_reduce_fusion = (bf16[2048]{0:T(1024)(128)(2,1)S(1)}, bf16[1024,2048]{1,0:T(8,128)(2,1)S(1)}) fusion(f32[1024,2048]{1,0:T(8,128)} %get-tuple-element.226, f32[2048]{0:T(1024)S(1)} %bitcast.514, bf16[2048,1024]{1,0:T(8,128)(2,1)} %bitcast.526, bf16[512,1024]{1,0:T(8,128)(2,1)} %collective-permute-done.40, bf16[512,1024]{1,0:T(8,128)(2,1)} %bitcast.96), kind=kOutput, calls=%fused_computation.7 | convolution fusion | flops 4326422528 | bytes 18886656 | tf_op jit(solution)/shard_map/dot_general | solution.py:28
  317.7 8.1 %convolution_convert_fusion = bf16[1024,2048]{1,0:T(8,128)(2,1)} fusion(bf16[1024,2048]{1,0:T(8,128)(2,1)S(1)} %get-tuple-element.229, bf16[512,1024]{1,0:T(8,128)(2,1)} %collective-permute-done.32, bf16[512,1024]{1,0:T(8,128)(2,1)} %add_convert_fusion.3), kind=kOutput, calls=%fused_computation.14 | convolution fusion | flops 4301258752 | bytes 10485760 | tf_op jit(solution)/shard_map/dot_general | solution.py:28
  328.1 5.4 fusion.40
  357.3 8.7 %shard_map.249 = (bf16[512,512]{1,0:T(8,128)(2,1)S(1)}, bf16[640,512]{1,0:T(8,128)(2,1)S(1)}, bf16[640,512]{1,0:T(8,128)(2,1)S(1)}) custom-call(s32[1]{0:T(128)} %bitcast.61.limit_ref, bf16[512,512]{1,0:T(8,128)(2,1)S(1)} %copy-done.14, bf16[640,1024]{1,0:T(8,128)(2,1)S(1)} %get-tuple-element.149.k_ref.v_ref, ...), custom_call_target="tpu_custom_call" | custom-call | flops 1677721600 | bytes 5505024 | tf_op jit(solution)/shard_map/pallas_call | solution.py:304
  367.0 8.7 %shard_map.250 = (bf16[512,512]{1,0:T(8,128)(2,1)S(1)}, bf16[640,512]{1,0:T(8,128)(2,1)S(1)}, bf16[640,512]{1,0:T(8,128)(2,1)S(1)}) custom-call(s32[1]{0:T(128)} %bitcast.76.limit_ref, bf16[512,512]{1,0:T(8,128)(2,1)S(1)} %copy-done.12, bf16[640,1024]{1,0:T(8,128)(2,1)S(1)} %get-tuple-element.148.k_ref.v_ref, ...), custom_call_target="tpu_custom_call" | custom-call | flops 1677721600 | bytes 5505024 | tf_op jit(solution)/shard_map/pallas_call | solution.py:304
  383.9 30.0 %reduce-scatter.10.cloned.1.call-done = bf16[256,2048]{1,0:T(8,128)(2,1)} async-done(((bf16[1024,2048]{1,0:T(8,128)(2,1)}), bf16[256,2048]{1,0:T(8,128)(2,1)}) %reduce-scatter.10.cloned.1.call-update) | async-done | bytes 1048592 | tf_op jit(solution)/shard_map/reduce_scatter | solution.py:485
  423.3 5.0 fusion.32
  463.4 9.3 %collective-permute-done.49 = bf16[2,512,128]{2,1,0:T(8,128)(2,1)S(1)} collective-permute-done((bf16[2,512,128]{2,1,0:T(8,128)(2,1)}, bf16[2,512,128]{2,1,0:T(8,128)(2,1)S(1)}, u32[]{:S(2)}, u32[]{:S(2)}) %collective-permute-start.49) | collective-permute-done | bytes 262176 | tf_op jit(solution)/shard_map/ppermute | solution.py:382
  475.0 17.4 %shard_map.251 = bf16[1,2048,384]{2,1,0:T(8,128)(2,1)S(1)} custom-call(bf16[2,2048,384]{2,1,0:T(8,128)(2,1)} %bitcast.450, bf16[2,2048,384]{2,1,0:T(8,128)(2,1)} %bitcast.451, bf16[2,2048,128]{2,1,0:T(8,128)(2,1)S(1)} %bitcast.462, bf16[1,2048,128]{2,1,0:T(8,128)(2,1)S(1)} %copy-done.10, f32[1,2,1,2048]{3,2,1,0:T(1,128)S(1)} %get-tuple-element.70.lse_ref), custom_call_target="tpu_custom_call" | custom-call | flops 5368709120 | bytes 9437184 | tf_op jit(solution)/shard_map/pallas_call | solution.py:201
  508.5 17.3 %shard_map.252 = bf16[1,2048,384]{2,1,0:T(8,128)(2,1)S(1)} custom-call(bf16[2,2048,384]{2,1,0:T(8,128)(2,1)} %bitcast.452, bf16[2,2048,384]{2,1,0:T(8,128)(2,1)} %bitcast.453, bf16[2,2048,128]{2,1,0:T(8,128)(2,1)S(1)} %bitcast.463, bf16[1,2048,128]{2,1,0:T(8,128)(2,1)S(1)} %copy-done.8, f32[1,2,1,2048]{3,2,1,0:T(1,128)S(1)} %add_add_fusion.3.lse_ref), custom_call_target="tpu_custom_call" | custom-call | flops 5368709120 | bytes 9437184 | tf_op jit(solution)/shard_map/pallas_call | solution.py:201
  540.3 9.2 %collective-permute-done.52 = bf16[512,512]{1,0:T(8,128)(2,1)S(1)} collective-permute-done((bf16[512,512]{1,0:T(8,128)(2,1)S(1)}, bf16[512,512]{1,0:T(8,128)(2,1)S(1)}, u32[]{:S(2)}, u32[]{:S(2)}) %collective-permute-start.52) | collective-permute-done | bytes 524320 | tf_op jit(solution)/shard_map/ppermute | solution.py:382
  564.8 8.3 %fusion.151 = (bf16[1024,384]{0,1:T(8,128)(2,1)}, f32[1024,384]{0,1:T(8,128)}) fusion(bf16[4096,1024]{1,0:T(8,128)(2,1)} %bitcast.445, bf16[2048,384]{1,0:T(8,128)(2,1)S(1)} %bitcast.460, bf16[2048,384]{1,0:T(8,128)(2,1)S(1)} %bitcast.458, bf16[]{:T(256)S(6)} %convert_element_type.532, bf16[]{:T(256)} %bitcast.151), kind=kOutput, calls=%fused_computation.395 | convolution fusion | flops 3234201600 | bytes 13893636 | tf_op jit(solution)/shard_map/dot_general | solution.py:28
  597.2 4.7 collective-permute-start.58
  606.0 41.4 %collective-permute-done.65 = bf16[2,32,512]{2,1,0:T(8,128)(2,1)S(1)} collective-permute-done((bf16[2,32,512]{2,1,0:T(8,128)(2,1)S(1)}, bf16[2,32,512]{2,1,0:T(8,128)(2,1)S(1)}, u32[]{:S(2)}, u32[]{:S(2)}) %collective-permute-start.65) | collective-permute-done | bytes 65568 | tf_op jit(solution)/shard_map/ppermute | solution.py:382
  666.6 7.0 %collective-permute-done.57 = bf16[512,512]{1,0:T(8,128)(2,1)} collective-permute-done((bf16[512,512]{1,0:T(8,128)(2,1)}, bf16[512,512]{1,0:T(8,128)(2,1)}, u32[]{:S(2)}, u32[]{:S(2)}) %collective-permute-start.57) | collective-permute-done | bytes 524320 | tf_op jit(solution)/shard_map/ppermute | solution.py:382
  (665 shorter events, 312.6 us)
Async XLA Ops:
  7.2 231.1 %all-gather.4.cloned.1.call-start = ((), (), s32[]{:S(2)}) async-start(), calls=%async_computation.7 | async-start | bytes 6553600 | tf_op jit(solution)/shard_map/all_gather | solution.py:480
  51.8 232.8 %all-gather.6.cloned.1.call-start = ((), (), s32[]{:S(2)}) async-start(), calls=%async_computation.8 | async-start | bytes 5242880 | tf_op jit(solution)/shard_map/all_gather | solution.py:480
  54.2 28.5 %collective-permute-start.5 = (bf16[512,1024]{1,0:T(8,128)(2,1)S(1)}, bf16[512,1024]{1,0:T(8,128)(2,1)}, u32[]{:S(2)}, u32[]{:S(2)}) collective-permute-start(bf16[512,1024]{1,0:T(8,128)(2,1)S(1)} %add_bitcast_fusion.x_ref), channel_id=1, source_target_pairs={{0,4},{1,5},{2,6},{3,7},{4,0},{5,1},{6,2},{7,3},{8,12},{9,13},{10,... | collective-permute-start | bytes 3145736 | tf_op jit(solution)/shard_map/ppermute | solution.py:379
  54.3 32.9 %collective-permute-start.4 = (bf16[512,1024]{1,0:T(8,128)(2,1)S(1)}, bf16[512,1024]{1,0:T(8,128)(2,1)S(1)}, u32[]{:S(2)}, u32[]{:S(2)}) collective-permute-start(bf16[512,1024]{1,0:T(8,128)(2,1)S(1)} %add_bitcast_fusion.x_ref), channel_id=1, source_target_pairs={{0,1},{1,2},{2,3},{3,0},{4,5},{5,6},{6,7},{7,4},{8,9},{9,10},{10,1... | collective-permute-start | bytes 3145736 | tf_op jit(solution)/shard_map/ppermute | solution.py:382
  54.5 47.8 %collective-permute-start.12 = (bf16[512,1024]{1,0:T(8,128)(2,1)S(1)}, bf16[512,1024]{1,0:T(8,128)(2,1)S(1)}, u32[]{:S(2)}, u32[]{:S(2)}) collective-permute-start(bf16[512,1024]{1,0:T(8,128)(2,1)S(1)} %add_bitcast_fusion.x_ref), channel_id=1, source_target_pairs={{0,3},{1,0},{2,1},{3,2},{4,7},{5,4},{6,5},{7,6},{8,11},{9,8},{10,9... | collective-permute-start | bytes 3145736 | tf_op jit(solution)/shard_map/ppermute | solution.py:382
  87.2 39.4 %collective-permute-start.10 = (bf16[512,1024]{1,0:T(8,128)(2,1)S(1)}, bf16[512,1024]{1,0:T(8,128)(2,1)S(1)}, u32[]{:S(2)}, u32[]{:S(2)}) collective-permute-start(bf16[512,1024]{1,0:T(8,128)(2,1)S(1)} %broadcast_add_fusion.1), channel_id=1, source_target_pairs={{0,1},{1,2},{2,3},{3,0},{4,5},{5,6},{6,7},{7,4},{8,9},{9,10},{10,1... | collective-permute-start | bytes 3145736 | tf_op jit(solution)/shard_map/ppermute | solution.py:382
  87.4 43.8 %collective-permute-start.14 = (bf16[512,1024]{1,0:T(8,128)(2,1)S(1)}, bf16[512,1024]{1,0:T(8,128)(2,1)S(1)}, u32[]{:S(2)}, u32[]{:S(2)}) collective-permute-start(bf16[512,1024]{1,0:T(8,128)(2,1)S(1)} %collective-permute-done.4.x_ref), channel_id=1, source_target_pairs={{0,4},{1,5},{2,6},{3,7},{4,0},{5,1},{6,2},{7,3},{8,12},{9,13},{10,... | collective-permute-start | bytes 3145736 | tf_op jit(solution)/shard_map/ppermute | solution.py:379
  102.3 36.3 %collective-permute-start.13 = (bf16[512,1024]{1,0:T(8,128)(2,1)S(1)}, bf16[512,1024]{1,0:T(8,128)(2,1)S(1)}, u32[]{:S(2)}, u32[]{:S(2)}) collective-permute-start(bf16[512,1024]{1,0:T(8,128)(2,1)S(1)} %collective-permute-done.12.x_ref), channel_id=1, source_target_pairs={{0,4},{1,5},{2,6},{3,7},{4,0},{5,1},{6,2},{7,3},{8,12},{9,13},{10,... | collective-permute-start | bytes 3145736 | tf_op jit(solution)/shard_map/ppermute | solution.py:379
  130.3 42.7 %collective-permute-start.33 = (bf16[2,32,2048]{2,1,0:T(8,128)(2,1)S(1)}, bf16[2,32,2048]{2,1,0:T(8,128)(2,1)}, u32[]{:S(2)}, u32[]{:S(2)}) collective-permute-start(bf16[2,32,2048]{2,1,0:T(8,128)(2,1)S(1)} %get-tuple-element.131), channel_id=1, source_target_pairs={{0,1},{1,2},{2,3},{3,0},{4,5},{5,6},{6,7},{7,4},{8,9},{9,10},{10,1... | collective-permute-start | bytes 786440 | tf_op jit(solution)/shard_map/ppermute | solution.py:382
  130.4 43.7 %collective-permute-start.34 = (bf16[2,32,2048]{2,1,0:T(8,128)(2,1)S(1)}, bf16[2,32,2048]{2,1,0:T(8,128)(2,1)S(1)}, u32[]{:S(2)}, u32[]{:S(2)}) collective-permute-start(bf16[2,32,2048]{2,1,0:T(8,128)(2,1)S(1)} %get-tuple-element.131), channel_id=1, source_target_pairs={{0,2},{1,3},{2,0},{3,1},{4,6},{5,7},{6,4},{7,5},{8,10},{9,11},{10,... | collective-permute-start | bytes 786440 | tf_op jit(solution)/shard_map/ppermute | solution.py:382
  131.2 42.9 %collective-permute-start.35 = (bf16[2,32,2048]{2,1,0:T(8,128)(2,1)S(1)}, bf16[2,32,2048]{2,1,0:T(8,128)(2,1)}, u32[]{:S(2)}, u32[]{:S(2)}) collective-permute-start(bf16[2,32,2048]{2,1,0:T(8,128)(2,1)S(1)} %get-tuple-element.131), channel_id=1, source_target_pairs={{0,3},{1,0},{2,1},{3,2},{4,7},{5,4},{6,5},{7,6},{8,11},{9,8},{10,9... | collective-permute-start | bytes 786440 | tf_op jit(solution)/shard_map/ppermute | solution.py:382
  176.2 128.5 %all-gather.8.cloned.1.call-start = ((), (), s32[]{:S(2)}) async-start(), calls=%async_computation.9 | async-start | bytes 5242880 | tf_op jit(solution)/shard_map/all_gather | solution.py:480
  218.8 39.2 %collective-permute-start.30 = (bf16[640,1024]{1,0:T(8,128)(2,1)}, bf16[640,1024]{1,0:T(8,128)(2,1)}, u32[]{:S(2)}, u32[]{:S(2)}) collective-permute-start(bf16[640,1024]{1,0:T(8,128)(2,1)} %bitcast.70), channel_id=1, source_target_pairs={{0,4},{1,5},{2,6},{3,7},{4,0},{5,1},{6,2},{7,3},{8,12},{9,13},{10,... | collective-permute-start | bytes 3932168 | tf_op jit(solution)/shard_map/ppermute | solution.py:379
  249.6 127.9 %reduce-scatter.8.cloned.1.call-start = ((), (), s32[]{:S(2)}) async-start(), calls=%async_computation.10 | async-start | bytes 5242880 | tf_op jit(solution)/shard_map/reduce_scatter | solution.py:485
  304.6 109.3 %reduce-scatter.10.cloned.1.call-start = ((), (), s32[]{:S(2)}) async-start(), calls=%async_computation.11 | async-start | bytes 5242880 | tf_op jit(solution)/shard_map/reduce_scatter | solution.py:485
  325.8 117.9 %reduce-scatter.12.cloned.1.call-start = ((), (), s32[]{:S(2)}) async-start(), calls=%async_computation.12 | async-start | bytes 1310720 | tf_op jit(solution)/shard_map/reduce_scatter | solution.py:493
  379.8 38.5 %collective-permute-start.43 = (bf16[128,1024]{1,0:T(8,128)(2,1)}, bf16[128,1024]{1,0:T(8,128)(2,1)}, u32[]{:S(2)}, u32[]{:S(2)}) collective-permute-start(bf16[128,1024]{1,0:T(8,128)(2,1)} %get-tuple-element.169), channel_id=1, source_target_pairs={{0,1},{1,2},{2,3},{3,0},{4,5},{5,6},{6,7},{7,4},{8,9},{9,10},{10,1... | collective-permute-start | bytes 786440 | tf_op jit(solution)/shard_map/ppermute | solution.py:382
  381.5 36.7 %collective-permute-start.44 = (bf16[128,1024]{1,0:T(8,128)(2,1)}, bf16[128,1024]{1,0:T(8,128)(2,1)}, u32[]{:S(2)}, u32[]{:S(2)}) collective-permute-start(bf16[128,1024]{1,0:T(8,128)(2,1)} %get-tuple-element.171), channel_id=1, source_target_pairs={{0,2},{1,3},{2,0},{3,1},{4,6},{5,7},{6,4},{7,5},{8,10},{9,11},{10,... | collective-permute-start | bytes 786440 | tf_op jit(solution)/shard_map/ppermute | solution.py:382
  382.0 36.3 %collective-permute-start.45 = (bf16[128,1024]{1,0:T(8,128)(2,1)S(1)}, bf16[128,1024]{1,0:T(8,128)(2,1)}, u32[]{:S(2)}, u32[]{:S(2)}) collective-permute-start(bf16[128,1024]{1,0:T(8,128)(2,1)S(1)} %get-tuple-element.170), channel_id=1, source_target_pairs={{0,3},{1,0},{2,1},{3,2},{4,7},{5,4},{6,5},{7,6},{8,11},{9,8},{10,9... | collective-permute-start | bytes 786440 | tf_op jit(solution)/shard_map/ppermute | solution.py:382
  416.3 89.3 %reduce-scatter.14.cloned.1.call-start = ((), (), s32[]{:S(2)}) async-start(), calls=%async_computation.13 | async-start | bytes 3932160 | tf_op jit(solution)/shard_map/reduce_scatter | solution.py:485
  433.6 120.3 %reduce-scatter.16.cloned.1.call-start = ((), (), s32[]{:S(2)}) async-start(), calls=%async_computation.14 | async-start | bytes 2621440 | tf_op jit(solution)/shard_map/reduce_scatter | solution.py:485
  495.0 158.0 %reduce-scatter.20.cloned.1.call-start = ((), (), s32[]{:S(2)}) async-start(), calls=%async_computation.16 | async-start | bytes 1638400 | tf_op jit(solution)/shard_map/reduce_scatter | solution.py:493
  528.5 29.6 %collective-permute-start.55 = (bf16[2048,512]{1,0:T(8,128)(2,1)}, bf16[2048,512]{1,0:T(8,128)(2,1)}, u32[]{:S(2)}, u32[]{:S(2)}) collective-permute-start(bf16[2048,512]{1,0:T(8,128)(2,1)} %convolution_convert_fusion.2), channel_id=1, source_target_pairs={{0,4},{1,5},{2,6},{3,7},{4,0},{5,1},{6,2},{7,3},{8,12},{9,13},{10,... | collective-permute-start | bytes 6291464 | tf_op jit(solution)/shard_map/ppermute | solution.py:379
  538.5 50.8 %collective-permute-start.60 = (bf16[640,1024]{1,0:T(8,128)(2,1)}, bf16[640,1024]{1,0:T(8,128)(2,1)}, u32[]{:S(2)}, u32[]{:S(2)}) collective-permute-start(bf16[640,1024]{1,0:T(8,128)(2,1)} %convolution_convert_fusion.4), channel_id=1, source_target_pairs={{0,4},{1,5},{2,6},{3,7},{4,0},{5,1},{6,2},{7,3},{8,12},{9,13},{10,... | collective-permute-start | bytes 3932168 | tf_op jit(solution)/shard_map/ppermute | solution.py:379
  538.8 43.1 %collective-permute-start.54 = (bf16[512,512]{1,0:T(8,128)(2,1)}, bf16[512,512]{1,0:T(8,128)(2,1)}, u32[]{:S(2)}, u32[]{:S(2)}) collective-permute-start(bf16[512,512]{1,0:T(8,128)(2,1)} %get-tuple-element.145), channel_id=1, source_target_pairs={{0,3},{1,0},{2,1},{3,2},{4,7},{5,4},{6,5},{7,6},{8,11},{9,8},{10,9... | collective-permute-start | bytes 1572872 | tf_op jit(solution)/shard_map/ppermute | solution.py:382
  551.7 30.2 %collective-permute-start.53 = (bf16[512,512]{1,0:T(8,128)(2,1)}, bf16[512,512]{1,0:T(8,128)(2,1)}, u32[]{:S(2)}, u32[]{:S(2)}) collective-permute-start(bf16[512,512]{1,0:T(8,128)(2,1)} %fusion.60), channel_id=1, source_target_pairs={{0,1},{1,2},{2,3},{3,0},{4,5},{5,6},{6,7},{7,4},{8,9},{9,10},{10,1... | collective-permute-start | bytes 1572872 | tf_op jit(solution)/shard_map/ppermute | solution.py:382
  556.2 103.0 %reduce-scatter.18.cloned.1.call-start = ((), (), s32[]{:S(2)}) async-start(), calls=%async_computation.15 | async-start | bytes 1638400 | tf_op jit(solution)/shard_map/reduce_scatter | solution.py:493
  595.9 59.2 %collective-permute-start.56 = (bf16[512,512]{1,0:T(8,128)(2,1)}, bf16[512,512]{1,0:T(8,128)(2,1)S(1)}, u32[]{:S(2)}, u32[]{:S(2)}) collective-permute-start(bf16[512,512]{1,0:T(8,128)(2,1)} %get-tuple-element.142), channel_id=1, source_target_pairs={{0,1},{1,2},{2,3},{3,0},{4,5},{5,6},{6,7},{7,4},{8,9},{9,10},{10,1... | collective-permute-start | bytes 1572872 | tf_op jit(solution)/shard_map/ppermute | solution.py:382
  597.2 69.4 %collective-permute-start.58 = (bf16[512,512]{1,0:T(8,128)(2,1)}, bf16[512,512]{1,0:T(8,128)(2,1)}, u32[]{:S(2)}, u32[]{:S(2)}) collective-permute-start(bf16[512,512]{1,0:T(8,128)(2,1)} %get-tuple-element.143), channel_id=1, source_target_pairs={{0,3},{1,0},{2,1},{3,2},{4,7},{5,4},{6,5},{7,6},{8,11},{9,8},{10,9... | collective-permute-start | bytes 1572872 | tf_op jit(solution)/shard_map/ppermute | solution.py:382
  602.1 45.4 %collective-permute-start.65 = (bf16[2,32,512]{2,1,0:T(8,128)(2,1)S(1)}, bf16[2,32,512]{2,1,0:T(8,128)(2,1)S(1)}, u32[]{:S(2)}, u32[]{:S(2)}) collective-permute-start(bf16[2,32,512]{2,1,0:T(8,128)(2,1)S(1)} %get-tuple-element.209), channel_id=1, source_target_pairs={{0,1},{1,2},{2,3},{3,0},{4,5},{5,6},{6,7},{7,4},{8,9},{9,10},{10,1... | collective-permute-start | bytes 196616 | tf_op jit(solution)/shard_map/ppermute | solution.py:382
  602.1 46.8 %collective-permute-start.66 = (bf16[2,32,512]{2,1,0:T(8,128)(2,1)S(1)}, bf16[2,32,512]{2,1,0:T(8,128)(2,1)S(1)}, u32[]{:S(2)}, u32[]{:S(2)}) collective-permute-start(bf16[2,32,512]{2,1,0:T(8,128)(2,1)S(1)} %get-tuple-element.208), channel_id=1, source_target_pairs={{0,2},{1,3},{2,0},{3,1},{4,6},{5,7},{6,4},{7,5},{8,10},{9,11},{10,... | collective-permute-start | bytes 196616 | tf_op jit(solution)/shard_map/ppermute | solution.py:382
  604.7 44.2 %collective-permute-start.67 = (bf16[2,32,512]{2,1,0:T(8,128)(2,1)S(1)}, bf16[2,32,512]{2,1,0:T(8,128)(2,1)S(1)}, u32[]{:S(2)}, u32[]{:S(2)}) collective-permute-start(bf16[2,32,512]{2,1,0:T(8,128)(2,1)S(1)} %get-tuple-element.207), channel_id=1, source_target_pairs={{0,3},{1,0},{2,1},{3,2},{4,7},{5,4},{6,5},{7,6},{8,11},{9,8},{10,9... | collective-permute-start | bytes 196616 | tf_op jit(solution)/shard_map/ppermute | solution.py:382
  (158 other events, 1313.6 us)
Sparse Core Ops, SparseCore 0:
  51.9 62.2 all-gather.3
  176.3 52.5 all-gather.5
  249.7 52.6 all-gather.7
  305.2 52.7 reduce-scatter.7
  361.1 52.6 reduce-scatter.9
  416.4 27.1 reduce-scatter.11
  446.8 42.5 reduce-scatter.13
  495.1 37.0 reduce-scatter.15
  556.3 37.4 reduce-scatter.19
  595.9 50.8 reduce-scatter.17

commit v3 on v2

--- a/solution.py
+++ b/solution.py
@@ -513,13 +513,13 @@
     return line_scatter(net, plane_scatter(net, parts), 0)
 
 
-def line_two_way_scatter(net, parts):
+def line_two_way_scatter(net, parts, hold=()):
     total = pick(parts, net.z)
     for way, far in ((1, net.seq // 2), (-1, (net.seq - 1) // 2)):
         got = None
         for by in range(far, 0, -1):
             mine = pick(parts, net.z_at(way * by))
-            sent = (mine if got is None else mine + got).astype(BF16)
+            sent = mine.astype(BF16) if got is None else after((mine + got).astype(BF16), *hold)
             got = net.along(sent, way).astype(F32)
         if got is not None:
             total += got
@@ -748,6 +748,7 @@
     g_pre = (dot(cot_two, w_down, NT) * slope).astype(BF16)
     grad_down = dot(act, cot_two, TN).astype(BF16)
     grad_up = dot(h_three, g_pre, TN).astype(BF16)
+    grad_up = after(grad_up, grad_down)
     part_down = plane_scatter(net, grad_down.reshape(chips, seq, ff_shard, width))
     part_up = plane_scatter(net, grad_up.reshape(chips, 2, seq, shard, hidden // 2))
     cot_wide = cot.astype(F32)
@@ -757,7 +758,6 @@
     g_cross = both_pages(after(g_two.astype(BF16), grad_down, grad_up))
     grad_cross_out = dot(o_cross, g_cross, TN).astype(BF16)
     d_oc = dot(g_cross, w_cross_out, NT).astype(BF16)
-    sum_down = line_scatter(net, after(part_down, g_cross), 0)
     dq_own, dk_own, dv_own = cross_bwd(
         limit_own, q_cross[:rows], kv_own, d_oc[:rows], oc_own, lse_own
     )
@@ -765,7 +765,7 @@
         limit_other, q_cross[rows:], kv_other, d_oc[rows:], oc_other, lse_other
     )
     dq_cross = jnp.concatenate([dq_own, dq_other], axis=0)
-    dq_cross = after(dq_cross, sum_down)
+    dq_cross = after(dq_cross, part_down)
     dkv_own = jnp.concatenate([dk_own, dv_own], axis=1)
     dkv_other = jnp.concatenate([dk_other, dv_other], axis=1)
     dkv_cross = jnp.concatenate([dkv_own, dkv_other], axis=0)
@@ -778,30 +778,41 @@
     back, d_gain1, d_shift1 = norm_back(x_one, gain[1], summed(dq_cross, w_cross_q, NT))
     g_one = g_two + back
 
+    grad_memory = seq_scatter(mem_grad.reshape(seq, -1, width).astype(BF16))
     g_self = both_pages(after(g_one.astype(BF16), grad_cross))
     grad_self_out = turned(dot(attended, g_self, TN).astype(BF16), lax.rem(seq - z, seq))
     grad_outs = jnp.concatenate([grad_self_out, grad_cross_out], axis=1)
     part_outs = plane_scatter(net, grad_outs.reshape(chips, seq, shard, 2 * width))
     d_os = to_heads(dot(g_self, w_self_out, NT).astype(BF16))
-    sum_up = jnp.concatenate([part_up[0], part_up[1]], axis=1)
-    sum_up = seq_scatter(sum_up).reshape(2, shard, hidden // 2)
-    d_os = after(d_os, grad_outs, sum_up)
-    grad_memory = seq_scatter(after(mem_grad, part_outs).reshape(seq, -1, width).astype(BF16))
+    d_os = after(d_os, grad_outs, grad_memory)
+    ff_rows = 2 * shard
+    low_down = part_down.reshape(seq, 2, ff_shard // 2, width)
+    low_down = jnp.concatenate([low_down[:, 0], low_down[:, 1]], axis=2)
+    low_up = part_up.transpose(1, 0, 2, 3).reshape(seq, ff_rows, hidden // 2)
+    sum_ff = seq_scatter(after(jnp.concatenate([low_up, low_down], axis=1), d_os))
     page_grads, d_hs = [], []
     for k in range(2):
-        lse = after(lse_self[k], here, part_cross) if k else lse_self[k]
+        lse = after(lse_self[k], here) if k else lse_self[k]
         page_grad = self_bwd(qkv, d_os, o_self[k], lse, att_rows, k)[0]
         page_grads.append(page_grad)
         sides = w_qkv.reshape(2, half, 3 * lanes)
         there = dot(page_grad, pick(sides, 1 - core), NT).astype(BF16)
         here = dot(page_grad, pick(sides, core), NT) + net.sibling(there).astype(F32)
-        d_hs.append(line_two_way_scatter(net, here.reshape(seq, rows, half)))
+        d_hs.append(here)
+    d_hs = [
+        line_two_way_scatter(net, d_hs[k].reshape(seq, rows, half), () if k else (here,)) for k in range(2)
+    ]
     own, other = own_first(net, jnp.stack(d_hs))
     other = net.sibling(other)
     d_h = jnp.concatenate(
         [jnp.where(core == 0, own, other), jnp.where(core == 0, other, own)], axis=1
     )
-    last = seq_scatter(jnp.concatenate([part_cross[0], part_cross[1], part_outs], axis=2))
+    sum_ff = after(sum_ff, d_hs[0])
+    sum_up = sum_ff[:ff_rows].reshape(2, shard, hidden // 2)
+    sum_down = sum_ff[ff_rows:]
+    sum_down = jnp.concatenate([sum_down[:, :width], sum_down[:, width:]], axis=0)
+    last = jnp.concatenate([part_cross[0], part_cross[1], part_outs], axis=2)
+    last = seq_scatter(after(last, here))
     sum_outs = last[:, 6 * half :]
     sum_cross = jnp.stack([last[:, : 3 * half], last[:, 3 * half : 6 * half]])
     columns = jnp.concatenate([sum_up, sum_cross], axis=2)
@@ -815,7 +826,7 @@
 
     sum_up = joined(0, hidden // 2)
     sum_cross = jnp.stack([joined(hidden // 2 + k * half, half) for k in range(3)])
-    flat = after(jnp.concatenate(page_grads, axis=0), here, part_outs)
+    flat = after(jnp.concatenate(page_grads, axis=0), here, part_cross)
     back, _, _ = norm_back(x_in, gain[0], d_h)
     token_grad = g_one + back
 

time: 703 us -> 679 us (0.966)
  waiting for transfers between devices: 216 us -> 203 us
  starting transfers between devices: 76.3 us -> 65.4 us
    reduce_scatter x4, waiting for transfers between devices: 30 us -> 3.83 us  [plane_scatter(): lax.psum_scatter(flat, AXES, scatter_dimension=0, axis_index_groups=net.p...]
    reduce_scatter x3, waiting for transfers between devices: 0.01 us -> 15.1 us  [seq_scatter(): mine = lax.psum_scatter(flat, 'seq', scatter_dimension=0, tiled=True)]
    ppermute x39 -> x36, starting transfers between devices: 62.8 us -> 51.6 us  [along(): return lax.ppermute(value, AXES, self.line_map[by % self.seq])]
    unnamed x224 -> x202, local copies, waits for them, and re-layouts: 31.8 us -> 26.4 us
    ppermute x39 -> x36, waiting for transfers between devices: 171 us -> 167 us  [along(): return lax.ppermute(value, AXES, self.line_map[by % self.seq])]
  transfers between devices with their start and end apart: 81 -> 78, of which waited for: 30 -> 34; matrix products, arithmetic and copies ran while one was open for 33% -> 34% of each run, Pallas kernels for 15% -> 16%
where the time goes in v3:
time: 679 us; the launch traced here: 669 us
  waiting for transfers between devices  203 us (30%)
  matrix products  108 us (16%)
  Pallas kernels  105 us (15%)
  local copies, waits for them, and re-layouts  96.5 us (14%)
  starting transfers between devices  65.4 us (10%)
  other arithmetic  60.1 us (9%)
  between operations  30.5 us (4%)
    ppermute x36, waiting for transfers between devices, along(): return lax.ppermute(value, AXES, self.line_map[by % self.seq])  167 us
    dot_general x29, matrix products, dot(): return lax.dot_general(a, b, dims, preferred_element_type=F32)  108 us
    ppermute x36, starting transfers between devices, along(): return lax.ppermute(value, AXES, self.line_map[by % self.seq])  51.6 us
    pallas_call x2, Pallas kernels, self_bwd(): pl.pallas_call(functools.partial(self_bwd_kernel, rows=rows, width=width)...  34.7 us
    unnamed x202, local copies, waits for them, and re-layouts  26.4 us
    pallas_call x2, Pallas kernels, self_fwd(): pl.pallas_call(functools.partial(self_fwd_kernel, rows=rows, width=width)...  22.4 us
    pallas_call x8, Pallas kernels, project(): pl.pallas_call(project_kernel, grid_spec=pltpu.PrefetchScalarGridSpec(num...  18.3 us
    pallas_call x2, Pallas kernels, cross_bwd(): pl.pallas_call(cross_bwd_kernel, grid_spec=pltpu.PrefetchScalarGridSpec(n...  17.6 us
  transfers between devices with their start and end apart: 78, of which 34 were waited for; matrix products, arithmetic and copies ran while one was open for 34% of the time, Pallas kernels for 16%

profile of v3, /device:TPU:0, one launch (start us, length us, event | category | flops | bytes accessed | tf_op | source)
XLA Modules:
  0.0 669.0 jit_solution(16836334097734155570)
XLA Ops:
  29.7 8.4 %collective-permute-done.22 = bf16[32,5120]{1,0:T(8,128)(2,1)S(1)} collective-permute-done((bf16[32,5120]{1,0:T(8,128)(2,1)S(1)}, bf16[32,5120]{1,0:T(8,128)(2,1)S(1)}, u32[]{:S(2)}, u32[]{:S(2)}) %collective-permute-start.22) | collective-permute-done | bytes 327712 | tf_op jit(solution)/shard_map/ppermute | solution.py:382
  38.2 6.7 collective-permute-done.23
  44.9 5.8 collective-permute-done.24
  61.2 5.6 collective-permute-done.8
  84.8 17.6 %collective-permute-done.12.x_ref = bf16[512,1024]{1,0:T(8,128)(2,1)} collective-permute-done((bf16[512,1024]{1,0:T(8,128)(2,1)S(1)}, bf16[512,1024]{1,0:T(8,128)(2,1)}, u32[]{:S(2)}, u32[]{:S(2)}) %collective-permute-start.12) | collective-permute-done | bytes 1048608 | tf_op jit(solution)/shard_map/ppermute | solution.py:382
  102.5 24.1 %collective-permute-done.10.x_ref = bf16[512,1024]{1,0:T(8,128)(2,1)S(1)} collective-permute-done((bf16[512,1024]{1,0:T(8,128)(2,1)S(1)}, bf16[512,1024]{1,0:T(8,128)(2,1)S(1)}, u32[]{:S(2)}, u32[]{:S(2)}) %collective-permute-start.10) | collective-permute-done | bytes 1048608 | tf_op jit(solution)/shard_map/ppermute | solution.py:382
  150.9 11.2 %shard_map.245 = (bf16[1,2048,128]{2,1,0:T(8,128)(2,1)S(1)}, f32[1,2,1,2048]{3,2,1,0:T(1,128)S(1)}) custom-call(s32[1]{0:T(128)} %constant.268.clone.1.order_ref, bf16[2,2048,384]{2,1,0:T(8,128)(2,1)S(1)} %bitcast.446, bf16[2,2048,384]{2,1,0:T(8,128)(2,1)S(1)} %bitcast.447), custom_call_target="tpu_custom_call" | custom-call | flops 2147483648 | bytes 6291456 | tf_op jit(solution)/shard_map/pallas_call | solution.py:123
  163.4 11.2 %shard_map.246 = (bf16[1,2048,128]{2,1,0:T(8,128)(2,1)S(1)}, f32[1,2,1,2048]{3,2,1,0:T(1,128)S(1)}) custom-call(s32[1]{0:T(128)} %bitcast.36.order_ref, bf16[2,2048,384]{2,1,0:T(8,128)(2,1)S(1)} %bitcast.448, bf16[2,2048,384]{2,1,0:T(8,128)(2,1)S(1)} %bitcast.449), custom_call_target="tpu_custom_call" | custom-call | flops 2147483648 | bytes 6291456 | tf_op jit(solution)/shard_map/pallas_call | solution.py:123
  187.0 6.7 %collective-permute-done.27 = bf16[160,1024]{1,0:T(8,128)(2,1)} collective-permute-done((bf16[160,1024]{1,0:T(8,128)(2,1)}, bf16[160,1024]{1,0:T(8,128)(2,1)}, u32[]{:S(2)}, u32[]{:S(2)}) %collective-permute-start.27) | collective-permute-done | bytes 327712 | tf_op jit(solution)/shard_map/ppermute | solution.py:382
  215.4 8.4 %collective-permute-done.19 = bf16[512,128]{1,0:T(8,128)(2,1)S(1)} collective-permute-done((bf16[512,128]{1,0:T(8,128)(2,1)S(1)}, bf16[512,128]{1,0:T(8,128)(2,1)S(1)}, u32[]{:S(2)}, u32[]{:S(2)}) %collective-permute-start.19) | collective-permute-done | bytes 131104 | tf_op jit(solution)/shard_map/ppermute | solution.py:382
  226.1 14.5 %collective-permute-done.16 = bf16[512,128]{1,0:T(8,128)(2,1)S(1)} collective-permute-done((bf16[512,128]{1,0:T(8,128)(2,1)S(1)}, bf16[512,128]{1,0:T(8,128)(2,1)S(1)}, u32[]{:S(2)}, u32[]{:S(2)}) %collective-permute-start.16) | collective-permute-done | bytes 131104 | tf_op jit(solution)/shard_map/ppermute | solution.py:382
  263.1 5.3 add_convert_fusion
  270.1 6.1 shard_map.248
  277.9 6.1 shard_map.247
  289.7 9.9 %multiply_convert_fusion = (bf16[1024,2048]{1,0:T(8,128)(2,1)S(1)}, f32[1024,2048]{1,0:T(8,128)}) fusion(f32[2048]{0:T(1024)S(1)} %bitcast.515, bf16[1024,2048]{1,0:T(8,128)(2,1)} %bitcast.525, bf16[512,1024]{1,0:T(8,128)(2,1)} %collective-permute-done.32, bf16[512,1024]{1,0:T(8,128)(2,1)} %add_convert_fusion.3), kind=kOutput, calls=%fused_computation.8 | convolution fusion | flops 4311744512 | bytes 18882560 | tf_op jit(solution)/shard_map/dot_general | solution.py:28
  301.6 8.0 %convolution_convert_fusion = bf16[2048,1024]{1,0:T(8,128)(2,1)} fusion(bf16[1024,2048]{1,0:T(8,128)(2,1)S(1)} %get-tuple-element.224, bf16[512,1024]{1,0:T(8,128)(2,1)} %collective-permute-done.40, bf16[512,1024]{1,0:T(8,128)(2,1)} %bitcast.96), kind=kOutput, calls=%fused_computation.15 | convolution fusion | flops 4301258752 | bytes 10485760 | tf_op jit(solution)/shard_map/dot_general | solution.py:28
  311.5 11.0 %convert_reduce_fusion = (bf16[2048]{0:T(1024)(128)(2,1)S(1)}, bf16[1024,2048]{1,0:T(8,128)(2,1)S(1)}) fusion(f32[1024,2048]{1,0:T(8,128)} %get-tuple-element.225, f32[2048]{0:T(1024)S(1)} %bitcast.516, bf16[2048,1024]{1,0:T(8,128)(2,1)} %bitcast.528, bf16[512,1024]{1,0:T(8,128)(2,1)} %collective-permute-done.40, bf16[512,1024]{1,0:T(8,128)(2,1)} %bitcast.96), kind=kOutput, calls=%fused_computation.7 | convolution fusion | flops 4326422528 | bytes 18886656 | tf_op jit(solution)/shard_map/dot_general | solution.py:28
  324.5 8.2 %convert_add_fusion.2 = bf16[1024,2048]{1,0:T(8,128)(2,1)} fusion(bf16[1024,2048]{1,0:T(8,128)(2,1)S(1)} %get-tuple-element.228, bf16[]{:T(256)} %bitcast.97, bf16[512,1024]{1,0:T(8,128)(2,1)} %collective-permute-done.32, bf16[512,1024]{1,0:T(8,128)(2,1)} %add_convert_fusion.3), kind=kOutput, calls=%fused_computation.14 | convolution fusion | flops 4303355904 | bytes 10485762 | tf_op jit(solution)/shard_map/dot_general | solution.py:28
  334.6 5.4 fusion.40
  359.6 8.9 %shard_map.250 = (bf16[512,512]{1,0:T(8,128)(2,1)S(1)}, bf16[640,512]{1,0:T(8,128)(2,1)S(1)}, bf16[640,512]{1,0:T(8,128)(2,1)S(1)}) custom-call(s32[1]{0:T(128)} %bitcast.76.limit_ref, bf16[512,512]{1,0:T(8,128)(2,1)S(1)} %copy-done.11, bf16[640,1024]{1,0:T(8,128)(2,1)S(1)} %get-tuple-element.148.k_ref.v_ref, ...), custom_call_target="tpu_custom_call" | custom-call | flops 1677721600 | bytes 5505024 | tf_op jit(solution)/shard_map/pallas_call | solution.py:304
  372.2 8.7 %shard_map.249 = (bf16[512,512]{1,0:T(8,128)(2,1)S(1)}, bf16[640,512]{1,0:T(8,128)(2,1)S(1)}, bf16[640,512]{1,0:T(8,128)(2,1)S(1)}) custom-call(s32[1]{0:T(128)} %bitcast.61.limit_ref, bf16[512,512]{1,0:T(8,128)(2,1)S(1)} %copy-done.9, bf16[640,1024]{1,0:T(8,128)(2,1)S(1)} %get-tuple-element.149.k_ref.v_ref, ...), custom_call_target="tpu_custom_call" | custom-call | flops 1677721600 | bytes 5505024 | tf_op jit(solution)/shard_map/pallas_call | solution.py:304
  390.5 5.0 fusion.32
  434.8 9.0 %collective-permute-done.46 = bf16[2,512,128]{2,1,0:T(8,128)(2,1)S(1)} collective-permute-done((bf16[2,512,128]{2,1,0:T(8,128)(2,1)}, bf16[2,512,128]{2,1,0:T(8,128)(2,1)S(1)}, u32[]{:S(2)}, u32[]{:S(2)}) %collective-permute-start.46) | collective-permute-done | bytes 262176 | tf_op jit(solution)/shard_map/ppermute | solution.py:382
  445.0 17.3 %shard_map.251 = bf16[1,2048,384]{2,1,0:T(8,128)(2,1)S(1)} custom-call(bf16[2,2048,384]{2,1,0:T(8,128)(2,1)} %bitcast.450, bf16[2,2048,384]{2,1,0:T(8,128)(2,1)} %bitcast.451, bf16[2,2048,128]{2,1,0:T(8,128)(2,1)S(1)} %bitcast.462, bf16[1,2048,128]{2,1,0:T(8,128)(2,1)S(1)} %copy-done.7, f32[1,2,1,2048]{3,2,1,0:T(1,128)S(1)} %get-tuple-element.70.lse_ref), custom_call_target="tpu_custom_call" | custom-call | flops 5368709120 | bytes 9437184 | tf_op jit(solution)/shard_map/pallas_call | solution.py:201
  474.4 17.4 %shard_map.252 = bf16[1,2048,384]{2,1,0:T(8,128)(2,1)S(1)} custom-call(bf16[2,2048,384]{2,1,0:T(8,128)(2,1)} %bitcast.452, bf16[2,2048,384]{2,1,0:T(8,128)(2,1)} %bitcast.453, bf16[2,2048,128]{2,1,0:T(8,128)(2,1)S(1)} %bitcast.463, bf16[1,2048,128]{2,1,0:T(8,128)(2,1)S(1)} %copy-done.5, f32[1,2,1,2048]{3,2,1,0:T(1,128)S(1)} %broadcast_add_fusion.2.lse_ref), custom_call_target="tpu_custom_call" | custom-call | flops 5368709120 | bytes 9437184 | tf_op jit(solution)/shard_map/pallas_call | solution.py:201
  509.1 4.4 collective-permute-start.50
  531.0 5.0 fusion.152
  564.7 23.9 %collective-permute-done.62 = bf16[2,32,512]{2,1,0:T(8,128)(2,1)S(1)} collective-permute-done((bf16[2,32,512]{2,1,0:T(8,128)(2,1)S(1)}, bf16[2,32,512]{2,1,0:T(8,128)(2,1)S(1)}, u32[]{:S(2)}, u32[]{:S(2)}) %collective-permute-start.62) | collective-permute-done | bytes 65568 | tf_op jit(solution)/shard_map/ppermute | solution.py:382
  588.6 10.1 %collective-permute-done.63 = bf16[2,32,512]{2,1,0:T(8,128)(2,1)S(1)} collective-permute-done((bf16[2,32,512]{2,1,0:T(8,128)(2,1)S(1)}, bf16[2,32,512]{2,1,0:T(8,128)(2,1)S(1)}, u32[]{:S(2)}, u32[]{:S(2)}) %collective-permute-start.63) | collective-permute-done | bytes 65568 | tf_op jit(solution)/shard_map/ppermute | solution.py:382
  599.6 6.8 %collective-permute-done.64 = bf16[2,32,512]{2,1,0:T(8,128)(2,1)S(1)} collective-permute-done((bf16[2,32,512]{2,1,0:T(8,128)(2,1)S(1)}, bf16[2,32,512]{2,1,0:T(8,128)(2,1)S(1)}, u32[]{:S(2)}, u32[]{:S(2)}) %collective-permute-start.64) | collective-permute-done | bytes 65568 | tf_op jit(solution)/shard_map/ppermute | solution.py:382
  611.3 14.3 %collective-permute-done.55 = bf16[512,512]{1,0:T(8,128)(2,1)S(1)} collective-permute-done((bf16[512,512]{1,0:T(8,128)(2,1)S(1)}, bf16[512,512]{1,0:T(8,128)(2,1)S(1)}, u32[]{:S(2)}, u32[]{:S(2)}) %collective-permute-start.55) | collective-permute-done | bytes 524320 | tf_op jit(solution)/shard_map/ppermute | solution.py:382
  640.1 11.7 %reduce-scatter.16.cloned.1.call-done = bf16[32,5120]{1,0:T(8,128)(2,1)} async-done(((bf16[128,5120]{1,0:T(8,128)(2,1)}), bf16[32,5120]{1,0:T(8,128)(2,1)}) %reduce-scatter.16.cloned.1.call-update) | async-done | bytes 327696 | tf_op jit(solution)/shard_map/reduce_scatter | solution.py:493
  (639 shorter events, 315.8 us)
Async XLA Ops:
  7.2 235.9 %all-gather.4.cloned.1.call-start = ((), (), s32[]{:S(2)}) async-start(), calls=%async_computation.7 | async-start | bytes 6553600 | tf_op jit(solution)/shard_map/all_gather | solution.py:480
  51.8 237.8 %all-gather.6.cloned.1.call-start = ((), (), s32[]{:S(2)}) async-start(), calls=%async_computation.8 | async-start | bytes 5242880 | tf_op jit(solution)/shard_map/all_gather | solution.py:480
  54.2 26.1 %collective-permute-start.5 = (bf16[512,1024]{1,0:T(8,128)(2,1)S(1)}, bf16[512,1024]{1,0:T(8,128)(2,1)}, u32[]{:S(2)}, u32[]{:S(2)}) collective-permute-start(bf16[512,1024]{1,0:T(8,128)(2,1)S(1)} %add_bitcast_fusion.x_ref), channel_id=1, source_target_pairs={{0,4},{1,5},{2,6},{3,7},{4,0},{5,1},{6,2},{7,3},{8,12},{9,13},{10,... | collective-permute-start | bytes 3145736 | tf_op jit(solution)/shard_map/ppermute | solution.py:379
  54.3 30.3 %collective-permute-start.4 = (bf16[512,1024]{1,0:T(8,128)(2,1)S(1)}, bf16[512,1024]{1,0:T(8,128)(2,1)S(1)}, u32[]{:S(2)}, u32[]{:S(2)}) collective-permute-start(bf16[512,1024]{1,0:T(8,128)(2,1)S(1)} %add_bitcast_fusion.x_ref), channel_id=1, source_target_pairs={{0,1},{1,2},{2,3},{3,0},{4,5},{5,6},{6,7},{7,4},{8,9},{9,10},{10,1... | collective-permute-start | bytes 3145736 | tf_op jit(solution)/shard_map/ppermute | solution.py:382
  54.5 47.9 %collective-permute-start.12 = (bf16[512,1024]{1,0:T(8,128)(2,1)S(1)}, bf16[512,1024]{1,0:T(8,128)(2,1)}, u32[]{:S(2)}, u32[]{:S(2)}) collective-permute-start(bf16[512,1024]{1,0:T(8,128)(2,1)S(1)} %add_bitcast_fusion.x_ref), channel_id=1, source_target_pairs={{0,3},{1,0},{2,1},{3,2},{4,7},{5,4},{6,5},{7,6},{8,11},{9,8},{10,9... | collective-permute-start | bytes 3145736 | tf_op jit(solution)/shard_map/ppermute | solution.py:382
  84.6 42.0 %collective-permute-start.10 = (bf16[512,1024]{1,0:T(8,128)(2,1)S(1)}, bf16[512,1024]{1,0:T(8,128)(2,1)S(1)}, u32[]{:S(2)}, u32[]{:S(2)}) collective-permute-start(bf16[512,1024]{1,0:T(8,128)(2,1)S(1)} %broadcast_add_fusion), channel_id=1, source_target_pairs={{0,1},{1,2},{2,3},{3,0},{4,5},{5,6},{6,7},{7,4},{8,9},{9,10},{10,1... | collective-permute-start | bytes 3145736 | tf_op jit(solution)/shard_map/ppermute | solution.py:382
  84.8 48.1 %collective-permute-start.14 = (bf16[512,1024]{1,0:T(8,128)(2,1)S(1)}, bf16[512,1024]{1,0:T(8,128)(2,1)S(1)}, u32[]{:S(2)}, u32[]{:S(2)}) collective-permute-start(bf16[512,1024]{1,0:T(8,128)(2,1)S(1)} %collective-permute-done.4.x_ref), channel_id=1, source_target_pairs={{0,4},{1,5},{2,6},{3,7},{4,0},{5,1},{6,2},{7,3},{8,12},{9,13},{10,... | collective-permute-start | bytes 3145736 | tf_op jit(solution)/shard_map/ppermute | solution.py:379
  102.4 39.0 %collective-permute-start.13 = (bf16[512,1024]{1,0:T(8,128)(2,1)}, bf16[512,1024]{1,0:T(8,128)(2,1)S(1)}, u32[]{:S(2)}, u32[]{:S(2)}) collective-permute-start(bf16[512,1024]{1,0:T(8,128)(2,1)} %collective-permute-done.12.x_ref), channel_id=1, source_target_pairs={{0,4},{1,5},{2,6},{3,7},{4,0},{5,1},{6,2},{7,3},{8,12},{9,13},{10,... | collective-permute-start | bytes 3145736 | tf_op jit(solution)/shard_map/ppermute | solution.py:379
  132.1 43.7 %collective-permute-start.33 = (bf16[2,32,2048]{2,1,0:T(8,128)(2,1)}, bf16[2,32,2048]{2,1,0:T(8,128)(2,1)}, u32[]{:S(2)}, u32[]{:S(2)}) collective-permute-start(bf16[2,32,2048]{2,1,0:T(8,128)(2,1)} %get-tuple-element.131), channel_id=1, source_target_pairs={{0,1},{1,2},{2,3},{3,0},{4,5},{5,6},{6,7},{7,4},{8,9},{9,10},{10,1... | collective-permute-start | bytes 786440 | tf_op jit(solution)/shard_map/ppermute | solution.py:382
  132.1 45.4 %collective-permute-start.34 = (bf16[2,32,2048]{2,1,0:T(8,128)(2,1)}, bf16[2,32,2048]{2,1,0:T(8,128)(2,1)}, u32[]{:S(2)}, u32[]{:S(2)}) collective-permute-start(bf16[2,32,2048]{2,1,0:T(8,128)(2,1)} %get-tuple-element.131), channel_id=1, source_target_pairs={{0,2},{1,3},{2,0},{3,1},{4,6},{5,7},{6,4},{7,5},{8,10},{9,11},{10,... | collective-permute-start | bytes 786440 | tf_op jit(solution)/shard_map/ppermute | solution.py:382
  132.9 46.3 %collective-permute-start.35 = (bf16[2,32,2048]{2,1,0:T(8,128)(2,1)}, bf16[2,32,2048]{2,1,0:T(8,128)(2,1)}, u32[]{:S(2)}, u32[]{:S(2)}) collective-permute-start(bf16[2,32,2048]{2,1,0:T(8,128)(2,1)} %get-tuple-element.131), channel_id=1, source_target_pairs={{0,3},{1,0},{2,1},{3,2},{4,7},{5,4},{6,5},{7,6},{8,11},{9,8},{10,9... | collective-permute-start | bytes 786440 | tf_op jit(solution)/shard_map/ppermute | solution.py:382
  180.9 130.6 %all-gather.8.cloned.1.call-start = ((), (), s32[]{:S(2)}) async-start(), calls=%async_computation.9 | async-start | bytes 5242880 | tf_op jit(solution)/shard_map/all_gather | solution.py:480
  212.7 27.9 %collective-permute-start.16 = (bf16[512,128]{1,0:T(8,128)(2,1)S(1)}, bf16[512,128]{1,0:T(8,128)(2,1)S(1)}, u32[]{:S(2)}, u32[]{:S(2)}) collective-permute-start(bf16[512,128]{1,0:T(8,128)(2,1)S(1)} %get-tuple-element.185), channel_id=1, source_target_pairs={{0,2},{1,3},{2,0},{3,1},{4,6},{5,7},{6,4},{7,5},{8,10},{9,11},{10,... | collective-permute-start | bytes 393224 | tf_op jit(solution)/shard_map/ppermute | solution.py:382
  213.5 27.1 %collective-permute-start.17 = (bf16[512,128]{1,0:T(8,128)(2,1)S(1)}, bf16[512,128]{1,0:T(8,128)(2,1)S(1)}, u32[]{:S(2)}, u32[]{:S(2)}) collective-permute-start(bf16[512,128]{1,0:T(8,128)(2,1)S(1)} %get-tuple-element.184), channel_id=1, source_target_pairs={{0,1},{1,2},{2,3},{3,0},{4,5},{5,6},{6,7},{7,4},{8,9},{9,10},{10,1... | collective-permute-start | bytes 393224 | tf_op jit(solution)/shard_map/ppermute | solution.py:382
  223.7 39.3 %collective-permute-start.30 = (bf16[640,1024]{1,0:T(8,128)(2,1)}, bf16[640,1024]{1,0:T(8,128)(2,1)}, u32[]{:S(2)}, u32[]{:S(2)}) collective-permute-start(bf16[640,1024]{1,0:T(8,128)(2,1)} %bitcast.70), channel_id=1, source_target_pairs={{0,4},{1,5},{2,6},{3,7},{4,0},{5,1},{6,2},{7,3},{8,12},{9,13},{10,... | collective-permute-start | bytes 3932168 | tf_op jit(solution)/shard_map/ppermute | solution.py:379
  223.8 26.6 %collective-permute-start.36 = (bf16[128,1024]{1,0:T(8,128)(2,1)}, bf16[128,1024]{1,0:T(8,128)(2,1)}, u32[]{:S(2)}, u32[]{:S(2)}) collective-permute-start(bf16[128,1024]{1,0:T(8,128)(2,1)} %get-tuple-element.133), channel_id=1, source_target_pairs={{0,1},{1,2},{2,3},{3,0},{4,5},{5,6},{6,7},{7,4},{8,9},{9,10},{10,1... | collective-permute-start | bytes 786440 | tf_op jit(solution)/shard_map/ppermute | solution.py:382
  223.8 27.5 %collective-permute-start.37 = (bf16[128,1024]{1,0:T(8,128)(2,1)}, bf16[128,1024]{1,0:T(8,128)(2,1)}, u32[]{:S(2)}, u32[]{:S(2)}) collective-permute-start(bf16[128,1024]{1,0:T(8,128)(2,1)} %get-tuple-element.133), channel_id=1, source_target_pairs={{0,2},{1,3},{2,0},{3,1},{4,6},{5,7},{6,4},{7,5},{8,10},{9,11},{10,... | collective-permute-start | bytes 786440 | tf_op jit(solution)/shard_map/ppermute | solution.py:382
  254.4 130.2 %reduce-scatter.8.cloned.1.call-start = ((), (), s32[]{:S(2)}) async-start(), calls=%async_computation.10 | async-start | bytes 5242880 | tf_op jit(solution)/shard_map/reduce_scatter | solution.py:485
  311.4 103.8 %reduce-scatter.10.cloned.1.call-start = ((), (), s32[]{:S(2)}) async-start(), calls=%async_computation.11 | async-start | bytes 1638400 | tf_op jit(solution)/shard_map/reduce_scatter | solution.py:493
  383.9 115.6 %reduce-scatter.18.cloned.1.call-start = ((), (), s32[]{:S(2)}) async-start(), calls=%async_computation.15 | async-start | bytes 5242880 | tf_op jit(solution)/shard_map/reduce_scatter | solution.py:485
  384.5 132.4 %reduce-scatter.12.cloned.1.call-start = ((), (), s32[]{:S(2)}) async-start(), calls=%async_computation.12 | async-start | bytes 3932160 | tf_op jit(solution)/shard_map/reduce_scatter | solution.py:485
  400.8 156.4 %reduce-scatter.14.cloned.1.call-start = ((), (), s32[]{:S(2)}) async-start(), calls=%async_computation.13 | async-start | bytes 2621440 | tf_op jit(solution)/shard_map/reduce_scatter | solution.py:485
  422.5 21.3 %collective-permute-start.46 = (bf16[2,512,128]{2,1,0:T(8,128)(2,1)}, bf16[2,512,128]{2,1,0:T(8,128)(2,1)S(1)}, u32[]{:S(2)}, u32[]{:S(2)}) collective-permute-start(bf16[2,512,128]{2,1,0:T(8,128)(2,1)} %get-tuple-element.165), channel_id=1, source_target_pairs={{0,2},{1,3},{2,0},{3,1},{4,6},{5,7},{6,4},{7,5},{8,10},{9,11},{10,... | collective-permute-start | bytes 786440 | tf_op jit(solution)/shard_map/ppermute | solution.py:382
  465.0 167.4 %reduce-scatter.20.cloned.1.call-start = ((), (), s32[]{:S(2)}) async-start(), calls=%async_computation.16 | async-start | bytes 2621440 | tf_op jit(solution)/shard_map/reduce_scatter | solution.py:493
  494.4 26.3 %collective-permute-start.51 = (bf16[2048,512]{1,0:T(8,128)(2,1)}, bf16[2048,512]{1,0:T(8,128)(2,1)}, u32[]{:S(2)}, u32[]{:S(2)}) collective-permute-start(bf16[2048,512]{1,0:T(8,128)(2,1)} %convolution_convert_fusion.1), channel_id=1, source_target_pairs={{0,4},{1,5},{2,6},{3,7},{4,0},{5,1},{6,2},{7,3},{8,12},{9,13},{10,... | collective-permute-start | bytes 6291464 | tf_op jit(solution)/shard_map/ppermute | solution.py:379
  506.4 145.4 %reduce-scatter.16.cloned.1.call-start = ((), (), s32[]{:S(2)}) async-start(), calls=%async_computation.14 | async-start | bytes 1638400 | tf_op jit(solution)/shard_map/reduce_scatter | solution.py:493
  513.5 96.0 %collective-permute-start.53 = (bf16[512,512]{1,0:T(8,128)(2,1)}, bf16[512,512]{1,0:T(8,128)(2,1)}, u32[]{:S(2)}, u32[]{:S(2)}) collective-permute-start(bf16[512,512]{1,0:T(8,128)(2,1)} %get-tuple-element.145), channel_id=1, source_target_pairs={{0,3},{1,0},{2,1},{3,2},{4,7},{5,4},{6,5},{7,6},{8,11},{9,8},{10,9... | collective-permute-start | bytes 1572872 | tf_op jit(solution)/shard_map/ppermute | solution.py:382
  529.6 79.9 %collective-permute-start.52 = (bf16[512,512]{1,0:T(8,128)(2,1)}, bf16[512,512]{1,0:T(8,128)(2,1)}, u32[]{:S(2)}, u32[]{:S(2)}) collective-permute-start(bf16[512,512]{1,0:T(8,128)(2,1)} %fusion.66), channel_id=1, source_target_pairs={{0,1},{1,2},{2,3},{3,0},{4,5},{5,6},{6,7},{7,4},{8,9},{9,10},{10,1... | collective-permute-start | bytes 1572872 | tf_op jit(solution)/shard_map/ppermute | solution.py:382
  548.2 59.0 %collective-permute-start.54 = (bf16[512,512]{1,0:T(8,128)(2,1)}, bf16[512,512]{1,0:T(8,128)(2,1)S(1)}, u32[]{:S(2)}, u32[]{:S(2)}) collective-permute-start(bf16[512,512]{1,0:T(8,128)(2,1)} %get-tuple-element.142), channel_id=1, source_target_pairs={{0,1},{1,2},{2,3},{3,0},{4,5},{5,6},{6,7},{7,4},{8,9},{9,10},{10,1... | collective-permute-start | bytes 1572872 | tf_op jit(solution)/shard_map/ppermute | solution.py:382
  560.5 50.8 %collective-permute-start.56 = (bf16[512,512]{1,0:T(8,128)(2,1)S(1)}, bf16[512,512]{1,0:T(8,128)(2,1)S(1)}, u32[]{:S(2)}, u32[]{:S(2)}) collective-permute-start(bf16[512,512]{1,0:T(8,128)(2,1)S(1)} %get-tuple-element.143), channel_id=1, source_target_pairs={{0,3},{1,0},{2,1},{3,2},{4,7},{5,4},{6,5},{7,6},{8,11},{9,8},{10,9... | collective-permute-start | bytes 1572872 | tf_op jit(solution)/shard_map/ppermute | solution.py:382
  564.6 24.0 %collective-permute-start.62 = (bf16[2,32,512]{2,1,0:T(8,128)(2,1)S(1)}, bf16[2,32,512]{2,1,0:T(8,128)(2,1)S(1)}, u32[]{:S(2)}, u32[]{:S(2)}) collective-permute-start(bf16[2,32,512]{2,1,0:T(8,128)(2,1)S(1)} %get-tuple-element.208), channel_id=1, source_target_pairs={{0,1},{1,2},{2,3},{3,0},{4,5},{5,6},{6,7},{7,4},{8,9},{9,10},{10,1... | collective-permute-start | bytes 196616 | tf_op jit(solution)/shard_map/ppermute | solution.py:382
  607.1 28.4 %collective-permute-start.66 = (bf16[4,32,384]{2,1,0:T(8,128)(2,1)}, bf16[4,32,384]{2,1,0:T(8,128)(2,1)S(1)}, u32[]{:S(2)}, u32[]{:S(2)}) collective-permute-start(bf16[4,32,384]{2,1,0:T(8,128)(2,1)} %get-tuple-element.216), channel_id=1, source_target_pairs={{0,4},{1,5},{2,6},{3,7},{4,0},{5,1},{6,2},{7,3},{8,12},{9,13},{10,... | collective-permute-start | bytes 294920 | tf_op jit(solution)/shard_map/ppermute | solution.py:379
  (145 other events, 1192.9 us)
Sparse Core Ops, SparseCore 0:
  51.9 62.2 all-gather.3
  181.1 52.5 all-gather.5
  254.5 52.7 all-gather.7
  311.5 52.5 reduce-scatter.7
  384.0 31.1 reduce-scatter.9
  418.4 51.4 reduce-scatter.17
  472.9 43.9 reduce-scatter.11
  519.8 37.3 reduce-scatter.13
  559.6 56.6 reduce-scatter.19
  618.4 33.4 reduce-scatter.15

commit v4 on v3

--- a/solution.py
+++ b/solution.py
@@ -1,4 +1,5 @@
 import functools
+import math
 
 import jax
 import jax.numpy as jnp
@@ -702,7 +703,7 @@
     order = jnp.zeros((1,), jnp.int32)
     for k in range(2):
         order = after(order, o_self[0]) if k else order
-        out, lse = self_fwd(order, qkv, att_rows, k)
+        out, lse = self_fwd(order, qkv, math.gcd(1024, seq * rows), k)
         o_self.append(out)
         lse_self.append(lse)
         attended.append(to_tokens(out[0]))

time: 679 us -> 674 us (level)
  transfers between devices with their start and end apart: 78 -> 78, of which waited for: 34 -> 34; matrix products, arithmetic and copies ran while one was open for 34% -> 35% of each run, Pallas kernels for 16% -> 15%
where the time goes in v4:
time: 674 us; the launch traced here: 663 us
  waiting for transfers between devices  204 us (30%)
  matrix products  108 us (16%)
  Pallas kernels  99.6 us (15%)
  local copies, waits for them, and re-layouts  96.5 us (14%)
  starting transfers between devices  65.4 us (10%)
  other arithmetic  60.1 us (9%)
  between operations  30.4 us (5%)
    ppermute x36, waiting for transfers between devices, along(): return lax.ppermute(value, AXES, self.line_map[by % self.seq])  167 us
    dot_general x29, matrix products, dot(): return lax.dot_general(a, b, dims, preferred_element_type=F32)  108 us
    ppermute x36, starting transfers between devices, along(): return lax.ppermute(value, AXES, self.line_map[by % self.seq])  51.5 us
    pallas_call x2, Pallas kernels, self_bwd(): pl.pallas_call(functools.partial(self_bwd_kernel, rows=rows, width=width)...  34.7 us
    unnamed x202, local copies, waits for them, and re-layouts  26.3 us
    pallas_call x8, Pallas kernels, project(): pl.pallas_call(project_kernel, grid_spec=pltpu.PrefetchScalarGridSpec(num...  18.3 us
    pallas_call x2, Pallas kernels, cross_bwd(): pl.pallas_call(cross_bwd_kernel, grid_spec=pltpu.PrefetchScalarGridSpec(n...  17.6 us
    pallas_call x2, Pallas kernels, self_fwd(): pl.pallas_call(functools.partial(self_fwd_kernel, rows=rows, width=width)...  16.8 us
  transfers between devices with their start and end apart: 78, of which 34 were waited for; matrix products, arithmetic and copies ran while one was open for 35% of the time, Pallas kernels for 15%

profile of v4, /device:TPU:0, one launch (start us, length us, event | category | flops | bytes accessed | tf_op | source)
XLA Modules:
  0.0 663.4 jit_solution(2848627230701234057)
XLA Ops:
  29.7 8.4 %collective-permute-done.22 = bf16[32,5120]{1,0:T(8,128)(2,1)S(1)} collective-permute-done((bf16[32,5120]{1,0:T(8,128)(2,1)S(1)}, bf16[32,5120]{1,0:T(8,128)(2,1)S(1)}, u32[]{:S(2)}, u32[]{:S(2)}) %collective-permute-start.22) | collective-permute-done | bytes 327712 | tf_op jit(solution)/shard_map/ppermute | solution.py:383
  38.2 6.7 %collective-permute-done.23 = bf16[32,5120]{1,0:T(8,128)(2,1)S(1)} collective-permute-done((bf16[32,5120]{1,0:T(8,128)(2,1)S(1)}, bf16[32,5120]{1,0:T(8,128)(2,1)S(1)}, u32[]{:S(2)}, u32[]{:S(2)}) %collective-permute-start.23) | collective-permute-done | bytes 327712 | tf_op jit(solution)/shard_map/ppermute | solution.py:383
  44.9 5.8 collective-permute-done.24
  61.2 5.6 collective-permute-done.8
  84.8 17.6 %collective-permute-done.12.x_ref = bf16[512,1024]{1,0:T(8,128)(2,1)} collective-permute-done((bf16[512,1024]{1,0:T(8,128)(2,1)S(1)}, bf16[512,1024]{1,0:T(8,128)(2,1)}, u32[]{:S(2)}, u32[]{:S(2)}) %collective-permute-start.12) | collective-permute-done | bytes 1048608 | tf_op jit(solution)/shard_map/ppermute | solution.py:383
  102.5 24.1 %collective-permute-done.10.x_ref = bf16[512,1024]{1,0:T(8,128)(2,1)S(1)} collective-permute-done((bf16[512,1024]{1,0:T(8,128)(2,1)S(1)}, bf16[512,1024]{1,0:T(8,128)(2,1)S(1)}, u32[]{:S(2)}, u32[]{:S(2)}) %collective-permute-start.10) | collective-permute-done | bytes 1048608 | tf_op jit(solution)/shard_map/ppermute | solution.py:383
  150.8 8.2 %shard_map.245 = (bf16[1,2048,128]{2,1,0:T(8,128)(2,1)S(1)}, f32[1,2,1,2048]{3,2,1,0:T(1,128)S(1)}) custom-call(s32[1]{0:T(128)} %constant.268.clone.1.order_ref, bf16[2,2048,384]{2,1,0:T(8,128)(2,1)S(1)} %bitcast.446, bf16[2,2048,384]{2,1,0:T(8,128)(2,1)S(1)} %bitcast.447), custom_call_target="tpu_custom_call" | custom-call | flops 2147483648 | bytes 6291456 | tf_op jit(solution)/shard_map/pallas_call | solution.py:124
  160.2 8.6 %shard_map.246 = (bf16[1,2048,128]{2,1,0:T(8,128)(2,1)S(1)}, f32[1,2,1,2048]{3,2,1,0:T(1,128)S(1)}) custom-call(s32[1]{0:T(128)} %bitcast.36.order_ref, bf16[2,2048,384]{2,1,0:T(8,128)(2,1)S(1)} %bitcast.448, bf16[2,2048,384]{2,1,0:T(8,128)(2,1)S(1)} %bitcast.449), custom_call_target="tpu_custom_call" | custom-call | flops 2147483648 | bytes 6291456 | tf_op jit(solution)/shard_map/pallas_call | solution.py:124
  181.3 6.7 %collective-permute-done.27 = bf16[160,1024]{1,0:T(8,128)(2,1)} collective-permute-done((bf16[160,1024]{1,0:T(8,128)(2,1)}, bf16[160,1024]{1,0:T(8,128)(2,1)}, u32[]{:S(2)}, u32[]{:S(2)}) %collective-permute-start.27) | collective-permute-done | bytes 327712 | tf_op jit(solution)/shard_map/ppermute | solution.py:383
  209.7 8.4 %collective-permute-done.19 = bf16[512,128]{1,0:T(8,128)(2,1)S(1)} collective-permute-done((bf16[512,128]{1,0:T(8,128)(2,1)S(1)}, bf16[512,128]{1,0:T(8,128)(2,1)S(1)}, u32[]{:S(2)}, u32[]{:S(2)}) %collective-permute-start.19) | collective-permute-done | bytes 131104 | tf_op jit(solution)/shard_map/ppermute | solution.py:383
  220.4 14.5 %collective-permute-done.16 = bf16[512,128]{1,0:T(8,128)(2,1)S(1)} collective-permute-done((bf16[512,128]{1,0:T(8,128)(2,1)S(1)}, bf16[512,128]{1,0:T(8,128)(2,1)S(1)}, u32[]{:S(2)}, u32[]{:S(2)}) %collective-permute-start.16) | collective-permute-done | bytes 131104 | tf_op jit(solution)/shard_map/ppermute | solution.py:383
  257.5 5.2 add_convert_fusion
  264.4 6.1 shard_map.248
  272.3 6.1 shard_map.247
  284.1 9.9 %multiply_convert_fusion = (bf16[1024,2048]{1,0:T(8,128)(2,1)S(1)}, f32[1024,2048]{1,0:T(8,128)}) fusion(f32[2048]{0:T(1024)S(1)} %bitcast.515, bf16[1024,2048]{1,0:T(8,128)(2,1)} %bitcast.525, bf16[512,1024]{1,0:T(8,128)(2,1)} %collective-permute-done.32, bf16[512,1024]{1,0:T(8,128)(2,1)} %add_convert_fusion.3), kind=kOutput, calls=%fused_computation.8 | convolution fusion | flops 4311744512 | bytes 18882560 | tf_op jit(solution)/shard_map/dot_general | solution.py:29
  296.0 8.0 %convolution_convert_fusion = bf16[2048,1024]{1,0:T(8,128)(2,1)} fusion(bf16[1024,2048]{1,0:T(8,128)(2,1)S(1)} %get-tuple-element.224, bf16[512,1024]{1,0:T(8,128)(2,1)} %collective-permute-done.40, bf16[512,1024]{1,0:T(8,128)(2,1)} %bitcast.96), kind=kOutput, calls=%fused_computation.15 | convolution fusion | flops 4301258752 | bytes 10485760 | tf_op jit(solution)/shard_map/dot_general | solution.py:29
  305.9 11.0 %convert_reduce_fusion = (bf16[2048]{0:T(1024)(128)(2,1)S(1)}, bf16[1024,2048]{1,0:T(8,128)(2,1)S(1)}) fusion(f32[1024,2048]{1,0:T(8,128)} %get-tuple-element.225, f32[2048]{0:T(1024)S(1)} %bitcast.516, bf16[2048,1024]{1,0:T(8,128)(2,1)} %bitcast.528, bf16[512,1024]{1,0:T(8,128)(2,1)} %collective-permute-done.40, bf16[512,1024]{1,0:T(8,128)(2,1)} %bitcast.96), kind=kOutput, calls=%fused_computation.7 | convolution fusion | flops 4326422528 | bytes 18886656 | tf_op jit(solution)/shard_map/dot_general | solution.py:29
  318.9 8.2 %convert_add_fusion.2 = bf16[1024,2048]{1,0:T(8,128)(2,1)} fusion(bf16[1024,2048]{1,0:T(8,128)(2,1)S(1)} %get-tuple-element.228, bf16[]{:T(256)} %bitcast.97, bf16[512,1024]{1,0:T(8,128)(2,1)} %collective-permute-done.32, bf16[512,1024]{1,0:T(8,128)(2,1)} %add_convert_fusion.3), kind=kOutput, calls=%fused_computation.14 | convolution fusion | flops 4303355904 | bytes 10485762 | tf_op jit(solution)/shard_map/dot_general | solution.py:29
  329.0 5.4 fusion.40
  354.0 8.9 %shard_map.250 = (bf16[512,512]{1,0:T(8,128)(2,1)S(1)}, bf16[640,512]{1,0:T(8,128)(2,1)S(1)}, bf16[640,512]{1,0:T(8,128)(2,1)S(1)}) custom-call(s32[1]{0:T(128)} %bitcast.76.limit_ref, bf16[512,512]{1,0:T(8,128)(2,1)S(1)} %copy-done.11, bf16[640,1024]{1,0:T(8,128)(2,1)S(1)} %get-tuple-element.148.k_ref.v_ref, ...), custom_call_target="tpu_custom_call" | custom-call | flops 1677721600 | bytes 5505024 | tf_op jit(solution)/shard_map/pallas_call | solution.py:305
  366.6 8.7 %shard_map.249 = (bf16[512,512]{1,0:T(8,128)(2,1)S(1)}, bf16[640,512]{1,0:T(8,128)(2,1)S(1)}, bf16[640,512]{1,0:T(8,128)(2,1)S(1)}) custom-call(s32[1]{0:T(128)} %bitcast.61.limit_ref, bf16[512,512]{1,0:T(8,128)(2,1)S(1)} %copy-done.9, bf16[640,1024]{1,0:T(8,128)(2,1)S(1)} %get-tuple-element.149.k_ref.v_ref, ...), custom_call_target="tpu_custom_call" | custom-call | flops 1677721600 | bytes 5505024 | tf_op jit(solution)/shard_map/pallas_call | solution.py:305
  384.9 5.0 fusion.32
  429.1 9.0 %collective-permute-done.46 = bf16[2,512,128]{2,1,0:T(8,128)(2,1)S(1)} collective-permute-done((bf16[2,512,128]{2,1,0:T(8,128)(2,1)}, bf16[2,512,128]{2,1,0:T(8,128)(2,1)S(1)}, u32[]{:S(2)}, u32[]{:S(2)}) %collective-permute-start.46) | collective-permute-done | bytes 262176 | tf_op jit(solution)/shard_map/ppermute | solution.py:383
  439.4 17.3 %shard_map.251 = bf16[1,2048,384]{2,1,0:T(8,128)(2,1)S(1)} custom-call(bf16[2,2048,384]{2,1,0:T(8,128)(2,1)} %bitcast.450, bf16[2,2048,384]{2,1,0:T(8,128)(2,1)} %bitcast.451, bf16[2,2048,128]{2,1,0:T(8,128)(2,1)S(1)} %bitcast.462, bf16[1,2048,128]{2,1,0:T(8,128)(2,1)S(1)} %copy-done.7, f32[1,2,1,2048]{3,2,1,0:T(1,128)S(1)} %get-tuple-element.70.lse_ref), custom_call_target="tpu_custom_call" | custom-call | flops 5368709120 | bytes 9437184 | tf_op jit(solution)/shard_map/pallas_call | solution.py:202
  468.7 17.4 %shard_map.252 = bf16[1,2048,384]{2,1,0:T(8,128)(2,1)S(1)} custom-call(bf16[2,2048,384]{2,1,0:T(8,128)(2,1)} %bitcast.452, bf16[2,2048,384]{2,1,0:T(8,128)(2,1)} %bitcast.453, bf16[2,2048,128]{2,1,0:T(8,128)(2,1)S(1)} %bitcast.463, bf16[1,2048,128]{2,1,0:T(8,128)(2,1)S(1)} %copy-done.5, f32[1,2,1,2048]{3,2,1,0:T(1,128)S(1)} %broadcast_add_fusion.2.lse_ref), custom_call_target="tpu_custom_call" | custom-call | flops 5368709120 | bytes 9437184 | tf_op jit(solution)/shard_map/pallas_call | solution.py:202
  503.5 4.4 collective-permute-start.50
  525.3 5.0 fusion.152
  559.1 23.8 %collective-permute-done.62 = bf16[2,32,512]{2,1,0:T(8,128)(2,1)S(1)} collective-permute-done((bf16[2,32,512]{2,1,0:T(8,128)(2,1)S(1)}, bf16[2,32,512]{2,1,0:T(8,128)(2,1)S(1)}, u32[]{:S(2)}, u32[]{:S(2)}) %collective-permute-start.62) | collective-permute-done | bytes 65568 | tf_op jit(solution)/shard_map/ppermute | solution.py:383
  582.9 10.2 %collective-permute-done.63 = bf16[2,32,512]{2,1,0:T(8,128)(2,1)S(1)} collective-permute-done((bf16[2,32,512]{2,1,0:T(8,128)(2,1)S(1)}, bf16[2,32,512]{2,1,0:T(8,128)(2,1)S(1)}, u32[]{:S(2)}, u32[]{:S(2)}) %collective-permute-start.63) | collective-permute-done | bytes 65568 | tf_op jit(solution)/shard_map/ppermute | solution.py:383
  594.0 7.8 %collective-permute-done.64 = bf16[2,32,512]{2,1,0:T(8,128)(2,1)S(1)} collective-permute-done((bf16[2,32,512]{2,1,0:T(8,128)(2,1)S(1)}, bf16[2,32,512]{2,1,0:T(8,128)(2,1)S(1)}, u32[]{:S(2)}, u32[]{:S(2)}) %collective-permute-start.64) | collective-permute-done | bytes 65568 | tf_op jit(solution)/shard_map/ppermute | solution.py:383
  606.7 13.8 %collective-permute-done.55 = bf16[512,512]{1,0:T(8,128)(2,1)S(1)} collective-permute-done((bf16[512,512]{1,0:T(8,128)(2,1)S(1)}, bf16[512,512]{1,0:T(8,128)(2,1)S(1)}, u32[]{:S(2)}, u32[]{:S(2)}) %collective-permute-start.55) | collective-permute-done | bytes 524320 | tf_op jit(solution)/shard_map/ppermute | solution.py:383
  634.9 11.3 %reduce-scatter.16.cloned.1.call-done = bf16[32,5120]{1,0:T(8,128)(2,1)} async-done(((bf16[128,5120]{1,0:T(8,128)(2,1)}), bf16[32,5120]{1,0:T(8,128)(2,1)}) %reduce-scatter.16.cloned.1.call-update) | async-done | bytes 327696 | tf_op jit(solution)/shard_map/reduce_scatter | solution.py:494
  (639 shorter events, 315.7 us)
Async XLA Ops:
  7.2 230.2 %all-gather.4.cloned.1.call-start = ((), (), s32[]{:S(2)}) async-start(), calls=%async_computation.7 | async-start | bytes 6553600 | tf_op jit(solution)/shard_map/all_gather | solution.py:481
  51.8 232.2 %all-gather.6.cloned.1.call-start = ((), (), s32[]{:S(2)}) async-start(), calls=%async_computation.8 | async-start | bytes 5242880 | tf_op jit(solution)/shard_map/all_gather | solution.py:481
  54.2 26.1 %collective-permute-start.5 = (bf16[512,1024]{1,0:T(8,128)(2,1)S(1)}, bf16[512,1024]{1,0:T(8,128)(2,1)}, u32[]{:S(2)}, u32[]{:S(2)}) collective-permute-start(bf16[512,1024]{1,0:T(8,128)(2,1)S(1)} %add_bitcast_fusion.x_ref), channel_id=1, source_target_pairs={{0,4},{1,5},{2,6},{3,7},{4,0},{5,1},{6,2},{7,3},{8,12},{9,13},{10,... | collective-permute-start | bytes 3145736 | tf_op jit(solution)/shard_map/ppermute | solution.py:380
  54.3 30.3 %collective-permute-start.4 = (bf16[512,1024]{1,0:T(8,128)(2,1)S(1)}, bf16[512,1024]{1,0:T(8,128)(2,1)S(1)}, u32[]{:S(2)}, u32[]{:S(2)}) collective-permute-start(bf16[512,1024]{1,0:T(8,128)(2,1)S(1)} %add_bitcast_fusion.x_ref), channel_id=1, source_target_pairs={{0,1},{1,2},{2,3},{3,0},{4,5},{5,6},{6,7},{7,4},{8,9},{9,10},{10,1... | collective-permute-start | bytes 3145736 | tf_op jit(solution)/shard_map/ppermute | solution.py:383
  54.5 47.9 %collective-permute-start.12 = (bf16[512,1024]{1,0:T(8,128)(2,1)S(1)}, bf16[512,1024]{1,0:T(8,128)(2,1)}, u32[]{:S(2)}, u32[]{:S(2)}) collective-permute-start(bf16[512,1024]{1,0:T(8,128)(2,1)S(1)} %add_bitcast_fusion.x_ref), channel_id=1, source_target_pairs={{0,3},{1,0},{2,1},{3,2},{4,7},{5,4},{6,5},{7,6},{8,11},{9,8},{10,9... | collective-permute-start | bytes 3145736 | tf_op jit(solution)/shard_map/ppermute | solution.py:383
  84.6 42.0 %collective-permute-start.10 = (bf16[512,1024]{1,0:T(8,128)(2,1)S(1)}, bf16[512,1024]{1,0:T(8,128)(2,1)S(1)}, u32[]{:S(2)}, u32[]{:S(2)}) collective-permute-start(bf16[512,1024]{1,0:T(8,128)(2,1)S(1)} %broadcast_add_fusion), channel_id=1, source_target_pairs={{0,1},{1,2},{2,3},{3,0},{4,5},{5,6},{6,7},{7,4},{8,9},{9,10},{10,1... | collective-permute-start | bytes 3145736 | tf_op jit(solution)/shard_map/ppermute | solution.py:383
  84.8 48.1 %collective-permute-start.14 = (bf16[512,1024]{1,0:T(8,128)(2,1)S(1)}, bf16[512,1024]{1,0:T(8,128)(2,1)S(1)}, u32[]{:S(2)}, u32[]{:S(2)}) collective-permute-start(bf16[512,1024]{1,0:T(8,128)(2,1)S(1)} %collective-permute-done.4.x_ref), channel_id=1, source_target_pairs={{0,4},{1,5},{2,6},{3,7},{4,0},{5,1},{6,2},{7,3},{8,12},{9,13},{10,... | collective-permute-start | bytes 3145736 | tf_op jit(solution)/shard_map/ppermute | solution.py:380
  102.4 38.8 %collective-permute-start.13 = (bf16[512,1024]{1,0:T(8,128)(2,1)}, bf16[512,1024]{1,0:T(8,128)(2,1)S(1)}, u32[]{:S(2)}, u32[]{:S(2)}) collective-permute-start(bf16[512,1024]{1,0:T(8,128)(2,1)} %collective-permute-done.12.x_ref), channel_id=1, source_target_pairs={{0,4},{1,5},{2,6},{3,7},{4,0},{5,1},{6,2},{7,3},{8,12},{9,13},{10,... | collective-permute-start | bytes 3145736 | tf_op jit(solution)/shard_map/ppermute | solution.py:380
  132.1 37.9 %collective-permute-start.33 = (bf16[2,32,2048]{2,1,0:T(8,128)(2,1)}, bf16[2,32,2048]{2,1,0:T(8,128)(2,1)}, u32[]{:S(2)}, u32[]{:S(2)}) collective-permute-start(bf16[2,32,2048]{2,1,0:T(8,128)(2,1)} %get-tuple-element.131), channel_id=1, source_target_pairs={{0,1},{1,2},{2,3},{3,0},{4,5},{5,6},{6,7},{7,4},{8,9},{9,10},{10,1... | collective-permute-start | bytes 786440 | tf_op jit(solution)/shard_map/ppermute | solution.py:383
  132.1 39.6 %collective-permute-start.34 = (bf16[2,32,2048]{2,1,0:T(8,128)(2,1)}, bf16[2,32,2048]{2,1,0:T(8,128)(2,1)}, u32[]{:S(2)}, u32[]{:S(2)}) collective-permute-start(bf16[2,32,2048]{2,1,0:T(8,128)(2,1)} %get-tuple-element.131), channel_id=1, source_target_pairs={{0,2},{1,3},{2,0},{3,1},{4,6},{5,7},{6,4},{7,5},{8,10},{9,11},{10,... | collective-permute-start | bytes 786440 | tf_op jit(solution)/shard_map/ppermute | solution.py:383
  132.9 40.5 %collective-permute-start.35 = (bf16[2,32,2048]{2,1,0:T(8,128)(2,1)}, bf16[2,32,2048]{2,1,0:T(8,128)(2,1)}, u32[]{:S(2)}, u32[]{:S(2)}) collective-permute-start(bf16[2,32,2048]{2,1,0:T(8,128)(2,1)} %get-tuple-element.131), channel_id=1, source_target_pairs={{0,3},{1,0},{2,1},{3,2},{4,7},{5,4},{6,5},{7,6},{8,11},{9,8},{10,9... | collective-permute-start | bytes 786440 | tf_op jit(solution)/shard_map/ppermute | solution.py:383
  175.2 130.7 %all-gather.8.cloned.1.call-start = ((), (), s32[]{:S(2)}) async-start(), calls=%async_computation.9 | async-start | bytes 5242880 | tf_op jit(solution)/shard_map/all_gather | solution.py:481
  207.0 27.9 %collective-permute-start.16 = (bf16[512,128]{1,0:T(8,128)(2,1)S(1)}, bf16[512,128]{1,0:T(8,128)(2,1)S(1)}, u32[]{:S(2)}, u32[]{:S(2)}) collective-permute-start(bf16[512,128]{1,0:T(8,128)(2,1)S(1)} %get-tuple-element.185), channel_id=1, source_target_pairs={{0,2},{1,3},{2,0},{3,1},{4,6},{5,7},{6,4},{7,5},{8,10},{9,11},{10,... | collective-permute-start | bytes 393224 | tf_op jit(solution)/shard_map/ppermute | solution.py:383
  207.7 27.1 %collective-permute-start.17 = (bf16[512,128]{1,0:T(8,128)(2,1)S(1)}, bf16[512,128]{1,0:T(8,128)(2,1)S(1)}, u32[]{:S(2)}, u32[]{:S(2)}) collective-permute-start(bf16[512,128]{1,0:T(8,128)(2,1)S(1)} %get-tuple-element.184), channel_id=1, source_target_pairs={{0,1},{1,2},{2,3},{3,0},{4,5},{5,6},{6,7},{7,4},{8,9},{9,10},{10,1... | collective-permute-start | bytes 393224 | tf_op jit(solution)/shard_map/ppermute | solution.py:383
  218.0 39.5 %collective-permute-start.30 = (bf16[640,1024]{1,0:T(8,128)(2,1)}, bf16[640,1024]{1,0:T(8,128)(2,1)}, u32[]{:S(2)}, u32[]{:S(2)}) collective-permute-start(bf16[640,1024]{1,0:T(8,128)(2,1)} %bitcast.70), channel_id=1, source_target_pairs={{0,4},{1,5},{2,6},{3,7},{4,0},{5,1},{6,2},{7,3},{8,12},{9,13},{10,... | collective-permute-start | bytes 3932168 | tf_op jit(solution)/shard_map/ppermute | solution.py:380
  218.0 26.6 %collective-permute-start.36 = (bf16[128,1024]{1,0:T(8,128)(2,1)}, bf16[128,1024]{1,0:T(8,128)(2,1)}, u32[]{:S(2)}, u32[]{:S(2)}) collective-permute-start(bf16[128,1024]{1,0:T(8,128)(2,1)} %get-tuple-element.133), channel_id=1, source_target_pairs={{0,1},{1,2},{2,3},{3,0},{4,5},{5,6},{6,7},{7,4},{8,9},{9,10},{10,1... | collective-permute-start | bytes 786440 | tf_op jit(solution)/shard_map/ppermute | solution.py:383
  218.1 27.5 %collective-permute-start.37 = (bf16[128,1024]{1,0:T(8,128)(2,1)}, bf16[128,1024]{1,0:T(8,128)(2,1)}, u32[]{:S(2)}, u32[]{:S(2)}) collective-permute-start(bf16[128,1024]{1,0:T(8,128)(2,1)} %get-tuple-element.133), channel_id=1, source_target_pairs={{0,2},{1,3},{2,0},{3,1},{4,6},{5,7},{6,4},{7,5},{8,10},{9,11},{10,... | collective-permute-start | bytes 786440 | tf_op jit(solution)/shard_map/ppermute | solution.py:383
  248.7 130.3 %reduce-scatter.8.cloned.1.call-start = ((), (), s32[]{:S(2)}) async-start(), calls=%async_computation.10 | async-start | bytes 5242880 | tf_op jit(solution)/shard_map/reduce_scatter | solution.py:486
  305.8 103.8 %reduce-scatter.10.cloned.1.call-start = ((), (), s32[]{:S(2)}) async-start(), calls=%async_computation.11 | async-start | bytes 1638400 | tf_op jit(solution)/shard_map/reduce_scatter | solution.py:494
  378.3 115.6 %reduce-scatter.18.cloned.1.call-start = ((), (), s32[]{:S(2)}) async-start(), calls=%async_computation.15 | async-start | bytes 5242880 | tf_op jit(solution)/shard_map/reduce_scatter | solution.py:486
  378.9 132.3 %reduce-scatter.12.cloned.1.call-start = ((), (), s32[]{:S(2)}) async-start(), calls=%async_computation.12 | async-start | bytes 3932160 | tf_op jit(solution)/shard_map/reduce_scatter | solution.py:486
  395.1 156.4 %reduce-scatter.14.cloned.1.call-start = ((), (), s32[]{:S(2)}) async-start(), calls=%async_computation.13 | async-start | bytes 2621440 | tf_op jit(solution)/shard_map/reduce_scatter | solution.py:486
  416.8 21.3 %collective-permute-start.46 = (bf16[2,512,128]{2,1,0:T(8,128)(2,1)}, bf16[2,512,128]{2,1,0:T(8,128)(2,1)S(1)}, u32[]{:S(2)}, u32[]{:S(2)}) collective-permute-start(bf16[2,512,128]{2,1,0:T(8,128)(2,1)} %get-tuple-element.165), channel_id=1, source_target_pairs={{0,2},{1,3},{2,0},{3,1},{4,6},{5,7},{6,4},{7,5},{8,10},{9,11},{10,... | collective-permute-start | bytes 786440 | tf_op jit(solution)/shard_map/ppermute | solution.py:383
  459.4 167.8 %reduce-scatter.20.cloned.1.call-start = ((), (), s32[]{:S(2)}) async-start(), calls=%async_computation.16 | async-start | bytes 2621440 | tf_op jit(solution)/shard_map/reduce_scatter | solution.py:494
  488.8 26.3 %collective-permute-start.51 = (bf16[2048,512]{1,0:T(8,128)(2,1)}, bf16[2048,512]{1,0:T(8,128)(2,1)}, u32[]{:S(2)}, u32[]{:S(2)}) collective-permute-start(bf16[2048,512]{1,0:T(8,128)(2,1)} %convolution_convert_fusion.1), channel_id=1, source_target_pairs={{0,4},{1,5},{2,6},{3,7},{4,0},{5,1},{6,2},{7,3},{8,12},{9,13},{10,... | collective-permute-start | bytes 6291464 | tf_op jit(solution)/shard_map/ppermute | solution.py:380
  500.8 145.5 %reduce-scatter.16.cloned.1.call-start = ((), (), s32[]{:S(2)}) async-start(), calls=%async_computation.14 | async-start | bytes 1638400 | tf_op jit(solution)/shard_map/reduce_scatter | solution.py:494
  507.9 97.0 %collective-permute-start.53 = (bf16[512,512]{1,0:T(8,128)(2,1)}, bf16[512,512]{1,0:T(8,128)(2,1)}, u32[]{:S(2)}, u32[]{:S(2)}) collective-permute-start(bf16[512,512]{1,0:T(8,128)(2,1)} %get-tuple-element.145), channel_id=1, source_target_pairs={{0,3},{1,0},{2,1},{3,2},{4,7},{5,4},{6,5},{7,6},{8,11},{9,8},{10,9... | collective-permute-start | bytes 1572872 | tf_op jit(solution)/shard_map/ppermute | solution.py:383
  523.9 80.9 %collective-permute-start.52 = (bf16[512,512]{1,0:T(8,128)(2,1)}, bf16[512,512]{1,0:T(8,128)(2,1)}, u32[]{:S(2)}, u32[]{:S(2)}) collective-permute-start(bf16[512,512]{1,0:T(8,128)(2,1)} %fusion.66), channel_id=1, source_target_pairs={{0,1},{1,2},{2,3},{3,0},{4,5},{5,6},{6,7},{7,4},{8,9},{9,10},{10,1... | collective-permute-start | bytes 1572872 | tf_op jit(solution)/shard_map/ppermute | solution.py:383
  542.5 60.0 %collective-permute-start.54 = (bf16[512,512]{1,0:T(8,128)(2,1)}, bf16[512,512]{1,0:T(8,128)(2,1)S(1)}, u32[]{:S(2)}, u32[]{:S(2)}) collective-permute-start(bf16[512,512]{1,0:T(8,128)(2,1)} %get-tuple-element.142), channel_id=1, source_target_pairs={{0,1},{1,2},{2,3},{3,0},{4,5},{5,6},{6,7},{7,4},{8,9},{9,10},{10,1... | collective-permute-start | bytes 1572872 | tf_op jit(solution)/shard_map/ppermute | solution.py:383
  554.8 51.8 %collective-permute-start.56 = (bf16[512,512]{1,0:T(8,128)(2,1)S(1)}, bf16[512,512]{1,0:T(8,128)(2,1)S(1)}, u32[]{:S(2)}, u32[]{:S(2)}) collective-permute-start(bf16[512,512]{1,0:T(8,128)(2,1)S(1)} %get-tuple-element.143), channel_id=1, source_target_pairs={{0,3},{1,0},{2,1},{3,2},{4,7},{5,4},{6,5},{7,6},{8,11},{9,8},{10,9... | collective-permute-start | bytes 1572872 | tf_op jit(solution)/shard_map/ppermute | solution.py:383
  558.9 24.0 %collective-permute-start.62 = (bf16[2,32,512]{2,1,0:T(8,128)(2,1)S(1)}, bf16[2,32,512]{2,1,0:T(8,128)(2,1)S(1)}, u32[]{:S(2)}, u32[]{:S(2)}) collective-permute-start(bf16[2,32,512]{2,1,0:T(8,128)(2,1)S(1)} %get-tuple-element.208), channel_id=1, source_target_pairs={{0,1},{1,2},{2,3},{3,0},{4,5},{5,6},{6,7},{7,4},{8,9},{9,10},{10,1... | collective-permute-start | bytes 196616 | tf_op jit(solution)/shard_map/ppermute | solution.py:383
  602.5 27.8 %collective-permute-start.66 = (bf16[4,32,384]{2,1,0:T(8,128)(2,1)}, bf16[4,32,384]{2,1,0:T(8,128)(2,1)S(1)}, u32[]{:S(2)}, u32[]{:S(2)}) collective-permute-start(bf16[4,32,384]{2,1,0:T(8,128)(2,1)} %get-tuple-element.216), channel_id=1, source_target_pairs={{0,4},{1,5},{2,6},{3,7},{4,0},{5,1},{6,2},{7,3},{8,12},{9,13},{10,... | collective-permute-start | bytes 294920 | tf_op jit(solution)/shard_map/ppermute | solution.py:380
  (145 other events, 1181.4 us)
Sparse Core Ops, SparseCore 0:
  51.9 62.2 all-gather.3
  175.3 52.5 all-gather.5
  248.8 52.6 all-gather.7
  305.9 52.5 reduce-scatter.7
  378.4 31.1 reduce-scatter.9
  412.7 51.4 reduce-scatter.17
  467.2 43.9 reduce-scatter.11
  514.1 37.3 reduce-scatter.13
  553.9 55.5 reduce-scatter.19
  611.7 34.5 reduce-scatter.15
